TPU v7x, 512 devices: a whole 4x8x8 slice. The times are simulated.
512 devices in a mesh: seq: 32 (over y, x), head: 16 (over z, core).
Axes of the slice: x: 4, y: 8, z: 8, core: 2. Of those that a mesh axis runs over, the one named last changes fastest.
Arguments:
- queries: bfloat16 [8192, 2048], P('seq', 'head'), may hold values from -192 to 192
- keys: bfloat16 [8192, 2048], P('seq', 'head'), may hold values from -6 to 6
- values: bfloat16 [8192, 2048], P('seq', 'head'), may hold values from -6 to 6
- out_weight: bfloat16 [2048, 3072], P('head'), may hold values from -0.125 to 0.125
- grad_mixed: bfloat16 [8192, 3072], P('seq', 'head'), may hold values from -6 to 6
- kv_tiles: int32 [128, 8], replicated, may hold values from 0 to 127, as said below
- kv_counts: int32 [128], replicated, may hold values from 1 to 8, as said below
Outputs:
- mixed: bfloat16 [8192, 3072], P('seq', 'head')
- grad_queries: bfloat16 [8192, 2048], P('seq', 'head')
- grad_keys: bfloat16 [8192, 2048], P('seq', 'head')
- grad_values: bfloat16 [8192, 2048], P('seq', 'head')
- weight_grad: bfloat16 [2048, 3072], P('head')
Inputs may be any that keep to these rules, and one draw needn't show every extreme that they name: `kv_tiles`: row t lists key tiles for query tile t; the 8 entries of a row are distinct. Tile k belongs to index k // 4 of seq. Over the 4 rows i * 4 to (i + 1) * 4 - 1, all entries taken together, used or not, name the tiles of each index of seq exactly 1 times. Entries j < kv_counts[t] of row t are used.
All inputs are finite; a program needn't handle non-finite values.
Results may differ from a plain program's by a relative error of at most 0.034.
Values may be sent and summed in bfloat16 or wider, within the bound.
No kernel may reach another device: no remote copies, remote signals or barrier semaphores. Data moves between devices by JAX's collectives and lax.ppermute only.
A program may use at most 64 MiB of HBM per device.

v0:
```python
from functools import partial
import math

import jax
import jax.numpy as jnp
from jax import lax
from jax.sharding import PartitionSpec as P

TILE = 64
HD = 64


def entry_layout(tile_lists, tile_counts, per_owner, tiles_dev):
    list_length = tile_lists.shape[1]
    flat_lists = tile_lists.reshape(-1)
    entry_total = flat_lists.shape[0]
    owner_of = flat_lists // tiles_dev
    local_tile = flat_lists % tiles_dev
    positions = jnp.arange(entry_total, dtype=jnp.int32)
    same_owner = owner_of[:, None] == owner_of[None, :]
    earlier = positions[None, :] < positions[:, None]
    rank_in_owner = jnp.sum((same_owner & earlier).astype(jnp.int32), axis=1)
    slot_of_entry = owner_of * per_owner + rank_in_owner
    is_kept = positions % list_length < jnp.repeat(tile_counts, list_length)
    return (local_tile, slot_of_entry, is_kept)


def select_by_slot(slot_of_entry, entry_values, slot_span):
    wanted_slots = jnp.arange(slot_span, dtype=jnp.int32)
    placed = slot_of_entry[:, None] == wanted_slots[None, :]
    return jnp.sum(jnp.where(placed, entry_values[:, None], 0), axis=0)


def grouped(array, group_size):
    return array.reshape((array.shape[0] // group_size, group_size) + array.shape[1:])


def attend_block(operands, score_scale):
    query_block, key_block, value_block, key_kept = operands
    scores = (
        jnp.einsum("gqhd,gkhd->ghqk", query_block, key_block, preferred_element_type=jnp.float32)
        * score_scale
    )
    scores = jnp.where(key_kept[:, None, None, :], scores, -jnp.inf)
    row_max = jnp.max(scores, axis=-1, keepdims=True)
    log_total = row_max + jnp.log(jnp.sum(jnp.exp(scores - row_max), axis=-1, keepdims=True))
    weights = jnp.exp(scores - log_total).astype(jnp.bfloat16)
    attended = jnp.einsum(
        "ghqk,gkhd->gqhd", weights, value_block, preferred_element_type=jnp.float32
    )
    return (attended.astype(jnp.bfloat16), log_total[..., 0])


def gradient_block(operands, score_scale):
    query_block, key_block, value_block, key_kept, grad_block, log_total, delta_block = operands
    scores = (
        jnp.einsum("gqhd,gkhd->ghqk", query_block, key_block, preferred_element_type=jnp.float32)
        * score_scale
    )
    scores = jnp.where(key_kept[:, None, None, :], scores, -jnp.inf)
    probs = jnp.exp(scores - log_total[..., None])
    weights = probs.astype(jnp.bfloat16)
    grad_probs = jnp.einsum(
        "gqhd,gkhd->ghqk", grad_block, value_block, preferred_element_type=jnp.float32
    )
    grad_scores = (probs * (grad_probs - delta_block[..., None])).astype(jnp.bfloat16)
    grad_query = (
        jnp.einsum("ghqk,gkhd->gqhd", grad_scores, key_block, preferred_element_type=jnp.float32)
        * score_scale
    )
    grad_key = (
        jnp.einsum("ghqk,gqhd->gkhd", grad_scores, query_block, preferred_element_type=jnp.float32)
        * score_scale
    )
    grad_value = jnp.einsum(
        "ghqk,gqhd->gkhd", weights, grad_block, preferred_element_type=jnp.float32
    )
    return (grad_query, grad_key, grad_value)


def body(queries, keys, values, out_weight, grad_mixed, kv_tiles, kv_counts):
    tok_rows, row_width = queries.shape
    tiles_dev = tok_rows // TILE
    head_count = row_width // HD
    list_length = kv_tiles.shape[1]
    entries = tiles_dev * list_length
    seq_count = lax.axis_size("seq")
    per_owner = entries // seq_count
    score_scale = 1.0 / math.sqrt(HD)
    device = lax.axis_index("seq")
    own_lists = lax.dynamic_slice_in_dim(kv_tiles, device * tiles_dev, tiles_dev, 0)
    own_counts = lax.dynamic_slice_in_dim(kv_counts, device * tiles_dev, tiles_dev, 0)
    local_tile, slot_of_entry, is_kept = entry_layout(own_lists, own_counts, per_owner, tiles_dev)
    positions = jnp.arange(entries, dtype=jnp.int32)
    entry_of_slot = select_by_slot(slot_of_entry, positions, entries)
    asked_slots = select_by_slot(slot_of_entry, jnp.where(is_kept, local_tile, -1), entries)
    wanted = lax.all_to_all(
        asked_slots.reshape(seq_count, per_owner), "seq", split_axis=0, concat_axis=0, tiled=True
    ).reshape(-1)
    key_value = jnp.stack([keys, values], axis=1).reshape(tiles_dev, TILE, 2, row_width)
    outgoing = jnp.take(key_value, jnp.maximum(wanted, 0), axis=0)
    arrived = lax.all_to_all(outgoing, "seq", split_axis=0, concat_axis=0, tiled=True)
    fetched = jnp.take(arrived, slot_of_entry, axis=0).reshape(
        tiles_dev, list_length * TILE, 2, head_count, HD
    )
    key_rows = fetched[:, :, 0]
    value_rows = fetched[:, :, 1]
    key_kept = jnp.repeat(is_kept.reshape(tiles_dev, list_length), TILE, axis=1)
    query_rows = queries.reshape(tiles_dev, TILE, head_count, HD)
    group_size = math.gcd(tiles_dev, max(1, 512 // TILE))
    attended, log_totals = lax.map(
        partial(attend_block, score_scale=score_scale),
        (
            grouped(query_rows, group_size),
            grouped(key_rows, group_size),
            grouped(value_rows, group_size),
            grouped(key_kept, group_size),
        ),
    )
    attention = attended.reshape(tok_rows, row_width)
    log_totals = log_totals.reshape(tiles_dev, head_count, TILE)
    mixed_term = jnp.dot(attention, out_weight, preferred_element_type=jnp.float32)
    mixed = lax.psum_scatter(
        mixed_term.astype(jnp.bfloat16), "head", scatter_dimension=1, tiled=True
    )
    grad_flat = lax.dot_general(
        lax.all_gather(grad_mixed, "head", axis=1, tiled=True),
        out_weight,
        (((1,), (1,)), ((), ())),
        preferred_element_type=jnp.float32,
    )
    weight_part = lax.dot_general(
        attention,
        lax.all_gather(grad_mixed, "head", axis=1, tiled=True),
        (((0,), (0,)), ((), ())),
        preferred_element_type=jnp.float32,
    )
    grad_attention = grad_flat.astype(jnp.bfloat16)
    weight_grad = lax.psum(weight_part.astype(jnp.bfloat16), "seq")
    grad_rows = grad_attention.reshape(tiles_dev, TILE, head_count, HD)
    row_delta = jnp.sum(
        grad_rows.astype(jnp.float32)
        * attended.reshape(tiles_dev, TILE, head_count, HD).astype(jnp.float32),
        axis=-1,
    ).transpose(0, 2, 1)
    local_grads = lax.map(
        partial(gradient_block, score_scale=score_scale),
        (
            grouped(query_rows, group_size),
            grouped(key_rows, group_size),
            grouped(value_rows, group_size),
            grouped(key_kept, group_size),
            grouped(grad_rows, group_size),
            grouped(log_totals, group_size),
            grouped(row_delta, group_size),
        ),
    )
    grad_queries = local_grads[0].reshape(tok_rows, row_width).astype(jnp.bfloat16)
    grad_key, grad_value = (local_grads[1], local_grads[2])
    returned = jnp.stack(
        [grad_key.reshape(entries, TILE, row_width), grad_value.reshape(entries, TILE, row_width)],
        axis=2,
    )
    returned = jnp.take(returned, entry_of_slot, axis=0)
    summed_in = lax.all_to_all(
        returned.astype(jnp.bfloat16), "seq", split_axis=0, concat_axis=0, tiled=True
    ).astype(returned.dtype)
    owner_pick = (wanted[None, :] == jnp.arange(tiles_dev, dtype=jnp.int32)[:, None]).astype(
        jnp.float32
    )
    key_value_grads = jnp.einsum(
        "ts,sxyw->txyw", owner_pick, summed_in, precision=lax.Precision.HIGHEST
    )
    grad_keys = key_value_grads[:, :, 0].reshape(tok_rows, row_width).astype(jnp.bfloat16)
    grad_values = key_value_grads[:, :, 1].reshape(tok_rows, row_width).astype(jnp.bfloat16)
    return (mixed, grad_queries, grad_keys, grad_values, weight_grad)


def solution(mesh):
    return jax.shard_map(
        body,
        mesh=mesh,
        in_specs=(
            P("seq", "head"),
            P("seq", "head"),
            P("seq", "head"),
            P("head", None),
            P("seq", "head"),
            P(),
            P(),
        ),
        out_specs=(
            P("seq", "head"),
            P("seq", "head"),
            P("seq", "head"),
            P("seq", "head"),
            P("head", None),
        ),
        check_vma=False,
    )
```

profile of v0, /device:TPU:2, one launch (start us, length us, event | category | flops | bytes accessed | tf_op | source)
XLA Modules:
  0.0 324.2 jit_solution(10216280520418321318)
XLA Ops:
  7.2 0.8 dynamic_slice.33
  8.1 0.8 constant_dynamic-slice_fusion
  9.1 0.2 convert_reduce_fusion
  9.4 0.7 copy.88
  10.1 10.2 %all-to-all-start = ((s32[32,1,1]{2,1,0:T(1,128)}), s32[32,1,1]{2,1,0:T(1,128)S(1)}, u32[]{:S(2)}, u32[]{:S(2)}) async-start(s32[32,1,1]{2,1,0:T(1,128)} %copy.88), calls=%async_computation | async-start | bytes 32768 | tf_op jit(solution)/shard_map/all_to_all | solution.py:97
  20.3 0.9 pad_maximum_fusion.1
  21.2 7.6 %all-to-all-done = s32[32,1,1]{2,1,0:T(1,128)S(1)} async-done(((s32[32,1,1]{2,1,0:T(1,128)}), s32[32,1,1]{2,1,0:T(1,128)S(1)}, u32[]{:S(2)}, u32[]{:S(2)}) %all-to-all-start) | async-done | bytes 160 | tf_op jit(solution)/shard_map/all_to_all | solution.py:97
  28.8 1.2 fusion.23
  30.0 0.7 gather_fusion
  30.8 1.1 broadcast_select_fusion
  31.9 5.2 %all-to-all-start.1 = ((bf16[32,64,2,128]{3,1,2,0:T(8,128)(2,1)}), bf16[32,64,2,128]{3,1,2,0:T(8,128)(2,1)S(1)}, u32[]{:S(2)}, u32[]{:S(2)}) async-start(bf16[32,64,2,128]{3,1,2,0:T(8,128)(2,1)} %broadcast_select_fusion), calls=%async_computation.1 | async-start | bytes 2097152 | tf_op jit(solution)/shard_map/all_to_all | solution.py:102
  37.1 0.7 all-gather.2.cloned.1.call-update
  38.8 0.5 compare_and_fusion
  39.3 24.8 %all-to-all-done.1 = bf16[32,64,2,128]{3,1,2,0:T(8,128)(2,1)S(1)} async-done(((bf16[32,64,2,128]{3,1,2,0:T(8,128)(2,1)}), bf16[32,64,2,128]{3,1,2,0:T(8,128)(2,1)S(1)}, u32[]{:S(2)}, u32[]{:S(2)}) %all-to-all-start.1) | async-done | bytes 1048608 | tf_op jit(solution)/shard_map/all_to_all | solution.py:102
  64.1 1.6 gather_fusion.1
  65.7 3.9 %copy.89 = bf16[32,64,2,128]{1,0,3,2:T(8,128)(2,1)S(1)} copy(bf16[32,64,2,128]{3,1,2,0:T(8,128)(2,1)} %gather_fusion.1) | data formatting | bytes 2097152 | tf_op jit(solution)/shard_map/jit(_take)/gather | solution.py:103
  69.7 2.0 gather.16
  71.6 1.4 copy_select_fusion
  73.1 0.4 fusion.25
  73.5 0.3 exponential_reduce_fusion
  73.9 13.1 %all-gather.2.cloned.1.call-done = bf16[256,3072]{0,1:T(8,128)(2,1)} async-done(((bf16[256,192]{0,1:T(8,128)(2,1)}), bf16[256,3072]{0,1:T(8,128)(2,1)}) %all-gather.2.cloned.1.call-update) | async-done | bytes 1572880 | tf_op jit(solution)/shard_map/all_gather | solution.py:127
  87.0 2.0 convolution_convert_fusion.4
  89.2 0.4 multiply_reduce_fusion
  89.6 0.1 copy.92
  89.9 3.0 convolution_convert_fusion.1
  92.9 0.2 reduce-scatter.2.cloned.1.call-start
  93.1 0.4 fusion.4
  93.5 2.0 fusion
  95.5 3.6 %copy.107 = bf16[4,512,2,64]{3,2,1,0:T(2,128)(2,1)} copy(bf16[4,512,2,64]{1,3,2,0:T(8,128)(2,1)} %fusion) | data formatting | bytes 1048576 | tf_op jit(solution)/shard_map/stack;reshape | solution.py:160
  99.1 3.1 reshape.319
  102.2 2.6 convolution_convert_fusion
  104.8 1.2 convolution_bitcast_fusion
  106.0 2.3 copy.108
  108.3 1.3 reshape.320
  109.6 2.3 pad_maximum_fusion
  111.9 2.0 gather_fusion.2
  113.9 0.3 select_convert_fusion
  114.2 2.0 copy.102
  116.2 9.8 %all-to-all-start.2 = ((bf16[32,64,2,128]{3,2,1,0:T(2,128)(2,1)}), bf16[32,64,2,128]{3,2,1,0:T(2,128)(2,1)S(1)}, u32[]{:S(2)}, u32[]{:S(2)}) async-start(bf16[32,64,2,128]{3,2,1,0:T(2,128)(2,1)} %copy.102), calls=%async_computation.3 | async-start | bytes 2097152 | tf_op jit(solution)/shard_map/all_to_all | solution.py:165
  126.0 0.3 fusion.7
  126.5 0.7 convert_element_type.68
  127.2 26.9 %all-to-all-done.2 = bf16[32,64,2,128]{3,2,1,0:T(2,128)(2,1)S(1)} async-done(((bf16[32,64,2,128]{3,2,1,0:T(2,128)(2,1)}), bf16[32,64,2,128]{3,2,1,0:T(2,128)(2,1)S(1)}, u32[]{:S(2)}, u32[]{:S(2)}) %all-to-all-start.2) | async-done | bytes 1048608 | tf_op jit(solution)/shard_map/all_to_all | solution.py:165
  154.1 0.7 convolution_convert_fusion.3
  154.9 0.6 copy.105
  155.5 0.6 copy.104
  156.1 95.3 %all-reduce.2.cloned.1.call-done = bf16[128,3072]{1,0:T(8,128)(2,1)} async-done(((bf16[128,3072]{1,0:T(8,128)(2,1)}), bf16[128,3072]{1,0:T(8,128)(2,1)}) %all-reduce.2.cloned.1.call-update) | async-done | bytes 786448 | tf_op jit(solution)/shard_map/psum | solution.py:139
  251.4 64.2 %reduce-scatter.2.cloned.1.call-done = bf16[256,192]{0,1:T(8,128)(2,1)} async-done(((bf16[256,3072]{0,1:T(8,128)(2,1)}), bf16[256,192]{0,1:T(8,128)(2,1)}) %reduce-scatter.2.cloned.1.call-update) | async-done | bytes 98320 | tf_op jit(solution)/shard_map/reduce_scatter | solution.py:123
  315.6 2.1 copy.116
  (43 shorter events, 1.9 us)
Async XLA Ops:
  7.2 79.8 %copy-start = (bf16[128,3072]{1,0:T(8,128)(2,1)S(1)}, bf16[128,3072]{1,0:T(8,128)(2,1)}, u32[]{:S(2)}) copy-start(bf16[128,3072]{1,0:T(8,128)(2,1)} %param.10) | copy-start | bytes 2359300
  10.1 18.7 %all-to-all-start = ((s32[32,1,1]{2,1,0:T(1,128)}), s32[32,1,1]{2,1,0:T(1,128)S(1)}, u32[]{:S(2)}, u32[]{:S(2)}) async-start(s32[32,1,1]{2,1,0:T(1,128)} %copy.88), calls=%async_computation | async-start | bytes 32768 | tf_op jit(solution)/shard_map/all_to_all | solution.py:97
  31.9 6.5 %copy-start.3 = (bf16[256,128]{1,0:T(8,128)(2,1)S(1)}, bf16[256,128]{1,0:T(8,128)(2,1)}, u32[]{:S(2)}) copy-start(bf16[256,128]{1,0:T(8,128)(2,1)} %param.7) | copy-start | bytes 196612
  31.9 32.2 %all-to-all-start.1 = ((bf16[32,64,2,128]{3,1,2,0:T(8,128)(2,1)}), bf16[32,64,2,128]{3,1,2,0:T(8,128)(2,1)S(1)}, u32[]{:S(2)}, u32[]{:S(2)}) async-start(bf16[32,64,2,128]{3,1,2,0:T(8,128)(2,1)} %broadcast_select_fusion), calls=%async_computation.1 | async-start | bytes 2097152 | tf_op jit(solution)/shard_map/all_to_all | solution.py:102
  37.1 49.9 %all-gather.2.cloned.1.call-start = ((), (), s32[]{:S(2)}) async-start(), calls=%async_computation.5 | async-start | bytes 1671168 | tf_op jit(solution)/shard_map/all_gather | solution.py:127
  37.8 213.6 %all-reduce.2.cloned.1.call-start = ((), (), s32[]{:S(2)}) async-start(), calls=%async_computation.6 | async-start | bytes 1572864 | tf_op jit(solution)/shard_map/psum | solution.py:139
  38.7 34.4 %copy-start.1 = (bf16[4,64,2,64]{1,3,2,0:T(8,128)(2,1)}, bf16[4,64,2,64]{1,3,2,0:T(8,128)(2,1)S(1)}, u32[]{:S(2)}) copy-start(bf16[4,64,2,64]{1,3,2,0:T(8,128)(2,1)S(1)} %copy.96) | copy-start | bytes 196612
  89.9 3.0 copy-start.2
  92.9 222.7 %reduce-scatter.2.cloned.1.call-start = ((), (), s32[]{:S(2)}) async-start(), calls=%async_computation.4 | async-start | bytes 1671168 | tf_op jit(solution)/shard_map/reduce_scatter | solution.py:123
  111.9 2.0 copy-start.4
  116.2 37.9 %all-to-all-start.2 = ((bf16[32,64,2,128]{3,2,1,0:T(2,128)(2,1)}), bf16[32,64,2,128]{3,2,1,0:T(2,128)(2,1)S(1)}, u32[]{:S(2)}, u32[]{:S(2)}) async-start(bf16[32,64,2,128]{3,2,1,0:T(2,128)(2,1)} %copy.102), calls=%async_computation.3 | async-start | bytes 2097152 | tf_op jit(solution)/shard_map/all_to_all | solution.py:165
Sparse Core Ops, SparseCore 0:
  40.0 46.8 all-gather.1
  93.0 158.3 all-reduce.1
  254.8 60.7 reduce-scatter.1
where the time goes:
time: 325 us; the launch traced here: 324 us
  waiting for transfers between devices  233 us (72%)
  local copies, waits for them, and re-layouts  30.7 us (9%)
  starting transfers between devices  25.5 us (8%)
  between operations  14 us (4%)
  matrix products  12.9 us (4%)
  other arithmetic  8.53 us (3%)
    psum x1, waiting for transfers between devices, body(): weight_grad = lax.psum(weight_part.astype(jnp.bfloat16), 'seq')  95.3 us
    reduce_scatter x1, waiting for transfers between devices, body(): lax.psum_scatter(mixed_term.astype(jnp.bfloat16), 'head', scatter_dimensi...  64.2 us
    all_to_all x1, waiting for transfers between devices, body(): lax.all_to_all(returned.astype(jnp.bfloat16), 'seq', split_axis=0, concat...  26.9 us
    all_to_all x1, waiting for transfers between devices, body(): lax.all_to_all(outgoing, 'seq', split_axis=0, concat_axis=0, tiled=True)  24.8 us
    all_gather x1, waiting for transfers between devices, body(): lax.all_gather(grad_mixed, 'head', axis=1, tiled=True)  13.1 us
    another operation x4, local copies, waits for them, and re-layouts, body(): jnp.stack([grad_key.reshape(entries, TILE, row_width), grad_value.reshape...  10.3 us
    all_to_all x1, starting transfers between devices, body(): lax.all_to_all(asked_slots.reshape(seq_count, per_owner), 'seq', split_ax...  10.2 us
    all_to_all x1, starting transfers between devices, body(): lax.all_to_all(returned.astype(jnp.bfloat16), 'seq', split_axis=0, concat...  9.81 us
  transfers between devices with their start and end apart: 6, of which 6 were waited for; matrix products, arithmetic and copies ran while one was open for 12% of the time, Pallas kernels for 0%

commit v1 on v0

v1 whole, which is shorter than its diff:
```python
import functools
import math

import jax
import jax.numpy as jnp
from jax import lax
from jax.experimental import pallas as pl
from jax.experimental.pallas import tpu as pltpu
from jax.sharding import PartitionSpec as P

TILE = 64
HD = 64
WIDTH = 2 * HD
STAT_ROWS = 16
BF16 = jnp.bfloat16
F32 = jnp.float32
VMEM = pl.BlockSpec(memory_space=pltpu.VMEM)
SMEM = pl.BlockSpec(memory_space=pltpu.SMEM)
PARAMS = pltpu.CompilerParams(vmem_limit_bytes=32 * 1024 * 1024)
NT = (((1,), (1,)), ((), ()))


def dot(a, b):
    return jnp.dot(a, b, preferred_element_type=F32)


def dot_nt(a, b):
    return lax.dot_general(a, b, NT, preferred_element_type=F32)


def split_heads(rows):
    lane = lax.broadcasted_iota(jnp.int32, rows.shape, 1)
    zero = jnp.zeros_like(rows)
    return jnp.concatenate(
        [jnp.where(lane < HD, rows, zero), jnp.where(lane < HD, zero, rows)], axis=0
    )


def join_heads(rows):
    half = rows.shape[0] // 2
    lane = lax.broadcasted_iota(jnp.int32, (half, rows.shape[1]), 1)
    return jnp.where(lane < HD, rows[:half], rows[half:])


def tables(kv_tiles, kv_counts, seq_count, tiles_dev, device):
    list_length = kv_tiles.shape[1]
    entries = tiles_dev * list_length
    lists = kv_tiles.reshape(seq_count, entries)
    owner = lists // tiles_dev
    position = jnp.arange(entries, dtype=jnp.int32)
    kept = (position % list_length)[None, :] < jnp.repeat(
        kv_counts.reshape(seq_count, tiles_dev), list_length, axis=1
    )
    here = owner == device
    tile_asked = jnp.sum(jnp.where(here, lists % tiles_dev, 0), axis=1)
    used = jnp.sum(jnp.where(here & kept, 1, 0), axis=1)
    own = lax.dynamic_slice_in_dim(owner, device, 1, 0)[0]
    owners = jnp.arange(seq_count, dtype=jnp.int32)
    query_tile = jnp.sum(
        jnp.where(own[None, :] == owners[:, None], position[None, :] // list_length, 0), axis=1
    )
    counts = lax.dynamic_slice_in_dim(kv_counts, device * tiles_dev, tiles_dev, 0)
    counts = jnp.pad(counts, (0, entries - tiles_dev))
    return jnp.stack([tile_asked, used, own, query_tile, counts])


def pack_kernel(table, queries, keys, values, out):
    def step(i, carry):
        tile = pl.ds(pl.multiple_of(table[0, i] * TILE, TILE), TILE)
        out[i, 0:TILE, :] = keys[tile, :]
        out[i, TILE : 2 * TILE, :] = values[tile, :]
        mine = pl.ds(pl.multiple_of(table[3, i] * TILE, TILE), TILE)
        out[i, 2 * TILE : 3 * TILE, :] = queries[mine, :]
        return carry

    lax.fori_loop(0, out.shape[0], step, 0)


def listed(table, fetched, tile, list_length, part):
    return jnp.concatenate(
        [
            fetched[table[2, tile * list_length + j], part * TILE : (part + 1) * TILE, :]
            for j in range(list_length)
        ],
        axis=0,
    )


def tile_scores(table, query2, key_rows, tile, scale):
    scores = dot_nt(query2, key_rows) * scale
    column = lax.broadcasted_iota(jnp.int32, scores.shape, 1)
    return jnp.where(column < table[4, tile] * TILE, scores, -jnp.inf)


def forward_kernel(
    scale, list_length, table, fetched, queries, grad_t, weight, out, attention, grads, stats, spread
):
    tiles = queries.shape[0] // TILE
    seq_count = out.shape[0]
    chunk = grad_t.shape[0] // seq_count
    grads[...] = dot(weight[...], grad_t[...]).T.astype(BF16)
    lane = lax.broadcasted_iota(jnp.int32, (WIDTH, WIDTH), 1)
    table_of_stats = jnp.zeros((WIDTH, WIDTH), F32)
    for tile in range(tiles):
        rows = slice(tile * TILE, (tile + 1) * TILE)
        query2 = split_heads(queries[rows, :])
        key_rows = listed(table, fetched, tile, list_length, 0)
        value_rows = listed(table, fetched, tile, list_length, 1)
        scores = tile_scores(table, query2, key_rows, tile, scale)
        top = jnp.max(scores, axis=1, keepdims=True)
        log_total = top + jnp.log(jnp.sum(jnp.exp(scores - top), axis=1, keepdims=True))
        weights = jnp.exp(scores - log_total).astype(BF16)
        attended = join_heads(dot(weights, value_rows)).astype(BF16)
        attention[rows, :] = attended
        product = grads[rows, :].astype(F32) * attended.astype(F32)
        delta = jnp.sum(split_heads(product), axis=1, keepdims=True)
        table_of_stats = jnp.where(lane == tile, log_total, table_of_stats)
        table_of_stats = jnp.where(lane == tiles + tile, delta, table_of_stats)
    stats[...] = table_of_stats
    by_row = table_of_stats.T
    row = lax.broadcasted_iota(jnp.int32, (STAT_ROWS, WIDTH), 0)
    for tile in range(tiles):
        block = jnp.zeros((STAT_ROWS, WIDTH), F32)
        for at, value in ((0, by_row[tile : tile + 1]), (3, by_row[tiles + tile : tiles + tile + 1])):
            for part in range(3):
                rounded = value.astype(BF16).astype(F32)
                block = jnp.where(row == at + part, rounded, block)
                value = value - rounded
        spread[tile, 0:TILE, :] = grads[tile * TILE : (tile + 1) * TILE, :]
        spread[tile, TILE : TILE + STAT_ROWS, :] = block.astype(BF16)

    def step(i, carry):
        start = pl.multiple_of(i * chunk, chunk)
        part = dot(grad_t[pl.ds(start, chunk), :], attention[...])
        out[i, 0:chunk, :] = part.astype(BF16)
        out[i, chunk : chunk + TILE + STAT_ROWS, :] = spread[table[3, i]]
        return carry

    lax.fori_loop(0, seq_count, step, 0, unroll=4)


def query_kernel(scale, list_length, table, fetched, queries, grads, stats, out):
    tiles = queries.shape[0] // TILE
    for tile in range(tiles):
        rows = slice(tile * TILE, (tile + 1) * TILE)
        key_rows = listed(table, fetched, tile, list_length, 0)
        value_rows = listed(table, fetched, tile, list_length, 1)
        scores = tile_scores(table, split_heads(queries[rows, :]), key_rows, tile, scale)
        probs = jnp.exp(scores - stats[:, tile : tile + 1])
        grad_probs = dot_nt(split_heads(grads[rows, :]), value_rows)
        grad_scores = (probs * (grad_probs - stats[:, tiles + tile : tiles + tile + 1])).astype(BF16)
        out[rows, :] = (join_heads(dot(grad_scores, key_rows)) * scale).astype(BF16)


def sum_kernel(chunk, arrived, out):
    total = arrived[0, 0:chunk, :].astype(F32)
    for i in range(1, arrived.shape[0]):
        total += arrived[i, 0:chunk, :].astype(F32)
    total = total.astype(BF16)
    for i in range(out.shape[0]):
        out[i] = total


def owner_kernel(scale, chunk, group, table, fetched, arrived, keys, values, grad_keys, grad_values, key_sum, value_sum):
    tok_rows = keys.shape[0]
    senders = arrived.shape[0]
    key_tile = lax.broadcasted_iota(jnp.int32, (tok_rows, WIDTH), 0) // TILE
    key_sum[...] = jnp.zeros_like(key_sum)
    value_sum[...] = jnp.zeros_like(value_sum)

    def step(at, carry):
        query2, grad2, logs, deltas, keeps = [], [], [], [], []
        for k in range(group):
            i = at * group + k
            query2.append(split_heads(fetched[i, 2 * TILE : 3 * TILE, :]))
            grad2.append(split_heads(arrived[i, chunk : chunk + TILE, :]))
            parts = arrived[i, chunk + TILE : chunk + TILE + STAT_ROWS, :].astype(F32)
            logs.append(parts[0:1] + parts[1:2] + parts[2:3])
            deltas.append(parts[3:4] + parts[4:5] + parts[5:6])
            wanted = jnp.where(table[1, i] > 0, table[0, i], -1)
            keeps.append(key_tile == wanted)
        query2 = jnp.concatenate(query2, axis=0)
        grad2 = jnp.concatenate(grad2, axis=0)
        log_total = jnp.concatenate(logs, axis=1)
        delta = jnp.concatenate(deltas, axis=1)
        scores = dot_nt(keys[...], query2) * scale
        gaps = scores - log_total
        gaps = jnp.concatenate(
            [
                jnp.where(keeps[k], gaps[:, k * WIDTH : (k + 1) * WIDTH], -jnp.inf)
                for k in range(group)
            ],
            axis=1,
        )
        probs = jnp.exp(gaps)
        grad_probs = dot_nt(values[...], grad2)
        grad_scores = (probs * (grad_probs - delta)).astype(BF16)
        key_sum[...] += dot(grad_scores, query2)
        value_sum[...] += dot(probs.astype(BF16), grad2)
        return carry

    lax.fori_loop(0, senders // group, step, 0)
    grad_keys[...] = (key_sum[...] * scale).astype(BF16)
    grad_values[...] = value_sum[...].astype(BF16)


def exchange(blocks):
    return lax.all_to_all(blocks, "seq", split_axis=0, concat_axis=0, tiled=True)


def body(queries, keys, values, out_weight, grad_mixed, kv_tiles, kv_counts):
    tok_rows, row_width = queries.shape
    tiles_dev = tok_rows // TILE
    list_length = kv_tiles.shape[1]
    seq_count = lax.axis_size("seq")
    scale = 1.0 / math.sqrt(HD)
    model = out_weight.shape[1]
    chunk = model // seq_count
    device = lax.axis_index("seq")
    block = jax.ShapeDtypeStruct((tok_rows, row_width), BF16)

    table = tables(kv_tiles, kv_counts, seq_count, tiles_dev, device)
    outgoing = pl.pallas_call(
        pack_kernel,
        out_shape=jax.ShapeDtypeStruct((seq_count, 3 * TILE, row_width), BF16),
        in_specs=[SMEM, VMEM, VMEM, VMEM],
        out_specs=VMEM,
        compiler_params=PARAMS,
        name="pack",
    )(table, queries, keys, values)
    grad_t = lax.all_gather(grad_mixed.T, "head", axis=0, tiled=True)
    fetched = exchange(outgoing)

    second, attention, grads, stats = pl.pallas_call(
        functools.partial(forward_kernel, scale, list_length),
        out_shape=(
            jax.ShapeDtypeStruct((seq_count, chunk + TILE + STAT_ROWS, row_width), BF16),
            block,
            block,
            jax.ShapeDtypeStruct((WIDTH, WIDTH), F32),
        ),
        in_specs=[SMEM, VMEM, VMEM, VMEM, VMEM],
        out_specs=(VMEM, VMEM, VMEM, VMEM),
        scratch_shapes=[pltpu.VMEM((tiles_dev, TILE + STAT_ROWS, row_width), BF16)],
        compiler_params=PARAMS,
        name="forward",
    )(table, fetched, queries, grad_t, out_weight)
    arrived = exchange(second)

    mixed_t = lax.dot_general(
        out_weight, attention, (((0,), (1,)), ((), ())), preferred_element_type=F32
    ).astype(BF16)
    mixed = lax.psum_scatter(mixed_t, "head", scatter_dimension=0, tiled=True).T

    grad_queries = pl.pallas_call(
        functools.partial(query_kernel, scale, list_length),
        out_shape=block,
        in_specs=[SMEM, VMEM, VMEM, VMEM, VMEM],
        out_specs=VMEM,
        compiler_params=PARAMS,
        cost_estimate=pl.CostEstimate(flops=400_000_000, bytes_accessed=4_000_000, transcendentals=300_000),
        name="query_grad",
    )(table, fetched, queries, grads, stats)

    third = pl.pallas_call(
        functools.partial(sum_kernel, chunk),
        out_shape=jax.ShapeDtypeStruct((seq_count, chunk, row_width), BF16),
        in_specs=[VMEM],
        out_specs=VMEM,
        compiler_params=PARAMS,
        name="sum_share",
    )(arrived)
    gathered = exchange(third)

    grad_keys, grad_values = pl.pallas_call(
        functools.partial(owner_kernel, scale, chunk, 4),
        out_shape=(block, block),
        in_specs=[SMEM, VMEM, VMEM, VMEM, VMEM],
        out_specs=(VMEM, VMEM),
        scratch_shapes=[pltpu.VMEM((tok_rows, row_width), F32), pltpu.VMEM((tok_rows, row_width), F32)],
        compiler_params=PARAMS,
        cost_estimate=pl.CostEstimate(flops=1_100_000_000, bytes_accessed=4_000_000, transcendentals=1_000_000),
        name="owner_grad",
    )(table, fetched, arrived, keys, values)
    weight_grad = gathered.reshape(model, row_width).T
    return (mixed, grad_queries, grad_keys, grad_values, weight_grad)


def solution(mesh):
    return jax.shard_map(
        body,
        mesh=mesh,
        in_specs=(
            P("seq", "head"),
            P("seq", "head"),
            P("seq", "head"),
            P("head", None),
            P("seq", "head"),
            P(),
            P(),
        ),
        out_specs=(
            P("seq", "head"),
            P("seq", "head"),
            P("seq", "head"),
            P("seq", "head"),
            P("head", None),
        ),
        check_vma=False,
    )
```

time: 325 us -> 167 us (0.51)
  waiting for transfers between devices: 233 us -> 93.9 us
  local copies, waits for them, and re-layouts: 30.7 us -> 12.6 us
  Pallas kernels: 0 us -> 14.2 us
  matrix products: 12.9 us -> 2.86 us
  other arithmetic: 8.53 us -> 1.21 us
    psum x1 -> x0, waiting for transfers between devices: 95.3 us -> none  [body(): weight_grad = lax.psum(weight_part.astype(jnp.bfloat16), 'seq')]
    reduce_scatter x1 -> x0, waiting for transfers between devices: 64.2 us -> none  [body(): lax.psum_scatter(mixed_term.astype(jnp.bfloat16), 'head', scatter_dimensi...]
    all_gather x1, waiting for transfers between devices: 13.1 us -> 48.9 us  [body(): grad_t = lax.all_gather(grad_mixed.T, 'head', axis=0, tiled=True)]
    all_to_all x3, waiting for transfers between devices: 59.3 us -> 44.3 us  [exchange(): lax.all_to_all(blocks, 'seq', split_axis=0, concat_axis=0, tiled=True)]
    pallas_call x0 -> x5, Pallas kernels: none -> 14.2 us  [the longest x1 5.66 us: body(): pl.pallas_call(functools.partial(owner_kernel, scale, chunk, 4), out_shap...]
    gather x5 -> x0, local copies, waits for them, and re-layouts: 10.3 us -> none  [the longest x3 7.54 us: body(): jnp.take(arrived, slot_of_entry, axis=0)]
    another operation x4 -> x2, local copies, waits for them, and re-layouts: 10.3 us -> 0.03 us  [tables(): return jnp.stack([tile_asked, used, own, query_tile, counts])]
    dot_general x10 -> x1, matrix products: 12.9 us -> 2.86 us  [body(): lax.dot_general(out_weight, attention, (((0,), (1,)), ((), ())), preferre...]
  transfers between devices with their start and end apart: 6 -> 5, of which waited for: 6 -> 3; matrix products, arithmetic and copies ran while one was open for 12% -> 5% of each run, Pallas kernels for 0% -> 5%
where the time goes in v1:
time: 167 us; the launch traced here: 166 us
  waiting for transfers between devices  93.9 us (56%)
  starting transfers between devices  26.9 us (16%)
  Pallas kernels  14.2 us (9%)
  between operations  14.2 us (9%)
  local copies, waits for them, and re-layouts  12.6 us (8%)
  matrix products  2.86 us (2%)
    all_gather x1, waiting for transfers between devices, body(): grad_t = lax.all_gather(grad_mixed.T, 'head', axis=0, tiled=True)  48.9 us
    all_to_all x3, waiting for transfers between devices, exchange(): lax.all_to_all(blocks, 'seq', split_axis=0, concat_axis=0, tiled=True)  44.3 us
    all_to_all x3, starting transfers between devices, exchange(): lax.all_to_all(blocks, 'seq', split_axis=0, concat_axis=0, tiled=True)  26.9 us
    unnamed x22, local copies, waits for them, and re-layouts  9.28 us
    pallas_call x1, Pallas kernels, body(): pl.pallas_call(functools.partial(owner_kernel, scale, chunk, 4), out_shap...  5.66 us
    pallas_call x1, Pallas kernels, body(): pl.pallas_call(functools.partial(forward_kernel, scale, list_length), out...  4.11 us
  transfers between devices with their start and end apart: 5, of which 3 were waited for; matrix products, arithmetic and copies ran while one was open for 5% of the time, Pallas kernels for 5%

profile of v1, /device:TPU:2, one launch (start us, length us, event | category | flops | bytes accessed | tf_op | source)
XLA Modules:
  0.0 166.0 jit_solution(10773298275629535975)
XLA Ops:
  7.2 0.8 copy.22
  8.0 0.1 reshape.72
  8.1 0.7 dynamic_slice.7
  8.8 0.8 select_reduce_fusion
  9.7 0.1 reduce_sum.45
  9.8 0.1 reduce_sum.46
  9.9 0.1 reduce_sum.32
  10.0 0.1 reduce_sum.36
  10.2 0.1 select_reduce_fusion.1
  10.3 0.0 copy-start.4
  10.3 0.8 copy-done.4
  11.1 0.0 copy-start.6
  11.1 0.8 copy-done.6
  12.0 0.0 copy-start.8
  12.0 0.8 copy-done.8
  12.8 2.1 %pack.1 = bf16[32,192,128]{2,1,0:T(8,128)(2,1)} custom-call(s32[5,32]{1,0:T(8,128)S(1)} %stack.19.table, bf16[256,128]{1,0:T(8,128)(2,1)S(1)} %copy-done.4, bf16[256,128]{1,0:T(8,128)(2,1)S(1)} %copy-done.6, bf16[256,128]{1,0:T(8,128)(2,1)S(1)} %copy-done.8), custom_call_target="tpu_custom_call" | custom-call | tf_op jit(solution)/shard_map/pack/pallas_call | solution.py:223
  14.9 0.0 copy-start.1
  14.9 0.0 copy-start.5
  14.9 10.4 %all-to-all-start = ((bf16[32,192,128]{2,1,0:T(8,128)(2,1)}), bf16[32,192,128]{2,1,0:T(8,128)(2,1)S(1)}, u32[]{:S(2)}, u32[]{:S(2)}) async-start(bf16[32,192,128]{2,1,0:T(8,128)(2,1)} %pack.1), calls=%async_computation | async-start | bytes 3145728 | tf_op jit(solution)/shard_map/all_to_all | solution.py:208
  25.3 0.0 all-gather.2.cloned.1.call-start
  25.3 0.7 all-gather.2.cloned.1.call-update
  26.0 48.9 %all-gather.2.cloned.1.call-done.grad_t = bf16[3072,256]{1,0:T(8,128)(2,1)} async-done(((bf16[192,256]{1,0:T(8,128)(2,1)}), bf16[3072,256]{1,0:T(8,128)(2,1)}) %all-gather.2.cloned.1.call-update) | async-done | bytes 1572880 | tf_op jit(solution)/shard_map/all_gather | solution.py:231
  74.9 0.0 all-to-all-done.fetched
  74.9 0.0 copy-done.1
  74.9 0.0 copy-done.5
  74.9 0.0 copy-start.2
  74.9 1.4 copy-done.2
  76.3 4.1 %forward.1 = (bf16[32,176,128]{2,1,0:T(8,128)(2,1)S(1)}, bf16[256,128]{1,0:T(8,128)(2,1)S(1)}, bf16[256,128]{1,0:T(8,128)(2,1)S(1)}, f32[128,128]{1,0:T(8,128)S(1)}) custom-call(s32[5,32]{1,0:T(8,128)S(1)} %stack.19.table, bf16[32,192,128]{2,1,0:T(8,128)(2,1)S(1)} %all-to-all-done.fetched, bf16[256,128]{1,0:T(8,128)(2,1)S(1)} %copy-done.5, ...), custom_call_target="tpu_custom_call" | custom-call | tf_op jit(solution)/shard_map/forward/pallas_call | solution.py:234
  80.4 0.0 copy-start.3
  80.5 1.1 copy-done.3
  81.5 9.9 %all-to-all-start.1 = ((bf16[32,176,128]{2,1,0:T(8,128)(2,1)}), bf16[32,176,128]{2,1,0:T(8,128)(2,1)S(1)}, u32[]{:S(2)}, u32[]{:S(2)}) async-start(bf16[32,176,128]{2,1,0:T(8,128)(2,1)} %copy-done.3), calls=%async_computation.1 | async-start | bytes 2883584 | tf_op jit(solution)/shard_map/all_to_all | solution.py:208
  91.4 0.0 reduce-scatter.4.cloned.1.call-start
  91.5 2.9 %fusion = bf16[3072,256]{0,1:T(8,128)(2,1)} fusion(bf16[256,128]{1,0:T(8,128)(2,1)S(1)} %get-tuple-element.11, bf16[128,3072]{1,0:T(8,128)(2,1)} %weight.1), kind=kOutput, calls=%fused_computation.1 | convolution fusion | flops 202113024 | bytes 2424832 | tf_op jit(solution)/shard_map/dot_general | solution.py:250
  94.3 2.6 %copy.29 = bf16[3072,256]{1,0:T(8,128)(2,1)} copy(bf16[3072,256]{0,1:T(8,128)(2,1)} %fusion) | data formatting | bytes 3145728
  96.9 0.0 reduce-scatter.4.cloned.1.call-update
  96.9 30.5 %all-to-all-done.1.arrived = bf16[32,176,128]{2,1,0:T(8,128)(2,1)S(1)} async-done(((bf16[32,176,128]{2,1,0:T(8,128)(2,1)}), bf16[32,176,128]{2,1,0:T(8,128)(2,1)S(1)}, u32[]{:S(2)}, u32[]{:S(2)}) %all-to-all-start.1) | async-done | bytes 1441824 | tf_op jit(solution)/shard_map/all_to_all | solution.py:208
  127.5 0.1 sum_share.1
  127.6 0.0 copy-start
  127.6 0.9 copy-done
  128.5 0.0 copy-start.7
  128.5 0.0 copy-start.9
  128.5 6.6 %all-to-all-start.2 = ((bf16[32,96,128]{2,1,0:T(8,128)(2,1)}), bf16[32,96,128]{2,1,0:T(8,128)(2,1)}, u32[]{:S(2)}, u32[]{:S(2)}) async-start(bf16[32,96,128]{2,1,0:T(8,128)(2,1)} %copy-done), calls=%async_computation.2 | async-start | bytes 1572864 | tf_op jit(solution)/shard_map/all_to_all | solution.py:208
  135.1 2.3 %query_grad.1 = bf16[256,128]{1,0:T(8,128)(2,1)} custom-call(s32[5,32]{1,0:T(8,128)S(1)} %stack.19.table, bf16[32,192,128]{2,1,0:T(8,128)(2,1)S(1)} %all-to-all-done.fetched, bf16[256,128]{1,0:T(8,128)(2,1)S(1)} %copy-done.5, bf16[256,128]{1,0:T(8,128)(2,1)S(1)} %get-tuple-element.12.grads, f32[128,128]{1,0:T(8,128)S(1)} %get-tuple-element.13.stats), custom_call_target="tpu_custom_call" | custom-call | flops 400000000 | bytes 4000000 | tf_op jit(solution)/shard_map/query_grad/pallas_call | solution.py:255
  137.4 0.0 copy-done.7
  137.4 0.0 copy-done.9
  137.4 5.7 %owner_grad.1 = (bf16[256,128]{1,0:T(8,128)(2,1)}, bf16[256,128]{1,0:T(8,128)(2,1)}) custom-call(s32[5,32]{1,0:T(8,128)S(1)} %stack.19.table, bf16[32,192,128]{2,1,0:T(8,128)(2,1)S(1)} %all-to-all-done.fetched, bf16[32,176,128]{2,1,0:T(8,128)(2,1)S(1)} %all-to-all-done.1.arrived, bf16[256,128]{1,0:T(8,128)(2,1)S(1)} %copy-done.7, bf16[256,128]{1,0:T(8,128)(2,1)S(1)} %copy-done.9), custom_call_target="tpu_custom_call" | custom-call | flops 1100000000 | bytes 4000000 | tf_op jit(solution)/shard_map/owner_grad/pallas_call | solution.py:275
  143.0 13.8 %all-to-all-done.2 = bf16[32,96,128]{2,1,0:T(8,128)(2,1)} async-done(((bf16[32,96,128]{2,1,0:T(8,128)(2,1)}), bf16[32,96,128]{2,1,0:T(8,128)(2,1)}, u32[]{:S(2)}, u32[]{:S(2)}) %all-to-all-start.2) | async-done | bytes 786464 | tf_op jit(solution)/shard_map/all_to_all | solution.py:208
  156.8 2.3 %copy.27 = bf16[3072,128]{0,1:T(8,128)(2,1)} copy(bf16[3072,128]{1,0:T(8,128)(2,1)} %bitcast.9) | data formatting | bytes 1572864 | tf_op jit(solution)/shard_map/reshape | solution.py:285
  (9 shorter events, 0.1 us)
Async XLA Ops:
  10.3 0.8 copy-start.4
  11.1 0.8 copy-start.6
  12.0 0.8 copy-start.8
  14.9 60.0 %copy-start.1 = (bf16[128,3072]{1,0:T(8,128)(2,1)S(1)}, bf16[128,3072]{1,0:T(8,128)(2,1)}, u32[]{:S(2)}) copy-start(bf16[128,3072]{1,0:T(8,128)(2,1)} %weight.1) | copy-start | bytes 2359300
  14.9 60.0 %copy-start.5 = (bf16[256,128]{1,0:T(8,128)(2,1)S(1)}, bf16[256,128]{1,0:T(8,128)(2,1)}, u32[]{:S(2)}) copy-start(bf16[256,128]{1,0:T(8,128)(2,1)} %queries.5) | copy-start | bytes 196612
  14.9 60.0 %all-to-all-start = ((bf16[32,192,128]{2,1,0:T(8,128)(2,1)}), bf16[32,192,128]{2,1,0:T(8,128)(2,1)S(1)}, u32[]{:S(2)}, u32[]{:S(2)}) async-start(bf16[32,192,128]{2,1,0:T(8,128)(2,1)} %pack.1), calls=%async_computation | async-start | bytes 3145728 | tf_op jit(solution)/shard_map/all_to_all | solution.py:208
  25.3 49.6 %all-gather.2.cloned.1.call-start = ((), (), s32[]{:S(2)}) async-start(), calls=%async_computation.4 | async-start | bytes 1671168 | tf_op jit(solution)/shard_map/all_gather | solution.py:231
  74.9 1.4 copy-start.2
  80.4 1.1 copy-start.3
  81.5 45.9 %all-to-all-start.1 = ((bf16[32,176,128]{2,1,0:T(8,128)(2,1)}), bf16[32,176,128]{2,1,0:T(8,128)(2,1)S(1)}, u32[]{:S(2)}, u32[]{:S(2)}) async-start(bf16[32,176,128]{2,1,0:T(8,128)(2,1)} %copy-done.3), calls=%async_computation.1 | async-start | bytes 2883584 | tf_op jit(solution)/shard_map/all_to_all | solution.py:208
  91.4 67.7 %reduce-scatter.4.cloned.1.call-start = ((), (), s32[]{:S(2)}) async-start(), calls=%async_computation.5 | async-start | bytes 1671168
  127.6 0.9 copy-start
  128.5 8.9 %copy-start.7 = (bf16[256,128]{1,0:T(8,128)(2,1)S(1)}, bf16[256,128]{1,0:T(8,128)(2,1)}, u32[]{:S(2)}) copy-start(bf16[256,128]{1,0:T(8,128)(2,1)} %keys.3) | copy-start | bytes 196612
  128.5 8.9 %copy-start.9 = (bf16[256,128]{1,0:T(8,128)(2,1)S(1)}, bf16[256,128]{1,0:T(8,128)(2,1)}, u32[]{:S(2)}) copy-start(bf16[256,128]{1,0:T(8,128)(2,1)} %values.3) | copy-start | bytes 196612
  128.5 28.4 %all-to-all-start.2 = ((bf16[32,96,128]{2,1,0:T(8,128)(2,1)}), bf16[32,96,128]{2,1,0:T(8,128)(2,1)}, u32[]{:S(2)}, u32[]{:S(2)}) async-start(bf16[32,96,128]{2,1,0:T(8,128)(2,1)} %copy-done), calls=%async_computation.2 | async-start | bytes 1572864 | tf_op jit(solution)/shard_map/all_to_all | solution.py:208
Sparse Core Ops, SparseCore 0:
  28.2 46.6 all-gather.1
  97.1 60.8 reduce-scatter.3

commit v2 on v1

--- a/solution.py
+++ b/solution.py
@@ -6,18 +6,25 @@
 from jax import lax
 from jax.experimental import pallas as pl
 from jax.experimental.pallas import tpu as pltpu
-from jax.sharding import PartitionSpec as P
+from jax.sharding import Mesh, PartitionSpec as P
 
 TILE = 64
 HD = 64
 WIDTH = 2 * HD
-STAT_ROWS = 16
+STAT_ROWS = 8
+ROW_BLOCKS = 4
+COL_BLOCKS = 8
 BF16 = jnp.bfloat16
 F32 = jnp.float32
 VMEM = pl.BlockSpec(memory_space=pltpu.VMEM)
 SMEM = pl.BlockSpec(memory_space=pltpu.SMEM)
+HBM = pl.BlockSpec(memory_space=pltpu.HBM)
 PARAMS = pltpu.CompilerParams(vmem_limit_bytes=32 * 1024 * 1024)
 NT = (((1,), (1,)), ((), ()))
+
+
+def stay(array):
+    return pltpu.with_memory_space_constraint(array, pltpu.HBM)
 
 
 def dot(a, b):
@@ -42,38 +49,100 @@
     return jnp.where(lane < HD, rows[:half], rows[half:])
 
 
-def tables(kv_tiles, kv_counts, seq_count, tiles_dev, device):
-    list_length = kv_tiles.shape[1]
-    entries = tiles_dev * list_length
-    lists = kv_tiles.reshape(seq_count, entries)
-    owner = lists // tiles_dev
-    position = jnp.arange(entries, dtype=jnp.int32)
-    kept = (position % list_length)[None, :] < jnp.repeat(
-        kv_counts.reshape(seq_count, tiles_dev), list_length, axis=1
-    )
-    here = owner == device
-    tile_asked = jnp.sum(jnp.where(here, lists % tiles_dev, 0), axis=1)
-    used = jnp.sum(jnp.where(here & kept, 1, 0), axis=1)
-    own = lax.dynamic_slice_in_dim(owner, device, 1, 0)[0]
-    owners = jnp.arange(seq_count, dtype=jnp.int32)
-    query_tile = jnp.sum(
-        jnp.where(own[None, :] == owners[:, None], position[None, :] // list_length, 0), axis=1
-    )
-    counts = lax.dynamic_slice_in_dim(kv_counts, device * tiles_dev, tiles_dev, 0)
-    counts = jnp.pad(counts, (0, entries - tiles_dev))
-    return jnp.stack([tile_asked, used, own, query_tile, counts])
-
-
-def pack_kernel(table, queries, keys, values, out):
-    def step(i, carry):
-        tile = pl.ds(pl.multiple_of(table[0, i] * TILE, TILE), TILE)
-        out[i, 0:TILE, :] = keys[tile, :]
-        out[i, TILE : 2 * TILE, :] = values[tile, :]
-        mine = pl.ds(pl.multiple_of(table[3, i] * TILE, TILE), TILE)
-        out[i, 2 * TILE : 3 * TILE, :] = queries[mine, :]
-        return carry
-
-    lax.fori_loop(0, out.shape[0], step, 0)
+def pack_kernel(
+    place, lists_h, counts_h, queries, keys, values, out, table,
+    lists, counts, lists_v, counts_v, staged, codes_v, codes, held, sems,
+):
+    list_length, tile_count = lists_v.shape
+    seq_count = out.shape[0]
+    tiles = tile_count // seq_count
+    device = place[0]
+    pairs = (
+        (lists_h, lists_v), (counts_h, counts_v), (lists_h, lists), (counts_h, counts),
+        (keys, held.at[0]), (values, held.at[1]), (queries, held.at[2]),
+    )
+    loads = [pltpu.make_async_copy(*pair, sems.at[k]) for k, pair in enumerate(pairs)]
+    for load in loads:
+        load.start()
+    for load in loads[:2]:
+        load.wait()
+    listed_tile = lists_v[...]
+    entry = lax.broadcasted_iota(jnp.int32, listed_tile.shape, 0)
+    code = lax.rem(listed_tile, tiles) + jnp.where(entry < counts_v[...], tiles, 0)
+    code = jnp.where(lax.div(listed_tile, tiles) == device, code, 0)
+    code = jnp.broadcast_to(jnp.sum(code, axis=0, keepdims=True), code.shape)
+    codes_v[...] = sum(
+        (pltpu.roll(code, tile_count - tile, 1) for tile in range(1, tiles)), start=code
+    )
+    scalars = pltpu.make_async_copy(codes_v, codes, sems.at[7])
+    scalars.start()
+    for load in loads[2:4]:
+        load.wait()
+    for tile in range(tiles):
+        table[4, tile] = counts[0, device * tiles + tile]
+        for j in range(list_length):
+            owner = lax.div(lists[j, device * tiles + tile], tiles)
+            table[2, tile * list_length + j] = owner
+            table[3, owner] = tile
+    scalars.wait()
+    for load in loads[4:]:
+        load.wait()
+    groups = staged.shape[0]
+    stores = []
+    for group in range(groups):
+        for k in range(seq_count // groups):
+            i = group * (seq_count // groups) + k
+            code = codes[0, i * tiles]
+            asked = lax.rem(code, tiles)
+            table[0, i] = asked
+            table[1, i] = lax.div(code, tiles)
+            tile = pl.ds(pl.multiple_of(asked * TILE, TILE), TILE)
+            staged[group, k, 0:TILE, :] = held[0, tile, :]
+            staged[group, k, TILE : 2 * TILE, :] = held[1, tile, :]
+            mine = pl.ds(pl.multiple_of(table[3, i] * TILE, TILE), TILE)
+            staged[group, k, 2 * TILE : 3 * TILE, :] = held[2, mine, :]
+        span = pl.ds(group * (seq_count // groups), seq_count // groups)
+        stores.append(pltpu.make_async_copy(staged.at[group], out.at[span], sems.at[8 + group]))
+        stores[-1].start()
+    for store in stores:
+        store.wait()
+
+
+def grad_kernel(weight_h, grad_h, grads, grad_t, weight, sems):
+    runs = sems.shape[0] - 1
+    span = grad_t.shape[0] // runs
+    loads = [pltpu.make_async_copy(weight_h, weight, sems.at[runs])]
+    for at in range(runs):
+        rows = pl.ds(at * span, span)
+        loads.append(pltpu.make_async_copy(grad_h.at[rows], grad_t.at[rows], sems.at[at]))
+    for load in loads:
+        load.start()
+    loads[0].wait()
+    total = jnp.zeros((WIDTH, grads.shape[0]), F32)
+    for at in range(runs):
+        loads[1 + at].wait()
+        rows = slice(at * span, (at + 1) * span)
+        total += dot(weight[:, rows], grad_t[rows, :])
+    grads[...] = total.T.astype(BF16)
+
+
+def halves_kernel(run, place, weight, kept, given):
+    weight_t = weight[...].T
+    mine = place[0] == 0
+    for z in range(kept.shape[0] // run):
+        first = weight_t[2 * z * run : (2 * z + 1) * run]
+        second = weight_t[(2 * z + 1) * run : (2 * z + 2) * run]
+        rows = slice(z * run, (z + 1) * run)
+        kept[rows, :] = jnp.where(mine, first, second)
+        given[rows, :] = jnp.where(mine, second, first)
+
+
+def mixed_kernel(kept, got, attention, other, out):
+    step = 256
+    for at in range(0, out.shape[0], step):
+        rows = slice(at, at + step)
+        total = dot_nt(kept[rows, :], attention[...]) + dot_nt(got[rows, :], other[...])
+        out[rows, :] = total.astype(BF16)
 
 
 def listed(table, fetched, tile, list_length, part):
@@ -93,12 +162,15 @@
 
 
 def forward_kernel(
-    scale, list_length, table, fetched, queries, grad_t, weight, out, attention, grads, stats, spread
+    scale, list_length, table, fetched, queries, grad_t, grads, out, attention, stats,
+    spread, staged, sems,
 ):
     tiles = queries.shape[0] // TILE
     seq_count = out.shape[0]
-    chunk = grad_t.shape[0] // seq_count
-    grads[...] = dot(weight[...], grad_t[...]).T.astype(BF16)
+    model = grad_t.shape[0]
+    chunk = model // seq_count
+    wide = model // COL_BLOCKS
+    tall = WIDTH // ROW_BLOCKS
     lane = lax.broadcasted_iota(jnp.int32, (WIDTH, WIDTH), 1)
     table_of_stats = jnp.zeros((WIDTH, WIDTH), F32)
     for tile in range(tiles):
@@ -129,14 +201,23 @@
         spread[tile, 0:TILE, :] = grads[tile * TILE : (tile + 1) * TILE, :]
         spread[tile, TILE : TILE + STAT_ROWS, :] = block.astype(BF16)
 
-    def step(i, carry):
-        start = pl.multiple_of(i * chunk, chunk)
-        part = dot(grad_t[pl.ds(start, chunk), :], attention[...])
-        out[i, 0:chunk, :] = part.astype(BF16)
-        out[i, chunk : chunk + TILE + STAT_ROWS, :] = spread[table[3, i]]
-        return carry
-
-    lax.fori_loop(0, seq_count, step, 0, unroll=4)
+    for i in range(seq_count):
+        staged[i, chunk : chunk + TILE + STAT_ROWS, :] = spread[table[3, i]]
+    attention_t = attention[...].astype(F32).T.astype(BF16)
+    stores = []
+    for at in range(COL_BLOCKS):
+        part = dot_nt(attention_t, grad_t[at * wide : (at + 1) * wide, :]).astype(BF16)
+        for down in range(ROW_BLOCKS):
+            for k in range(wide // WIDTH):
+                staged[at * ROW_BLOCKS + down, k * tall : (k + 1) * tall, :] = part[
+                    down * tall : (down + 1) * tall, k * WIDTH : (k + 1) * WIDTH
+                ]
+        if at % 2 == 1:
+            span = pl.ds((at - 1) * ROW_BLOCKS, 2 * ROW_BLOCKS)
+            stores.append(pltpu.make_async_copy(staged.at[span], out.at[span], sems.at[at // 2]))
+            stores[-1].start()
+    for store in stores:
+        store.wait()
 
 
 def query_kernel(scale, list_length, table, fetched, queries, grads, stats, out):
@@ -152,13 +233,20 @@
         out[rows, :] = (join_heads(dot(grad_scores, key_rows)) * scale).astype(BF16)
 
 
-def sum_kernel(chunk, arrived, out):
+def sum_kernel(chunk, arrived, out, total_of, sems):
     total = arrived[0, 0:chunk, :].astype(F32)
     for i in range(1, arrived.shape[0]):
         total += arrived[i, 0:chunk, :].astype(F32)
     total = total.astype(BF16)
-    for i in range(out.shape[0]):
-        out[i] = total
+    copies = total_of.shape[0]
+    for i in range(copies):
+        total_of[i] = total
+    stores = []
+    for at in range(out.shape[0] // copies):
+        stores.append(pltpu.make_async_copy(total_of, out.at[pl.ds(at * copies, copies)], sems.at[at]))
+        stores[-1].start()
+    for store in stores:
+        store.wait()
 
 
 def owner_kernel(scale, chunk, group, table, fetched, arrived, keys, values, grad_keys, grad_values, key_sum, value_sum):
@@ -204,8 +292,35 @@
     grad_values[...] = value_sum[...].astype(BF16)
 
 
+def assemble_kernel(gathered, out, held, staged, sems):
+    tall = out.shape[0] // ROW_BLOCKS
+    wide = out.shape[1] // COL_BLOCKS
+    loads, stores = [], []
+    for at in range(COL_BLOCKS):
+        span = pl.ds(at * ROW_BLOCKS, ROW_BLOCKS)
+        loads.append(pltpu.make_async_copy(gathered.at[span], held.at[span], sems.at[COL_BLOCKS + at]))
+        loads[-1].start()
+    for at in range(COL_BLOCKS):
+        loads[at].wait()
+        for down in range(ROW_BLOCKS):
+            for k in range(wide // WIDTH):
+                column = at * wide + k * WIDTH
+                staged[down * tall : (down + 1) * tall, column : column + WIDTH] = held[
+                    at * ROW_BLOCKS + down, k * tall : (k + 1) * tall, :
+                ]
+        span = pl.ds(at * wide, wide)
+        stores.append(pltpu.make_async_copy(staged.at[:, span], out.at[:, span], sems.at[at]))
+        stores[-1].start()
+    for store in stores:
+        store.wait()
+
+
 def exchange(blocks):
     return lax.all_to_all(blocks, "seq", split_axis=0, concat_axis=0, tiled=True)
+
+
+def swap_cores(array):
+    return lax.ppermute(array, "core", [(0, 1), (1, 0)])
 
 
 def body(queries, keys, values, out_weight, grad_mixed, kv_tiles, kv_counts):
@@ -219,38 +334,91 @@
     device = lax.axis_index("seq")
     block = jax.ShapeDtypeStruct((tok_rows, row_width), BF16)
 
-    table = tables(kv_tiles, kv_counts, seq_count, tiles_dev, device)
-    outgoing = pl.pallas_call(
+    grad_t = lax.all_gather(grad_mixed.T, ("z", "core"), axis=0, tiled=True)
+    lists = kv_tiles.T
+    groups = 4
+    outgoing, table = pl.pallas_call(
         pack_kernel,
-        out_shape=jax.ShapeDtypeStruct((seq_count, 3 * TILE, row_width), BF16),
-        in_specs=[SMEM, VMEM, VMEM, VMEM],
-        out_specs=VMEM,
+        out_shape=(
+            pltpu.HBM((seq_count, 3 * TILE, row_width), BF16),
+            jax.ShapeDtypeStruct((5, seq_count), jnp.int32),
+        ),
+        in_specs=[SMEM, HBM, HBM, HBM, HBM, HBM],
+        out_specs=(HBM, SMEM),
+        scratch_shapes=[
+            pltpu.SMEM(lists.shape, jnp.int32),
+            pltpu.SMEM((1,) + kv_counts.shape, jnp.int32),
+            pltpu.VMEM(lists.shape, jnp.int32),
+            pltpu.VMEM((1,) + kv_counts.shape, jnp.int32),
+            pltpu.VMEM((groups, seq_count // groups, 3 * TILE, row_width), BF16),
+            pltpu.VMEM(lists.shape, jnp.int32),
+            pltpu.SMEM(lists.shape, jnp.int32),
+            pltpu.VMEM((3, tok_rows, row_width), BF16),
+            pltpu.SemaphoreType.DMA((8 + groups,)),
+        ],
         compiler_params=PARAMS,
         name="pack",
-    )(table, queries, keys, values)
-    grad_t = lax.all_gather(grad_mixed.T, "head", axis=0, tiled=True)
+    )(
+        device[None].astype(jnp.int32),
+        stay(lists),
+        stay(kv_counts[None, :]),
+        stay(queries),
+        stay(keys),
+        stay(values),
+    )
     fetched = exchange(outgoing)
-
-    second, attention, grads, stats = pl.pallas_call(
+    half = jax.ShapeDtypeStruct((model // 2, row_width), BF16)
+    kept, given = pl.pallas_call(
+        functools.partial(halves_kernel, grad_mixed.shape[1]),
+        out_shape=(half, half),
+        in_specs=[SMEM, VMEM],
+        out_specs=(VMEM, VMEM),
+        compiler_params=PARAMS,
+        name="weight_halves",
+    )(lax.axis_index("core")[None].astype(jnp.int32), out_weight)
+    got = swap_cores(given)
+    grads, grad_t = pl.pallas_call(
+        grad_kernel,
+        out_shape=(block, jax.ShapeDtypeStruct((model, tok_rows), BF16)),
+        in_specs=[HBM, HBM],
+        out_specs=(VMEM, VMEM),
+        scratch_shapes=[
+            pltpu.VMEM(out_weight.shape, BF16),
+            pltpu.SemaphoreType.DMA((5,)),
+        ],
+        compiler_params=PARAMS,
+        cost_estimate=pl.CostEstimate(flops=30_000_000_000, bytes_accessed=100_000_000, transcendentals=0),
+        name="attention_grad",
+    )(stay(out_weight), stay(grad_t))
+
+    second, attention, stats = pl.pallas_call(
         functools.partial(forward_kernel, scale, list_length),
         out_shape=(
-            jax.ShapeDtypeStruct((seq_count, chunk + TILE + STAT_ROWS, row_width), BF16),
-            block,
+            pltpu.HBM((seq_count, chunk + TILE + STAT_ROWS, row_width), BF16),
             block,
             jax.ShapeDtypeStruct((WIDTH, WIDTH), F32),
         ),
         in_specs=[SMEM, VMEM, VMEM, VMEM, VMEM],
-        out_specs=(VMEM, VMEM, VMEM, VMEM),
-        scratch_shapes=[pltpu.VMEM((tiles_dev, TILE + STAT_ROWS, row_width), BF16)],
+        out_specs=(HBM, VMEM, VMEM),
+        scratch_shapes=[
+            pltpu.VMEM((tiles_dev, TILE + STAT_ROWS, row_width), BF16),
+            pltpu.VMEM((seq_count, chunk + TILE + STAT_ROWS, row_width), BF16),
+            pltpu.SemaphoreType.DMA((COL_BLOCKS // 2,)),
+        ],
         compiler_params=PARAMS,
         name="forward",
-    )(table, fetched, queries, grad_t, out_weight)
+    )(table, fetched, queries, grad_t, grads)
     arrived = exchange(second)
 
-    mixed_t = lax.dot_general(
-        out_weight, attention, (((0,), (1,)), ((), ())), preferred_element_type=F32
-    ).astype(BF16)
-    mixed = lax.psum_scatter(mixed_t, "head", scatter_dimension=0, tiled=True).T
+    mixed_t = pl.pallas_call(
+        mixed_kernel,
+        out_shape=jax.ShapeDtypeStruct((model // 2, tok_rows), BF16),
+        in_specs=[VMEM, VMEM, VMEM, VMEM],
+        out_specs=VMEM,
+        compiler_params=PARAMS,
+        name="mixed_share",
+    )(kept, got, attention, swap_cores(attention))
+    mixed = lax.psum_scatter(mixed_t, "z", scatter_dimension=0, tiled=True).T
 
     grad_queries = pl.pallas_call(
         functools.partial(query_kernel, scale, list_length),
@@ -264,9 +432,10 @@
 
     third = pl.pallas_call(
         functools.partial(sum_kernel, chunk),
-        out_shape=jax.ShapeDtypeStruct((seq_count, chunk, row_width), BF16),
+        out_shape=pltpu.HBM((seq_count, chunk, row_width), BF16),
         in_specs=[VMEM],
-        out_specs=VMEM,
+        out_specs=HBM,
+        scratch_shapes=[pltpu.VMEM((4, chunk, row_width), BF16), pltpu.SemaphoreType.DMA((seq_count // 4,))],
         compiler_params=PARAMS,
         name="sum_share",
     )(arrived)
@@ -282,29 +451,31 @@
         cost_estimate=pl.CostEstimate(flops=1_100_000_000, bytes_accessed=4_000_000, transcendentals=1_000_000),
         name="owner_grad",
     )(table, fetched, arrived, keys, values)
-    weight_grad = gathered.reshape(model, row_width).T
+    weight_grad = pl.pallas_call(
+        assemble_kernel,
+        out_shape=pltpu.HBM(out_weight.shape, BF16),
+        in_specs=[HBM],
+        out_specs=HBM,
+        scratch_shapes=[
+            pltpu.VMEM((seq_count, chunk, row_width), BF16),
+            pltpu.VMEM(out_weight.shape, BF16),
+            pltpu.SemaphoreType.DMA((2 * COL_BLOCKS,)),
+        ],
+        compiler_params=PARAMS,
+        name="assemble",
+    )(stay(gathered))
     return (mixed, grad_queries, grad_keys, grad_values, weight_grad)
 
 
 def solution(mesh):
+    seq_count, head_count = mesh.devices.shape
+    split = Mesh(mesh.devices.reshape(seq_count, head_count // 2, 2), ("seq", "z", "core"))
+    both = P("seq", ("z", "core"))
+    rows = P(("z", "core"), None)
     return jax.shard_map(
         body,
-        mesh=mesh,
-        in_specs=(
-            P("seq", "head"),
-            P("seq", "head"),
-            P("seq", "head"),
-            P("head", None),
-            P("seq", "head"),
-            P(),
-            P(),
-        ),
-        out_specs=(
-            P("seq", "head"),
-            P("seq", "head"),
-            P("seq", "head"),
-            P("seq", "head"),
-            P("head", None),
-        ),
+        mesh=split,
+        in_specs=(both, both, both, rows, both, P(), P()),
+        out_specs=(both, both, both, both, rows),
         check_vma=False,
     )

time: 167 us -> 147 us (0.88)
  waiting for transfers between devices: 93.9 us -> 78 us
  local copies, waits for them, and re-layouts: 12.6 us -> 2.02 us
  Pallas kernels: 14.2 us -> 21 us
  starting transfers between devices: 26.9 us -> 30.8 us
  matrix products: 2.86 us -> 0 us
    all_gather x1, waiting for transfers between devices: 48.9 us -> 35.8 us  [body(): grad_t = lax.all_gather(grad_mixed.T, ('z', 'core'), axis=0, tiled=True)]
    unnamed x22 -> x10, local copies, waits for them, and re-layouts: 9.28 us -> 2.02 us
    pallas_call x2 -> x6, Pallas kernels: 2.18 us -> 9.39 us  [the longest x1 3.31 us: body(): pl.pallas_call(pack_kernel, out_shape=(pltpu.HBM((seq_count, 3 * TILE, ro...]
    ppermute x0 -> x2, starting transfers between devices: none -> 4.33 us  [swap_cores(): return lax.ppermute(array, 'core', [(0, 1), (1, 0)])]
    all_to_all x3, waiting for transfers between devices: 44.3 us -> 40.7 us  [exchange(): lax.all_to_all(blocks, 'seq', split_axis=0, concat_axis=0, tiled=True)]
    dot_general x1 -> x0, matrix products: 2.86 us -> none  [body(): lax.dot_general(out_weight, attention, (((0,), (1,)), ((), ())), preferre...]
    reshape x2 -> x0, local copies, waits for them, and re-layouts: 2.37 us -> none  [the longest x1 2.29 us: body(): weight_grad = gathered.reshape(model, row_width).T]
  transfers between devices with their start and end apart: 5 -> 7, of which waited for: 3 -> 5; matrix products, arithmetic and copies ran while one was open for 5% -> 0% of each run, Pallas kernels for 5% -> 12%
where the time goes in v2:
time: 147 us; the launch traced here: 146 us
  waiting for transfers between devices  78 us (53%)
  starting transfers between devices  30.8 us (21%)
  Pallas kernels  21 us (14%)
  between operations  14.2 us (10%)
  local copies, waits for them, and re-layouts  2.02 us (1%)
    all_to_all x3, waiting for transfers between devices, exchange(): lax.all_to_all(blocks, 'seq', split_axis=0, concat_axis=0, tiled=True)  40.7 us
    all_gather x1, waiting for transfers between devices, body(): grad_t = lax.all_gather(grad_mixed.T, ('z', 'core'), axis=0, tiled=True)  35.8 us
    all_to_all x3, starting transfers between devices, exchange(): lax.all_to_all(blocks, 'seq', split_axis=0, concat_axis=0, tiled=True)  26.4 us
    pallas_call x1, Pallas kernels, body(): pl.pallas_call(functools.partial(owner_kernel, scale, chunk, 4), out_shap...  5.73 us
    ppermute x2, starting transfers between devices, swap_cores(): return lax.ppermute(array, 'core', [(0, 1), (1, 0)])  4.33 us
    pallas_call x1, Pallas kernels, body(): pl.pallas_call(functools.partial(forward_kernel, scale, list_length), out...  3.63 us
    pallas_call x1, Pallas kernels, body(): pl.pallas_call(pack_kernel, out_shape=(pltpu.HBM((seq_count, 3 * TILE, ro...  3.31 us
  transfers between devices with their start and end apart: 7, of which 5 were waited for; matrix products, arithmetic and copies ran while one was open for 0% of the time, Pallas kernels for 12%

profile of v2, /device:TPU:2, one launch (start us, length us, event | category | flops | bytes accessed | tf_op | source)
XLA Modules:
  0.0 146.0 jit_solution(2852038137821437042)
XLA Ops:
  7.2 0.0 all-gather.2.cloned.1.call-start
  7.2 0.7 all-gather.2.cloned.1.call-update
  7.9 3.3 %pack.1 = (bf16[32,192,128]{2,1,0:T(8,128)(2,1)}, s32[5,32]{1,0:T(8,128)S(1)}) custom-call(s32[1]{0:T(128)} %bitcast.1.place, s32[8,128]{1,0:T(8,128)} %bitcast.7, s32[1,128]{1,0:T(1,128)} %bitcast.8, bf16[256,128]{1,0:T(8,128)(2,1)} %queries.5, bf16[256,128]{1,0:T(8,128)(2,1)} %keys.3, bf16[256,128]{1,0:T(8,128)(2,1)} %values.3), custom_call_target="tpu_custom_call" | custom-call | tf_op jit(solution)/shard_map/pack/pallas_call | solution.py:340
  11.2 10.3 %all-to-all-start = ((bf16[32,192,128]{2,1,0:T(8,128)(2,1)}), bf16[32,192,128]{2,1,0:T(8,128)(2,1)S(1)}, u32[]{:S(2)}, u32[]{:S(2)}) async-start(bf16[32,192,128]{2,1,0:T(8,128)(2,1)} %get-tuple-element.19), calls=%async_computation | async-start | bytes 3145728 | tf_op jit(solution)/shard_map/all_to_all | solution.py:319
  21.5 0.0 copy-start.2
  21.5 35.8 %all-gather.2.cloned.1.call-done.grad_h = bf16[3072,256]{1,0:T(8,128)(2,1)} async-done(((bf16[192,256]{1,0:T(8,128)(2,1)}), bf16[3072,256]{1,0:T(8,128)(2,1)}) %all-gather.2.cloned.1.call-update) | async-done | bytes 1572880 | tf_op jit(solution)/shard_map/all_gather | solution.py:337
  57.3 2.2 %attention_grad.1 = (bf16[256,128]{1,0:T(8,128)(2,1)S(1)}, bf16[3072,256]{1,0:T(8,128)(2,1)S(1)}) custom-call(bf16[128,3072]{1,0:T(8,128)(2,1)} %weight_h.1, bf16[3072,256]{1,0:T(8,128)(2,1)} %all-gather.2.cloned.1.call-done.grad_h), custom_call_target="tpu_custom_call" | custom-call | flops 30000001024 | bytes 100000000 | tf_op jit(solution)/shard_map/attention_grad/pallas_call | solution.py:380
  59.5 0.4 all-to-all-done.fetched
  59.8 0.0 copy-done.2
  59.9 3.6 %forward.1 = (bf16[32,168,128]{2,1,0:T(8,128)(2,1)}, bf16[256,128]{1,0:T(8,128)(2,1)S(1)}, f32[128,128]{1,0:T(8,128)S(1)}) custom-call(s32[5,32]{1,0:T(8,128)S(1)} %get-tuple-element.18.table, bf16[32,192,128]{2,1,0:T(8,128)(2,1)S(1)} %all-to-all-done.fetched, bf16[256,128]{1,0:T(8,128)(2,1)S(1)} %copy-done.2, ...), custom_call_target="tpu_custom_call" | custom-call | tf_op jit(solution)/shard_map/forward/pallas_call | solution.py:394
  63.5 9.5 %all-to-all-start.1 = ((bf16[32,168,128]{2,1,0:T(8,128)(2,1)}), bf16[32,168,128]{2,1,0:T(8,128)(2,1)S(1)}, u32[]{:S(2)}, u32[]{:S(2)}) async-start(bf16[32,168,128]{2,1,0:T(8,128)(2,1)} %get-tuple-element.24), calls=%async_computation.2 | async-start | bytes 2752512 | tf_op jit(solution)/shard_map/all_to_all | solution.py:319
  73.0 0.0 reduce-scatter.2.cloned.1.call-start
  73.1 0.0 copy-start.1
  73.1 1.1 copy-done.1
  74.2 0.3 weight_halves.1
  74.5 1.9 %collective-permute-start = (bf16[1536,128]{1,0:T(8,128)(2,1)S(1)}, bf16[1536,128]{1,0:T(8,128)(2,1)S(1)}, u32[]{:S(2)}, u32[]{:S(2)}) collective-permute-start(bf16[1536,128]{1,0:T(8,128)(2,1)S(1)} %get-tuple-element.17), channel_id=1, source_target_pairs={{0,1},{1,0},{2,3},{3,2},{4,5},{5,4},{6,7},{7,6},{8,9},{9,8},{10,11... | collective-permute-start | bytes 1179656 | tf_op jit(solution)/shard_map/ppermute | solution.py:323
  76.4 2.4 %collective-permute-start.1 = (bf16[256,128]{1,0:T(8,128)(2,1)S(1)}, bf16[256,128]{1,0:T(8,128)(2,1)S(1)}, u32[]{:S(2)}, u32[]{:S(2)}) collective-permute-start(bf16[256,128]{1,0:T(8,128)(2,1)S(1)} %get-tuple-element.22.attention), channel_id=1, source_target_pairs={{0,1},{1,0},{2,3},{3,2},{4,5},{5,4},{6,7},{7,6},{8,9},{9,8},{10,11... | collective-permute-start | bytes 196616 | tf_op jit(solution)/shard_map/ppermute | solution.py:323
  78.8 0.0 collective-permute-done.got
  78.8 0.9 collective-permute-done.1.other
  79.7 0.6 mixed_share.1
  80.3 0.0 copy-start
  80.3 0.9 copy-done
  81.1 0.0 reduce-scatter.2.cloned.1.call-update
  81.2 26.5 %all-to-all-done.1.arrived = bf16[32,168,128]{2,1,0:T(8,128)(2,1)S(1)} async-done(((bf16[32,168,128]{2,1,0:T(8,128)(2,1)}), bf16[32,168,128]{2,1,0:T(8,128)(2,1)S(1)}, u32[]{:S(2)}, u32[]{:S(2)}) %all-to-all-start.1) | async-done | bytes 1376288 | tf_op jit(solution)/shard_map/all_to_all | solution.py:319
  107.7 1.1 sum_share.1
  108.8 0.0 copy-start.3
  108.8 0.0 copy-start.4
  108.8 6.6 %all-to-all-start.2 = ((bf16[32,96,128]{2,1,0:T(8,128)(2,1)}), bf16[32,96,128]{2,1,0:T(8,128)(2,1)}, u32[]{:S(2)}, u32[]{:S(2)}) async-start(bf16[32,96,128]{2,1,0:T(8,128)(2,1)} %sum_share.1), calls=%async_computation.3 | async-start | bytes 1572864 | tf_op jit(solution)/shard_map/all_to_all | solution.py:319
  115.4 2.3 %query_grad.1 = bf16[256,128]{1,0:T(8,128)(2,1)} custom-call(s32[5,32]{1,0:T(8,128)S(1)} %get-tuple-element.18.table, bf16[32,192,128]{2,1,0:T(8,128)(2,1)S(1)} %all-to-all-done.fetched, bf16[256,128]{1,0:T(8,128)(2,1)S(1)} %copy-done.2, bf16[256,128]{1,0:T(8,128)(2,1)S(1)} %get-tuple-element.21.grads, f32[128,128]{1,0:T(8,128)S(1)} %get-tuple-element.23.stats), custom_call_target="tpu_custom_call" | custom-call | flops 400000000 | bytes 4000000 | tf_op jit(solution)/shard_map/query_grad/pallas_call | solution.py:423
  117.6 0.0 copy-done.3
  117.6 0.0 copy-done.4
  117.6 5.7 %owner_grad.1 = (bf16[256,128]{1,0:T(8,128)(2,1)}, bf16[256,128]{1,0:T(8,128)(2,1)}) custom-call(s32[5,32]{1,0:T(8,128)S(1)} %get-tuple-element.18.table, bf16[32,192,128]{2,1,0:T(8,128)(2,1)S(1)} %all-to-all-done.fetched, bf16[32,168,128]{2,1,0:T(8,128)(2,1)S(1)} %all-to-all-done.1.arrived, bf16[256,128]{1,0:T(8,128)(2,1)S(1)} %copy-done.3, ...), custom_call_target="tpu_custom_call" | custom-call | flops 1100000000 | bytes 4000000 | tf_op jit(solution)/shard_map/owner_grad/pallas_call | solution.py:444
  123.4 13.7 %all-to-all-done.2.gathered = bf16[32,96,128]{2,1,0:T(8,128)(2,1)} async-done(((bf16[32,96,128]{2,1,0:T(8,128)(2,1)}), bf16[32,96,128]{2,1,0:T(8,128)(2,1)}, u32[]{:S(2)}, u32[]{:S(2)}) %all-to-all-start.2) | async-done | bytes 786464 | tf_op jit(solution)/shard_map/all_to_all | solution.py:319
  137.1 2.0 %assemble.1 = bf16[128,3072]{1,0:T(8,128)(2,1)} custom-call(bf16[32,96,128]{2,1,0:T(8,128)(2,1)} %all-to-all-done.2.gathered), custom_call_target="tpu_custom_call" | custom-call | tf_op jit(solution)/shard_map/assemble/pallas_call | solution.py:454
  139.1 0.0 reduce-scatter.2.cloned.1.call-done
Async XLA Ops:
  7.2 50.1 %all-gather.2.cloned.1.call-start = ((), (), s32[]{:S(2)}) async-start(), calls=%async_computation.4 | async-start | bytes 1671168 | tf_op jit(solution)/shard_map/all_gather | solution.py:337
  11.2 48.6 %all-to-all-start = ((bf16[32,192,128]{2,1,0:T(8,128)(2,1)}), bf16[32,192,128]{2,1,0:T(8,128)(2,1)S(1)}, u32[]{:S(2)}, u32[]{:S(2)}) async-start(bf16[32,192,128]{2,1,0:T(8,128)(2,1)} %get-tuple-element.19), calls=%async_computation | async-start | bytes 3145728 | tf_op jit(solution)/shard_map/all_to_all | solution.py:319
  21.5 38.4 %copy-start.2 = (bf16[256,128]{1,0:T(8,128)(2,1)S(1)}, bf16[256,128]{1,0:T(8,128)(2,1)}, u32[]{:S(2)}) copy-start(bf16[256,128]{1,0:T(8,128)(2,1)} %queries.5) | copy-start | bytes 196612
  63.5 44.2 %all-to-all-start.1 = ((bf16[32,168,128]{2,1,0:T(8,128)(2,1)}), bf16[32,168,128]{2,1,0:T(8,128)(2,1)S(1)}, u32[]{:S(2)}, u32[]{:S(2)}) async-start(bf16[32,168,128]{2,1,0:T(8,128)(2,1)} %get-tuple-element.24), calls=%async_computation.2 | async-start | bytes 2752512 | tf_op jit(solution)/shard_map/all_to_all | solution.py:319
  73.0 66.1 %reduce-scatter.2.cloned.1.call-start = ((), (), s32[]{:S(2)}) async-start(), calls=%async_computation.5 | async-start | bytes 884736 | tf_op jit(solution)/shard_map/reduce_scatter | solution.py:421
  73.1 1.1 copy-start.1
  74.5 4.3 %collective-permute-start = (bf16[1536,128]{1,0:T(8,128)(2,1)S(1)}, bf16[1536,128]{1,0:T(8,128)(2,1)S(1)}, u32[]{:S(2)}, u32[]{:S(2)}) collective-permute-start(bf16[1536,128]{1,0:T(8,128)(2,1)S(1)} %get-tuple-element.17), channel_id=1, source_target_pairs={{0,1},{1,0},{2,3},{3,2},{4,5},{5,4},{6,7},{7,6},{8,9},{9,8},{10,11... | collective-permute-start | bytes 1179656 | tf_op jit(solution)/shard_map/ppermute | solution.py:323
  76.4 3.3 %collective-permute-start.1 = (bf16[256,128]{1,0:T(8,128)(2,1)S(1)}, bf16[256,128]{1,0:T(8,128)(2,1)S(1)}, u32[]{:S(2)}, u32[]{:S(2)}) collective-permute-start(bf16[256,128]{1,0:T(8,128)(2,1)S(1)} %get-tuple-element.22.attention), channel_id=1, source_target_pairs={{0,1},{1,0},{2,3},{3,2},{4,5},{5,4},{6,7},{7,6},{8,9},{9,8},{10,11... | collective-permute-start | bytes 196616 | tf_op jit(solution)/shard_map/ppermute | solution.py:323
  80.3 0.9 copy-start
  108.8 8.9 %copy-start.3 = (bf16[256,128]{1,0:T(8,128)(2,1)S(1)}, bf16[256,128]{1,0:T(8,128)(2,1)}, u32[]{:S(2)}) copy-start(bf16[256,128]{1,0:T(8,128)(2,1)} %keys.3) | copy-start | bytes 196612
  108.8 8.9 %copy-start.4 = (bf16[256,128]{1,0:T(8,128)(2,1)S(1)}, bf16[256,128]{1,0:T(8,128)(2,1)}, u32[]{:S(2)}) copy-start(bf16[256,128]{1,0:T(8,128)(2,1)} %values.3) | copy-start | bytes 196612
  108.8 28.3 %all-to-all-start.2 = ((bf16[32,96,128]{2,1,0:T(8,128)(2,1)}), bf16[32,96,128]{2,1,0:T(8,128)(2,1)}, u32[]{:S(2)}, u32[]{:S(2)}) async-start(bf16[32,96,128]{2,1,0:T(8,128)(2,1)} %sum_share.1), calls=%async_computation.3 | async-start | bytes 1572864 | tf_op jit(solution)/shard_map/all_to_all | solution.py:319
Sparse Core Ops, SparseCore 0:
  10.1 47.1 all-gather.1
  81.3 42.4 reduce-scatter.1

commit v3 on v2

--- a/solution.py
+++ b/solution.py
@@ -14,12 +14,15 @@
 STAT_ROWS = 8
 ROW_BLOCKS = 4
 COL_BLOCKS = 8
+GATHERED = 16
+NEAR = 4
 BF16 = jnp.bfloat16
 F32 = jnp.float32
 VMEM = pl.BlockSpec(memory_space=pltpu.VMEM)
 SMEM = pl.BlockSpec(memory_space=pltpu.SMEM)
 HBM = pl.BlockSpec(memory_space=pltpu.HBM)
-PARAMS = pltpu.CompilerParams(vmem_limit_bytes=32 * 1024 * 1024)
+ANY = pl.BlockSpec(memory_space=pl.ANY)
+PARAMS = pltpu.CompilerParams(vmem_limit_bytes=16 * 1024 * 1024)
 NT = (((1,), (1,)), ((), ()))
 
 
@@ -108,41 +111,48 @@
         store.wait()
 
 
-def grad_kernel(weight_h, grad_h, grads, grad_t, weight, sems):
-    runs = sems.shape[0] - 1
-    span = grad_t.shape[0] // runs
-    loads = [pltpu.make_async_copy(weight_h, weight, sems.at[runs])]
-    for at in range(runs):
-        rows = pl.ds(at * span, span)
-        loads.append(pltpu.make_async_copy(grad_h.at[rows], grad_t.at[rows], sems.at[at]))
-    for load in loads:
-        load.start()
-    loads[0].wait()
-    total = jnp.zeros((WIDTH, grads.shape[0]), F32)
-    for at in range(runs):
-        loads[1 + at].wait()
-        rows = slice(at * span, (at + 1) * span)
-        total += dot(weight[:, rows], grad_t[rows, :])
-    grads[...] = total.T.astype(BF16)
-
-
-def halves_kernel(run, place, weight, kept, given):
+def mixed_kernel(core, weight_h, attention, keep, send, weight, sem):
+    load = pltpu.make_async_copy(weight_h, weight, sem)
+    load.start()
+    load.wait()
+    chips, run = keep.shape[0], keep.shape[1]
     weight_t = weight[...].T
-    mine = place[0] == 0
-    for z in range(kept.shape[0] // run):
-        first = weight_t[2 * z * run : (2 * z + 1) * run]
-        second = weight_t[(2 * z + 1) * run : (2 * z + 2) * run]
-        rows = slice(z * run, (z + 1) * run)
-        kept[rows, :] = jnp.where(mine, first, second)
-        given[rows, :] = jnp.where(mine, second, first)
-
-
-def mixed_kernel(kept, got, attention, other, out):
-    step = 256
-    for at in range(0, out.shape[0], step):
-        rows = slice(at, at + step)
-        total = dot_nt(kept[rows, :], attention[...]) + dot_nt(got[rows, :], other[...])
-        out[rows, :] = total.astype(BF16)
+    first_core = core[0] == 0
+    for z in range(chips):
+        shares = [
+            dot_nt(weight_t[(2 * z + k) * run : (2 * z + k + 1) * run], attention[...]).astype(BF16)
+            for k in range(2)
+        ]
+        keep[z] = jnp.where(first_core, shares[0], shares[1])
+        send[z] = jnp.where(first_core, shares[1], shares[0])
+
+
+def pair_kernel(place, mine, arrived, keep, *sends):
+    for z in range(mine.shape[0]):
+        total = mine[z].astype(F32) + arrived[z].astype(F32)
+        apart = jnp.bitwise_xor(place[0], z)
+        slot = lax.div(apart, NEAR)
+        for near, target in enumerate((keep,) + sends):
+
+            @pl.when(lax.rem(apart, NEAR) == near)
+            def _(target=target):
+                target[slot] = total.astype(target.dtype)
+
+
+def near_kernel(mine, *rest):
+    arrived, (keep, send) = rest[:-2], rest[-2:]
+    totals = []
+    for i in range(2):
+        total = mine[i]
+        for part in arrived:
+            total += part[i].astype(F32)
+        totals.append(total)
+    keep[...] = totals[0]
+    send[...] = totals[1].astype(BF16)
+
+
+def last_kernel(mine, arrived, grad_keys, out):
+    out[...] = (mine[...] + arrived[...].astype(F32)).astype(BF16)
 
 
 def listed(table, fetched, tile, list_length, part):
@@ -162,8 +172,8 @@
 
 
 def forward_kernel(
-    scale, list_length, table, fetched, queries, grad_t, grads, out, attention, stats,
-    spread, staged, sems,
+    scale, list_length, table, fetched, queries, place, grad_h, other_h, weight_h, out, attention, grads, stats,
+    grad_t, weight, spread, staged, sems,
 ):
     tiles = queries.shape[0] // TILE
     seq_count = out.shape[0]
@@ -171,6 +181,21 @@
     chunk = model // seq_count
     wide = model // COL_BLOCKS
     tall = WIDTH // ROW_BLOCKS
+    runs = COL_BLOCKS // 2
+    loads = []
+    run = model // GATHERED
+    core = place[0]
+    for at in range(GATHERED // 2):
+        span = pl.ds(at * run, run)
+        first = pl.ds(pl.multiple_of((2 * at + core) * run, run), run)
+        second = pl.ds(pl.multiple_of((2 * at + 1 - core) * run, run), run)
+        for source, target in ((grad_h.at[span], grad_t.at[first]), (other_h.at[span], grad_t.at[second])):
+            loads.append(pltpu.make_async_copy(source, target, sems.at[runs + len(loads)]))
+            loads[-1].start()
+    for at in range(runs):
+        span = pl.ds(at * 2 * wide, 2 * wide)
+        loads.append(pltpu.make_async_copy(weight_h.at[:, span], weight.at[:, span], sems.at[runs + len(loads)]))
+        loads[-1].start()
     lane = lax.broadcasted_iota(jnp.int32, (WIDTH, WIDTH), 1)
     table_of_stats = jnp.zeros((WIDTH, WIDTH), F32)
     for tile in range(tiles):
@@ -184,9 +209,19 @@
         weights = jnp.exp(scores - log_total).astype(BF16)
         attended = join_heads(dot(weights, value_rows)).astype(BF16)
         attention[rows, :] = attended
-        product = grads[rows, :].astype(F32) * attended.astype(F32)
+        table_of_stats = jnp.where(lane == tile, log_total, table_of_stats)
+    grads_t = jnp.zeros((WIDTH, queries.shape[0]), F32)
+    for at in range(runs):
+        for load in loads[at * GATHERED // runs : (at + 1) * GATHERED // runs]:
+            load.wait()
+        loads[GATHERED + at].wait()
+        span = slice(at * 2 * wide, (at + 1) * 2 * wide)
+        grads_t += dot(weight[:, span], grad_t[span, :])
+    grads[...] = grads_t.T.astype(BF16)
+    for tile in range(tiles):
+        rows = slice(tile * TILE, (tile + 1) * TILE)
+        product = grads[rows, :].astype(F32) * attention[rows, :].astype(F32)
         delta = jnp.sum(split_heads(product), axis=1, keepdims=True)
-        table_of_stats = jnp.where(lane == tile, log_total, table_of_stats)
         table_of_stats = jnp.where(lane == tiles + tile, delta, table_of_stats)
     stats[...] = table_of_stats
     by_row = table_of_stats.T
@@ -233,7 +268,7 @@
         out[rows, :] = (join_heads(dot(grad_scores, key_rows)) * scale).astype(BF16)
 
 
-def sum_kernel(chunk, arrived, out, total_of, sems):
+def sum_kernel(chunk, arrived, mixed_part, grad_queries, out, total_of, sems):
     total = arrived[0, 0:chunk, :].astype(F32)
     for i in range(1, arrived.shape[0]):
         total += arrived[i, 0:chunk, :].astype(F32)
@@ -292,20 +327,15 @@
     grad_values[...] = value_sum[...].astype(BF16)
 
 
-def assemble_kernel(gathered, out, held, staged, sems):
+def assemble_kernel(gathered, out, staged, sems):
     tall = out.shape[0] // ROW_BLOCKS
     wide = out.shape[1] // COL_BLOCKS
-    loads, stores = [], []
+    stores = []
     for at in range(COL_BLOCKS):
-        span = pl.ds(at * ROW_BLOCKS, ROW_BLOCKS)
-        loads.append(pltpu.make_async_copy(gathered.at[span], held.at[span], sems.at[COL_BLOCKS + at]))
-        loads[-1].start()
-    for at in range(COL_BLOCKS):
-        loads[at].wait()
         for down in range(ROW_BLOCKS):
             for k in range(wide // WIDTH):
                 column = at * wide + k * WIDTH
-                staged[down * tall : (down + 1) * tall, column : column + WIDTH] = held[
+                staged[down * tall : (down + 1) * tall, column : column + WIDTH] = gathered[
                     at * ROW_BLOCKS + down, k * tall : (k + 1) * tall, :
                 ]
         span = pl.ds(at * wide, wide)
@@ -321,6 +351,10 @@
 
 def swap_cores(array):
     return lax.ppermute(array, "core", [(0, 1), (1, 0)])
+
+
+def swap_chips(array, apart):
+    return lax.ppermute(array, "z", [(z, z ^ apart) for z in range(lax.axis_size("z"))])
 
 
 def body(queries, keys, values, out_weight, grad_mixed, kv_tiles, kv_counts):
@@ -334,7 +368,7 @@
     device = lax.axis_index("seq")
     block = jax.ShapeDtypeStruct((tok_rows, row_width), BF16)
 
-    grad_t = lax.all_gather(grad_mixed.T, ("z", "core"), axis=0, tiled=True)
+    grad_t = lax.all_gather(grad_mixed.T, "z", axis=0, tiled=True)
     lists = kv_tiles.T
     groups = 4
     outgoing, table = pl.pallas_call(
@@ -367,58 +401,64 @@
         stay(values),
     )
     fetched = exchange(outgoing)
-    half = jax.ShapeDtypeStruct((model // 2, row_width), BF16)
-    kept, given = pl.pallas_call(
-        functools.partial(halves_kernel, grad_mixed.shape[1]),
-        out_shape=(half, half),
-        in_specs=[SMEM, VMEM],
-        out_specs=(VMEM, VMEM),
-        compiler_params=PARAMS,
-        name="weight_halves",
-    )(lax.axis_index("core")[None].astype(jnp.int32), out_weight)
-    got = swap_cores(given)
-    grads, grad_t = pl.pallas_call(
-        grad_kernel,
-        out_shape=(block, jax.ShapeDtypeStruct((model, tok_rows), BF16)),
-        in_specs=[HBM, HBM],
-        out_specs=(VMEM, VMEM),
-        scratch_shapes=[
-            pltpu.VMEM(out_weight.shape, BF16),
-            pltpu.SemaphoreType.DMA((5,)),
-        ],
-        compiler_params=PARAMS,
-        cost_estimate=pl.CostEstimate(flops=30_000_000_000, bytes_accessed=100_000_000, transcendentals=0),
-        name="attention_grad",
-    )(stay(out_weight), stay(grad_t))
-
-    second, attention, stats = pl.pallas_call(
+    other_t = swap_cores(grad_t)
+    core = lax.axis_index("core")[None].astype(jnp.int32)
+
+    second, attention, grads, stats = pl.pallas_call(
         functools.partial(forward_kernel, scale, list_length),
         out_shape=(
             pltpu.HBM((seq_count, chunk + TILE + STAT_ROWS, row_width), BF16),
             block,
+            block,
             jax.ShapeDtypeStruct((WIDTH, WIDTH), F32),
         ),
-        in_specs=[SMEM, VMEM, VMEM, VMEM, VMEM],
-        out_specs=(HBM, VMEM, VMEM),
+        in_specs=[SMEM, VMEM, VMEM, SMEM, HBM, HBM, HBM],
+        out_specs=(HBM, VMEM, VMEM, VMEM),
         scratch_shapes=[
+            pltpu.VMEM((model, tok_rows), BF16),
+            pltpu.VMEM(out_weight.shape, BF16),
             pltpu.VMEM((tiles_dev, TILE + STAT_ROWS, row_width), BF16),
             pltpu.VMEM((seq_count, chunk + TILE + STAT_ROWS, row_width), BF16),
-            pltpu.SemaphoreType.DMA((COL_BLOCKS // 2,)),
+            pltpu.SemaphoreType.DMA((COL_BLOCKS + GATHERED,)),
         ],
         compiler_params=PARAMS,
         name="forward",
-    )(table, fetched, queries, grad_t, grads)
+    )(table, fetched, queries, core, stay(grad_t), stay(other_t), stay(out_weight))
     arrived = exchange(second)
 
-    mixed_t = pl.pallas_call(
+    run = grad_mixed.shape[1]
+    blocks = model // run // 2
+    shares = jax.ShapeDtypeStruct((blocks, run, tok_rows), BF16)
+    mine, sent = pl.pallas_call(
         mixed_kernel,
-        out_shape=jax.ShapeDtypeStruct((model // 2, tok_rows), BF16),
-        in_specs=[VMEM, VMEM, VMEM, VMEM],
-        out_specs=VMEM,
+        out_shape=(shares, shares),
+        in_specs=[SMEM, HBM, VMEM],
+        out_specs=(VMEM, VMEM),
+        scratch_shapes=[pltpu.VMEM(out_weight.shape, BF16), pltpu.SemaphoreType.DMA],
         compiler_params=PARAMS,
         name="mixed_share",
-    )(kept, got, attention, swap_cores(attention))
-    mixed = lax.psum_scatter(mixed_t, "z", scatter_dimension=0, tiled=True).T
+    )(core, stay(out_weight), attention)
+    far = blocks // NEAR
+    mine, *sent = pl.pallas_call(
+        pair_kernel,
+        out_shape=(jax.ShapeDtypeStruct((far, run, tok_rows), F32),)
+        + (jax.ShapeDtypeStruct((far, run, tok_rows), BF16),) * (NEAR - 1),
+        in_specs=[SMEM, VMEM, VMEM],
+        out_specs=(VMEM,) * NEAR,
+        compiler_params=PARAMS,
+        name="mixed_pair",
+    )(lax.axis_index("z")[None].astype(jnp.int32), mine, swap_cores(sent))
+    mine, sent = pl.pallas_call(
+        near_kernel,
+        out_shape=(
+            jax.ShapeDtypeStruct((run, tok_rows), F32),
+            jax.ShapeDtypeStruct((run, tok_rows), BF16),
+        ),
+        in_specs=[VMEM] * NEAR,
+        out_specs=(VMEM, VMEM),
+        compiler_params=PARAMS,
+        name="mixed_near",
+    )(mine, *(swap_chips(part, near + 1) for near, part in enumerate(sent)))
 
     grad_queries = pl.pallas_call(
         functools.partial(query_kernel, scale, list_length),
@@ -433,12 +473,12 @@
     third = pl.pallas_call(
         functools.partial(sum_kernel, chunk),
         out_shape=pltpu.HBM((seq_count, chunk, row_width), BF16),
-        in_specs=[VMEM],
+        in_specs=[VMEM, ANY, ANY],
         out_specs=HBM,
         scratch_shapes=[pltpu.VMEM((4, chunk, row_width), BF16), pltpu.SemaphoreType.DMA((seq_count // 4,))],
         compiler_params=PARAMS,
         name="sum_share",
-    )(arrived)
+    )(arrived, sent, grad_queries)
     gathered = exchange(third)
 
     grad_keys, grad_values = pl.pallas_call(
@@ -451,19 +491,26 @@
         cost_estimate=pl.CostEstimate(flops=1_100_000_000, bytes_accessed=4_000_000, transcendentals=1_000_000),
         name="owner_grad",
     )(table, fetched, arrived, keys, values)
+    mixed = pl.pallas_call(
+        last_kernel,
+        out_shape=jax.ShapeDtypeStruct((run, tok_rows), BF16),
+        in_specs=[VMEM, VMEM, ANY],
+        out_specs=VMEM,
+        compiler_params=PARAMS,
+        name="mixed_last",
+    )(mine, swap_chips(sent, 4), grad_keys).T
     weight_grad = pl.pallas_call(
         assemble_kernel,
         out_shape=pltpu.HBM(out_weight.shape, BF16),
-        in_specs=[HBM],
+        in_specs=[VMEM],
         out_specs=HBM,
         scratch_shapes=[
-            pltpu.VMEM((seq_count, chunk, row_width), BF16),
             pltpu.VMEM(out_weight.shape, BF16),
-            pltpu.SemaphoreType.DMA((2 * COL_BLOCKS,)),
+            pltpu.SemaphoreType.DMA((COL_BLOCKS,)),
         ],
         compiler_params=PARAMS,
         name="assemble",
-    )(stay(gathered))
+    )(gathered)
     return (mixed, grad_queries, grad_keys, grad_values, weight_grad)
 
 

time: 147 us -> 139 us (0.946)
  the two profiles are of different devices: /device:TPU:2 before, /device:TPU:66 now
where the time goes in v3:
time: 139 us; the launch traced here: 138 us
  starting transfers between devices  49.6 us (36%)
  blocking collectives  31.6 us (23%)
  waiting for transfers between devices  27 us (19%)
  Pallas kernels  25.2 us (18%)
  local copies, waits for them, and re-layouts  3.7 us (3%)
    all_gather x1, blocking collectives, body(): grad_t = lax.all_gather(grad_mixed.T, 'z', axis=0, tiled=True)  31.6 us
    all_to_all x3, starting transfers between devices, exchange(): lax.all_to_all(blocks, 'seq', split_axis=0, concat_axis=0, tiled=True)  27.6 us
    ppermute x4, starting transfers between devices, swap_chips(): lax.ppermute(array, 'z', [(z, z ^ apart) for z in range(lax.axis_size('z'...  18.2 us
    ppermute x4, waiting for transfers between devices, swap_chips(): lax.ppermute(array, 'z', [(z, z ^ apart) for z in range(lax.axis_size('z'...  13.3 us
    all_to_all x3, waiting for transfers between devices, exchange(): lax.all_to_all(blocks, 'seq', split_axis=0, concat_axis=0, tiled=True)  8.63 us
    pallas_call x1, Pallas kernels, body(): pl.pallas_call(functools.partial(forward_kernel, scale, list_length), out...  5.83 us
    pallas_call x1, Pallas kernels, body(): pl.pallas_call(functools.partial(owner_kernel, scale, chunk, 4), out_shap...  5.73 us
    ppermute x2, waiting for transfers between devices, swap_cores(): return lax.ppermute(array, 'core', [(0, 1), (1, 0)])  4.97 us
  transfers between devices with their start and end apart: 9, of which 6 were waited for; matrix products, arithmetic and copies ran while one was open for 0% of the time, Pallas kernels for 9%

profile of v3, /device:TPU:66, one launch (start us, length us, event | category | flops | bytes accessed | tf_op | source)
XLA Modules:
  0.0 137.9 jit_solution(348452738776841782)
XLA Ops:
  0.6 3.4 %pack.1 = (bf16[32,192,128]{2,1,0:T(8,128)(2,1)}, s32[5,32]{1,0:T(8,128)S(1)}) custom-call(s32[1]{0:T(128)} %bitcast.2.place, s32[8,128]{1,0:T(8,128)} %bitcast.9, s32[1,128]{1,0:T(1,128)} %bitcast.10, bf16[256,128]{1,0:T(8,128)(2,1)} %queries.5, bf16[256,128]{1,0:T(8,128)(2,1)} %keys.3, bf16[256,128]{1,0:T(8,128)(2,1)} %values.3), custom_call_target="tpu_custom_call" | custom-call | tf_op jit(solution)/shard_map/pack/pallas_call | solution.py:374
  4.0 0.0 copy-start.8
  4.0 0.0 copy-start.2
  4.0 10.4 %all-to-all-start = ((bf16[32,192,128]{2,1,0:T(8,128)(2,1)}), bf16[32,192,128]{2,1,0:T(8,128)(2,1)S(1)}, u32[]{:S(2)}, u32[]{:S(2)}) async-start(bf16[32,192,128]{2,1,0:T(8,128)(2,1)} %get-tuple-element.22), calls=%async_computation | async-start | bytes 3145728 | tf_op jit(solution)/shard_map/all_to_all | solution.py:349
  14.4 0.0 copy-done.8
  14.4 31.6 %all_gather.3.grad_h = bf16[1536,256]{1,0:T(8,128)(2,1)S(1)} all-gather(bf16[192,256]{1,0:T(8,128)(2,1)S(1)} %bitcast.7), channel_id=1, replica_groups=mesh['seq'=32,'z'=8,'core'=2] {'z'}, dimensions={0}, use_global_device_ids=true | all-gather | bytes 884736 | tf_op jit(solution)/shard_map/all_gather | solution.py:371
  46.1 0.0 copy-start.7
  46.1 1.9 %collective-permute-start = (bf16[1536,256]{1,0:T(8,128)(2,1)S(1)}, bf16[1536,256]{1,0:T(8,128)(2,1)}, u32[]{:S(2)}, u32[]{:S(2)}) collective-permute-start(bf16[1536,256]{1,0:T(8,128)(2,1)S(1)} %all_gather.3.grad_h), channel_id=1, source_target_pairs={{0,1},{1,0},{2,3},{3,2},{4,5},{5,4},{6,7},{7,6},{8,9},{9,8},{10,11... | collective-permute-start | bytes 2359304 | tf_op jit(solution)/shard_map/ppermute | solution.py:353
  48.0 2.4 %collective-permute-done.other_h = bf16[1536,256]{1,0:T(8,128)(2,1)} collective-permute-done((bf16[1536,256]{1,0:T(8,128)(2,1)S(1)}, bf16[1536,256]{1,0:T(8,128)(2,1)}, u32[]{:S(2)}, u32[]{:S(2)}) %collective-permute-start) | collective-permute-done | bytes 786464 | tf_op jit(solution)/shard_map/ppermute | solution.py:353
  50.4 2.4 %all-to-all-done.fetched = bf16[32,192,128]{2,1,0:T(8,128)(2,1)S(1)} async-done(((bf16[32,192,128]{2,1,0:T(8,128)(2,1)}), bf16[32,192,128]{2,1,0:T(8,128)(2,1)S(1)}, u32[]{:S(2)}, u32[]{:S(2)}) %all-to-all-start) | async-done | bytes 1572896 | tf_op jit(solution)/shard_map/all_to_all | solution.py:349
  52.8 0.0 copy-done.7
  52.8 0.0 copy-done.2
  52.8 5.8 %forward.1 = (bf16[32,168,128]{2,1,0:T(8,128)(2,1)}, bf16[256,128]{1,0:T(8,128)(2,1)S(1)}, bf16[256,128]{1,0:T(8,128)(2,1)S(1)}, f32[128,128]{1,0:T(8,128)S(1)}) custom-call(s32[5,32]{1,0:T(8,128)S(1)} %get-tuple-element.21.table, bf16[32,192,128]{2,1,0:T(8,128)(2,1)S(1)} %all-to-all-done.fetched, bf16[256,128]{1,0:T(8,128)(2,1)S(1)} %copy-done.2, ...), custom_call_target="tpu_custom_call" | custom-call | tf_op jit(solution)/shard_map/forward/pallas_call | solution.py:407
  58.6 7.4 %all-to-all-start.1 = ((bf16[32,168,128]{2,1,0:T(8,128)(2,1)}), bf16[32,168,128]{2,1,0:T(8,128)(2,1)S(1)}, u32[]{:S(2)}, u32[]{:S(2)}) async-start(bf16[32,168,128]{2,1,0:T(8,128)(2,1)} %get-tuple-element.32), calls=%async_computation.1 | async-start | bytes 2752512 | tf_op jit(solution)/shard_map/all_to_all | solution.py:349
  66.0 2.6 %mixed_share.1 = (bf16[8,192,256]{2,1,0:T(8,128)(2,1)S(1)}, bf16[8,192,256]{2,1,0:T(8,128)(2,1)}) custom-call(s32[1]{0:T(128)} %bitcast.1.place.core, bf16[128,3072]{1,0:T(8,128)(2,1)} %weight_h.3, bf16[256,128]{1,0:T(8,128)(2,1)S(1)} %get-tuple-element.23.attention), custom_call_target="tpu_custom_call" | custom-call | tf_op jit(solution)/shard_map/mixed_share/pallas_call | solution.py:432
  68.7 0.0 copy-start
  68.7 0.9 copy-done
  69.5 1.9 %collective-permute-start.1 = (bf16[8,192,256]{2,1,0:T(8,128)(2,1)}, bf16[8,192,256]{2,1,0:T(8,128)(2,1)}, u32[]{:S(2)}, u32[]{:S(2)}) collective-permute-start(bf16[8,192,256]{2,1,0:T(8,128)(2,1)} %get-tuple-element.25), channel_id=1, source_target_pairs={{0,1},{1,0},{2,3},{3,2},{4,5},{5,4},{6,7},{7,6},{8,9},{9,8},{10,11... | collective-permute-start | bytes 2359304 | tf_op jit(solution)/shard_map/ppermute | solution.py:353
  71.5 2.6 %collective-permute-done.1.arrived = bf16[8,192,256]{2,1,0:T(8,128)(2,1)} collective-permute-done((bf16[8,192,256]{2,1,0:T(8,128)(2,1)}, bf16[8,192,256]{2,1,0:T(8,128)(2,1)}, u32[]{:S(2)}, u32[]{:S(2)}) %collective-permute-start.1) | collective-permute-done | bytes 786464 | tf_op jit(solution)/shard_map/ppermute | solution.py:353
  74.0 0.0 copy-start.1
  74.0 1.1 copy-done.1
  75.2 1.5 %mixed_pair.1 = (f32[2,192,256]{2,1,0:T(8,128)S(1)}, bf16[2,192,256]{2,1,0:T(8,128)(2,1)S(1)}, bf16[2,192,256]{2,1,0:T(8,128)(2,1)S(1)}, bf16[2,192,256]{2,1,0:T(8,128)(2,1)S(1)}) custom-call(s32[1]{0:T(128)} %bitcast.place, bf16[8,192,256]{2,1,0:T(8,128)(2,1)S(1)} %copy-done.1, bf16[8,192,256]{2,1,0:T(8,128)(2,1)} %collective-permute-done.1.arrived), custom_call_target="tpu_custom_call" | custom-call | tf_op jit(solution)/shard_map/mixed_pair/pallas_call | solution.py:442
  76.7 2.4 %collective-permute-start.2 = (bf16[2,192,256]{2,1,0:T(8,128)(2,1)S(1)}, bf16[2,192,256]{2,1,0:T(8,128)(2,1)S(1)}, u32[]{:S(2)}, u32[]{:S(2)}) collective-permute-start(bf16[2,192,256]{2,1,0:T(8,128)(2,1)S(1)} %get-tuple-element.27), channel_id=1, source_target_pairs={{0,2},{2,0},{4,6},{6,4},{8,10},{10,8},{12,14},{14,12},{1,3},{3,1},... | collective-permute-start | bytes 589832 | tf_op jit(solution)/shard_map/ppermute | solution.py:357
  79.1 4.8 %collective-permute-start.3 = (bf16[2,192,256]{2,1,0:T(8,128)(2,1)S(1)}, bf16[2,192,256]{2,1,0:T(8,128)(2,1)S(1)}, u32[]{:S(2)}, u32[]{:S(2)}) collective-permute-start(bf16[2,192,256]{2,1,0:T(8,128)(2,1)S(1)} %get-tuple-element.28), channel_id=1, source_target_pairs={{0,4},{2,6},{4,0},{6,2},{8,12},{10,14},{12,8},{14,10},{1,5},{3,7},... | collective-permute-start | bytes 589832 | tf_op jit(solution)/shard_map/ppermute | solution.py:357
  83.9 2.5 %collective-permute-start.4 = (bf16[2,192,256]{2,1,0:T(8,128)(2,1)S(1)}, bf16[2,192,256]{2,1,0:T(8,128)(2,1)S(1)}, u32[]{:S(2)}, u32[]{:S(2)}) collective-permute-start(bf16[2,192,256]{2,1,0:T(8,128)(2,1)S(1)} %get-tuple-element.29), channel_id=1, source_target_pairs={{0,6},{2,4},{4,2},{6,0},{8,14},{10,12},{12,10},{14,8},{1,7},{3,5},... | collective-permute-start | bytes 589832 | tf_op jit(solution)/shard_map/ppermute | solution.py:357
  86.3 2.3 %query_grad.1.grad_queries = bf16[256,128]{1,0:T(8,128)(2,1)} custom-call(s32[5,32]{1,0:T(8,128)S(1)} %get-tuple-element.21.table, bf16[32,192,128]{2,1,0:T(8,128)(2,1)S(1)} %all-to-all-done.fetched, bf16[256,128]{1,0:T(8,128)(2,1)S(1)} %copy-done.2, bf16[256,128]{1,0:T(8,128)(2,1)S(1)} %get-tuple-element.34.grads, f32[128,128]{1,0:T(8,128)S(1)} %get-tuple-element.35.stats), custom_call_target="tpu_custom_call" | custom-call | flops 400000000 | bytes 4000000 | tf_op jit(solution)/shard_map/query_grad/pallas_call | solution.py:463
  88.6 0.0 collective-permute-done.2.rest_0_
  88.6 9.0 %collective-permute-done.3.rest_1_ = bf16[2,192,256]{2,1,0:T(8,128)(2,1)S(1)} collective-permute-done((bf16[2,192,256]{2,1,0:T(8,128)(2,1)S(1)}, bf16[2,192,256]{2,1,0:T(8,128)(2,1)S(1)}, u32[]{:S(2)}, u32[]{:S(2)}) %collective-permute-start.3) | collective-permute-done | bytes 196640 | tf_op jit(solution)/shard_map/ppermute | solution.py:357
  97.6 4.4 %collective-permute-done.4.rest_2_ = bf16[2,192,256]{2,1,0:T(8,128)(2,1)S(1)} collective-permute-done((bf16[2,192,256]{2,1,0:T(8,128)(2,1)S(1)}, bf16[2,192,256]{2,1,0:T(8,128)(2,1)S(1)}, u32[]{:S(2)}, u32[]{:S(2)}) %collective-permute-start.4) | collective-permute-done | bytes 196640 | tf_op jit(solution)/shard_map/ppermute | solution.py:357
  102.0 0.1 mixed_near.1
  102.0 0.0 all-to-all-done.1.arrived
  102.1 0.0 copy-start.3
  102.1 0.8 copy-done.3
  102.9 0.0 copy-start.4
  102.9 0.0 copy-start.5
  102.9 1.1 sum_share.1
  104.0 9.8 %all-to-all-start.2 = ((bf16[32,96,128]{2,1,0:T(8,128)(2,1)}), bf16[32,96,128]{2,1,0:T(8,128)(2,1)}, u32[]{:S(2)}, u32[]{:S(2)}) async-start(bf16[32,96,128]{2,1,0:T(8,128)(2,1)} %sum_share.1), calls=%async_computation.2 | async-start | bytes 1572864 | tf_op jit(solution)/shard_map/all_to_all | solution.py:349
  113.8 8.5 %collective-permute-start.5 = (bf16[192,256]{1,0:T(8,128)(2,1)S(1)}, bf16[192,256]{1,0:T(8,128)(2,1)S(1)}, u32[]{:S(2)}, u32[]{:S(2)}) collective-permute-start(bf16[192,256]{1,0:T(8,128)(2,1)S(1)} %get-tuple-element.31.mixed_part), channel_id=1, source_target_pairs={{0,8},{2,10},{4,12},{6,14},{8,0},{10,2},{12,4},{14,6},{1,9},{3,11}... | collective-permute-start | bytes 294920 | tf_op jit(solution)/shard_map/ppermute | solution.py:357
  122.3 0.0 copy-done.4
  122.3 0.0 copy-done.5
  122.4 5.7 %owner_grad.1 = (bf16[256,128]{1,0:T(8,128)(2,1)}, bf16[256,128]{1,0:T(8,128)(2,1)}) custom-call(s32[5,32]{1,0:T(8,128)S(1)} %get-tuple-element.21.table, bf16[32,192,128]{2,1,0:T(8,128)(2,1)S(1)} %all-to-all-done.fetched, bf16[32,168,128]{2,1,0:T(8,128)(2,1)S(1)} %all-to-all-done.1.arrived, bf16[256,128]{1,0:T(8,128)(2,1)S(1)} %copy-done.4, ...), custom_call_target="tpu_custom_call" | custom-call | flops 1100000000 | bytes 4000000 | tf_op jit(solution)/shard_map/owner_grad/pallas_call | solution.py:484
  128.1 0.0 collective-permute-done.5.arrived
  128.1 0.0 copy-start.6
  128.1 0.8 copy-done.6
  128.9 0.7 mixed_last.1
  129.6 6.2 %all-to-all-done.2.gathered = bf16[32,96,128]{2,1,0:T(8,128)(2,1)} async-done(((bf16[32,96,128]{2,1,0:T(8,128)(2,1)}), bf16[32,96,128]{2,1,0:T(8,128)(2,1)}, u32[]{:S(2)}, u32[]{:S(2)}) %all-to-all-start.2) | async-done | bytes 786464 | tf_op jit(solution)/shard_map/all_to_all | solution.py:349
  135.8 2.1 %assemble.1 = bf16[128,3072]{1,0:T(8,128)(2,1)} custom-call(bf16[32,96,128]{2,1,0:T(8,128)(2,1)} %all-to-all-done.2.gathered), custom_call_target="tpu_custom_call" | custom-call | tf_op jit(solution)/shard_map/assemble/pallas_call | solution.py:502
Async XLA Ops:
  4.0 10.4 %copy-start.8 = (bf16[256,192]{0,1:T(8,128)(2,1)S(1)}, bf16[256,192]{0,1:T(8,128)(2,1)}, u32[]{:S(2)}) copy-start(bf16[256,192]{0,1:T(8,128)(2,1)} %param.11) | copy-start | bytes 294916
  4.0 48.8 %copy-start.2 = (bf16[256,128]{1,0:T(8,128)(2,1)S(1)}, bf16[256,128]{1,0:T(8,128)(2,1)}, u32[]{:S(2)}) copy-start(bf16[256,128]{1,0:T(8,128)(2,1)} %queries.5) | copy-start | bytes 196612
  4.0 48.8 %all-to-all-start = ((bf16[32,192,128]{2,1,0:T(8,128)(2,1)}), bf16[32,192,128]{2,1,0:T(8,128)(2,1)S(1)}, u32[]{:S(2)}, u32[]{:S(2)}) async-start(bf16[32,192,128]{2,1,0:T(8,128)(2,1)} %get-tuple-element.22), calls=%async_computation | async-start | bytes 3145728 | tf_op jit(solution)/shard_map/all_to_all | solution.py:349
  46.1 6.7 %copy-start.7 = (bf16[1536,256]{1,0:T(8,128)(2,1)}, bf16[1536,256]{1,0:T(8,128)(2,1)S(1)}, u32[]{:S(2)}) copy-start(bf16[1536,256]{1,0:T(8,128)(2,1)S(1)} %all_gather.3.grad_h) | copy-start | bytes 2359300
  46.1 4.3 %collective-permute-start = (bf16[1536,256]{1,0:T(8,128)(2,1)S(1)}, bf16[1536,256]{1,0:T(8,128)(2,1)}, u32[]{:S(2)}, u32[]{:S(2)}) collective-permute-start(bf16[1536,256]{1,0:T(8,128)(2,1)S(1)} %all_gather.3.grad_h), channel_id=1, source_target_pairs={{0,1},{1,0},{2,3},{3,2},{4,5},{5,4},{6,7},{7,6},{8,9},{9,8},{10,11... | collective-permute-start | bytes 2359304 | tf_op jit(solution)/shard_map/ppermute | solution.py:353
  58.6 43.4 %all-to-all-start.1 = ((bf16[32,168,128]{2,1,0:T(8,128)(2,1)}), bf16[32,168,128]{2,1,0:T(8,128)(2,1)S(1)}, u32[]{:S(2)}, u32[]{:S(2)}) async-start(bf16[32,168,128]{2,1,0:T(8,128)(2,1)} %get-tuple-element.32), calls=%async_computation.1 | async-start | bytes 2752512 | tf_op jit(solution)/shard_map/all_to_all | solution.py:349
  68.7 0.9 copy-start
  69.5 4.5 %collective-permute-start.1 = (bf16[8,192,256]{2,1,0:T(8,128)(2,1)}, bf16[8,192,256]{2,1,0:T(8,128)(2,1)}, u32[]{:S(2)}, u32[]{:S(2)}) collective-permute-start(bf16[8,192,256]{2,1,0:T(8,128)(2,1)} %get-tuple-element.25), channel_id=1, source_target_pairs={{0,1},{1,0},{2,3},{3,2},{4,5},{5,4},{6,7},{7,6},{8,9},{9,8},{10,11... | collective-permute-start | bytes 2359304 | tf_op jit(solution)/shard_map/ppermute | solution.py:353
  74.0 1.1 copy-start.1
  76.7 11.9 %collective-permute-start.2 = (bf16[2,192,256]{2,1,0:T(8,128)(2,1)S(1)}, bf16[2,192,256]{2,1,0:T(8,128)(2,1)S(1)}, u32[]{:S(2)}, u32[]{:S(2)}) collective-permute-start(bf16[2,192,256]{2,1,0:T(8,128)(2,1)S(1)} %get-tuple-element.27), channel_id=1, source_target_pairs={{0,2},{2,0},{4,6},{6,4},{8,10},{10,8},{12,14},{14,12},{1,3},{3,1},... | collective-permute-start | bytes 589832 | tf_op jit(solution)/shard_map/ppermute | solution.py:357
  79.1 18.5 %collective-permute-start.3 = (bf16[2,192,256]{2,1,0:T(8,128)(2,1)S(1)}, bf16[2,192,256]{2,1,0:T(8,128)(2,1)S(1)}, u32[]{:S(2)}, u32[]{:S(2)}) collective-permute-start(bf16[2,192,256]{2,1,0:T(8,128)(2,1)S(1)} %get-tuple-element.28), channel_id=1, source_target_pairs={{0,4},{2,6},{4,0},{6,2},{8,12},{10,14},{12,8},{14,10},{1,5},{3,7},... | collective-permute-start | bytes 589832 | tf_op jit(solution)/shard_map/ppermute | solution.py:357
  83.9 18.1 %collective-permute-start.4 = (bf16[2,192,256]{2,1,0:T(8,128)(2,1)S(1)}, bf16[2,192,256]{2,1,0:T(8,128)(2,1)S(1)}, u32[]{:S(2)}, u32[]{:S(2)}) collective-permute-start(bf16[2,192,256]{2,1,0:T(8,128)(2,1)S(1)} %get-tuple-element.29), channel_id=1, source_target_pairs={{0,6},{2,4},{4,2},{6,0},{8,14},{10,12},{12,10},{14,8},{1,7},{3,5},... | collective-permute-start | bytes 589832 | tf_op jit(solution)/shard_map/ppermute | solution.py:357
  102.1 0.8 copy-start.3
  102.9 19.4 %copy-start.4 = (bf16[256,128]{1,0:T(8,128)(2,1)S(1)}, bf16[256,128]{1,0:T(8,128)(2,1)}, u32[]{:S(2)}) copy-start(bf16[256,128]{1,0:T(8,128)(2,1)} %keys.3) | copy-start | bytes 196612
  102.9 19.4 %copy-start.5 = (bf16[256,128]{1,0:T(8,128)(2,1)S(1)}, bf16[256,128]{1,0:T(8,128)(2,1)}, u32[]{:S(2)}) copy-start(bf16[256,128]{1,0:T(8,128)(2,1)} %values.3) | copy-start | bytes 196612
  104.0 31.8 %all-to-all-start.2 = ((bf16[32,96,128]{2,1,0:T(8,128)(2,1)}), bf16[32,96,128]{2,1,0:T(8,128)(2,1)}, u32[]{:S(2)}, u32[]{:S(2)}) async-start(bf16[32,96,128]{2,1,0:T(8,128)(2,1)} %sum_share.1), calls=%async_computation.2 | async-start | bytes 1572864 | tf_op jit(solution)/shard_map/all_to_all | solution.py:349
  113.8 14.3 %collective-permute-start.5 = (bf16[192,256]{1,0:T(8,128)(2,1)S(1)}, bf16[192,256]{1,0:T(8,128)(2,1)S(1)}, u32[]{:S(2)}, u32[]{:S(2)}) collective-permute-start(bf16[192,256]{1,0:T(8,128)(2,1)S(1)} %get-tuple-element.31.mixed_part), channel_id=1, source_target_pairs={{0,8},{2,10},{4,12},{6,14},{8,0},{10,2},{12,4},{14,6},{1,9},{3,11}... | collective-permute-start | bytes 294920 | tf_op jit(solution)/shard_map/ppermute | solution.py:357
  128.1 0.8 copy-start.6

commit v4 on v3

--- a/solution.py
+++ b/solution.py
@@ -12,10 +12,8 @@
 HD = 64
 WIDTH = 2 * HD
 STAT_ROWS = 8
-ROW_BLOCKS = 4
-COL_BLOCKS = 8
+FEW = 8
 GATHERED = 16
-NEAR = 4
 BF16 = jnp.bfloat16
 F32 = jnp.float32
 VMEM = pl.BlockSpec(memory_space=pltpu.VMEM)
@@ -87,10 +85,14 @@
             owner = lax.div(lists[j, device * tiles + tile], tiles)
             table[2, tile * list_length + j] = owner
             table[3, owner] = tile
+    groups = staged.shape[0]
+    loads[6].wait()
+    for i in range(seq_count):
+        mine = pl.ds(pl.multiple_of(table[3, i] * TILE, TILE), TILE)
+        staged[i * groups // seq_count, i % (seq_count // groups), 2 * TILE : 3 * TILE, :] = held[2, mine, :]
     scalars.wait()
-    for load in loads[4:]:
+    for load in loads[4:6]:
         load.wait()
-    groups = staged.shape[0]
     stores = []
     for group in range(groups):
         for k in range(seq_count // groups):
@@ -102,13 +104,29 @@
             tile = pl.ds(pl.multiple_of(asked * TILE, TILE), TILE)
             staged[group, k, 0:TILE, :] = held[0, tile, :]
             staged[group, k, TILE : 2 * TILE, :] = held[1, tile, :]
-            mine = pl.ds(pl.multiple_of(table[3, i] * TILE, TILE), TILE)
-            staged[group, k, 2 * TILE : 3 * TILE, :] = held[2, mine, :]
         span = pl.ds(group * (seq_count // groups), seq_count // groups)
         stores.append(pltpu.make_async_copy(staged.at[group], out.at[span], sems.at[8 + group]))
         stores[-1].start()
     for store in stores:
         store.wait()
+
+
+def joined(core, own, other, z):
+    run = 2 * own.shape[0] // GATHERED
+    mine, theirs = own[z * run : (z + 1) * run, :], other[z * run : (z + 1) * run, :]
+    first = core == 0
+    return jnp.concatenate([jnp.where(first, mine, theirs), jnp.where(first, theirs, mine)], axis=0)
+
+
+def grad_kernel(core, own, other, weight_h, grads, weight, sem):
+    load = pltpu.make_async_copy(weight_h, weight, sem)
+    load.start()
+    load.wait()
+    wide = 2 * weight.shape[1] // GATHERED
+    total = jnp.zeros((WIDTH, grads.shape[0]), F32)
+    for z in range(GATHERED // 2):
+        total += dot(weight[:, z * wide : (z + 1) * wide], joined(core[0], own, other, z))
+    grads[...] = total.T.astype(BF16)
 
 
 def mixed_kernel(core, weight_h, attention, keep, send, weight, sem):
@@ -127,28 +145,26 @@
         send[z] = jnp.where(first_core, shares[1], shares[0])
 
 
-def pair_kernel(place, mine, arrived, keep, *sends):
-    for z in range(mine.shape[0]):
+def pair_kernel(place, mine, arrived, keep, next_1, back_1, next_2, back_2):
+    chips = mine.shape[0]
+    homes = {
+        0: (keep, 0), 4: (keep, 1), 1: (next_1, 0), 5: (next_1, 1),
+        7: (back_1, 0), 3: (back_1, 1), 2: (next_2, 0), 6: (back_2, 0),
+    }
+    for z in range(chips):
         total = mine[z].astype(F32) + arrived[z].astype(F32)
-        apart = jnp.bitwise_xor(place[0], z)
-        slot = lax.div(apart, NEAR)
-        for near, target in enumerate((keep,) + sends):
-
-            @pl.when(lax.rem(apart, NEAR) == near)
-            def _(target=target):
+        apart = lax.rem(z + chips - place[0], chips)
+        for distance, (target, slot) in homes.items():
+
+            @pl.when(apart == distance)
+            def _(target=target, slot=slot):
                 target[slot] = total.astype(target.dtype)
 
 
-def near_kernel(mine, *rest):
-    arrived, (keep, send) = rest[:-2], rest[-2:]
-    totals = []
-    for i in range(2):
-        total = mine[i]
-        for part in arrived:
-            total += part[i].astype(F32)
-        totals.append(total)
-    keep[...] = totals[0]
-    send[...] = totals[1].astype(BF16)
+def near_kernel(mine, next_1, back_1, next_2, back_2, keep, send):
+    here, opposite = (mine[i] + next_1[i].astype(F32) + back_1[i].astype(F32) for i in range(2))
+    keep[...] = here + next_2[0].astype(F32) + back_2[0].astype(F32)
+    send[...] = opposite.astype(BF16)
 
 
 def last_kernel(mine, arrived, grad_keys, out):
@@ -172,30 +188,13 @@
 
 
 def forward_kernel(
-    scale, list_length, table, fetched, queries, place, grad_h, other_h, weight_h, out, attention, grads, stats,
-    grad_t, weight, spread, staged, sems,
+    scale, list_length, table, fetched, queries, core, own, other, grads, out, attention, stats,
+    spread, staged, sems,
 ):
     tiles = queries.shape[0] // TILE
     seq_count = out.shape[0]
-    model = grad_t.shape[0]
+    model = 2 * own.shape[0]
     chunk = model // seq_count
-    wide = model // COL_BLOCKS
-    tall = WIDTH // ROW_BLOCKS
-    runs = COL_BLOCKS // 2
-    loads = []
-    run = model // GATHERED
-    core = place[0]
-    for at in range(GATHERED // 2):
-        span = pl.ds(at * run, run)
-        first = pl.ds(pl.multiple_of((2 * at + core) * run, run), run)
-        second = pl.ds(pl.multiple_of((2 * at + 1 - core) * run, run), run)
-        for source, target in ((grad_h.at[span], grad_t.at[first]), (other_h.at[span], grad_t.at[second])):
-            loads.append(pltpu.make_async_copy(source, target, sems.at[runs + len(loads)]))
-            loads[-1].start()
-    for at in range(runs):
-        span = pl.ds(at * 2 * wide, 2 * wide)
-        loads.append(pltpu.make_async_copy(weight_h.at[:, span], weight.at[:, span], sems.at[runs + len(loads)]))
-        loads[-1].start()
     lane = lax.broadcasted_iota(jnp.int32, (WIDTH, WIDTH), 1)
     table_of_stats = jnp.zeros((WIDTH, WIDTH), F32)
     for tile in range(tiles):
@@ -209,19 +208,9 @@
         weights = jnp.exp(scores - log_total).astype(BF16)
         attended = join_heads(dot(weights, value_rows)).astype(BF16)
         attention[rows, :] = attended
+        product = grads[rows, :].astype(F32) * attended.astype(F32)
+        delta = jnp.sum(split_heads(product), axis=1, keepdims=True)
         table_of_stats = jnp.where(lane == tile, log_total, table_of_stats)
-    grads_t = jnp.zeros((WIDTH, queries.shape[0]), F32)
-    for at in range(runs):
-        for load in loads[at * GATHERED // runs : (at + 1) * GATHERED // runs]:
-            load.wait()
-        loads[GATHERED + at].wait()
-        span = slice(at * 2 * wide, (at + 1) * 2 * wide)
-        grads_t += dot(weight[:, span], grad_t[span, :])
-    grads[...] = grads_t.T.astype(BF16)
-    for tile in range(tiles):
-        rows = slice(tile * TILE, (tile + 1) * TILE)
-        product = grads[rows, :].astype(F32) * attention[rows, :].astype(F32)
-        delta = jnp.sum(split_heads(product), axis=1, keepdims=True)
         table_of_stats = jnp.where(lane == tiles + tile, delta, table_of_stats)
     stats[...] = table_of_stats
     by_row = table_of_stats.T
@@ -239,18 +228,25 @@
     for i in range(seq_count):
         staged[i, chunk : chunk + TILE + STAT_ROWS, :] = spread[table[3, i]]
     attention_t = attention[...].astype(F32).T.astype(BF16)
+    across = seq_count * FEW // WIDTH
+    steps = GATHERED // 4
     stores = []
-    for at in range(COL_BLOCKS):
-        part = dot_nt(attention_t, grad_t[at * wide : (at + 1) * wide, :]).astype(BF16)
-        for down in range(ROW_BLOCKS):
-            for k in range(wide // WIDTH):
-                staged[at * ROW_BLOCKS + down, k * tall : (k + 1) * tall, :] = part[
-                    down * tall : (down + 1) * tall, k * WIDTH : (k + 1) * WIDTH
-                ]
-        if at % 2 == 1:
-            span = pl.ds((at - 1) * ROW_BLOCKS, 2 * ROW_BLOCKS)
-            stores.append(pltpu.make_async_copy(staged.at[span], out.at[span], sems.at[at // 2]))
-            stores[-1].start()
+    for at in range(steps):
+        rows = jnp.concatenate([joined(core[0], own, other, 2 * at + k) for k in range(2)], axis=0)
+        part = dot_nt(attention_t, rows)
+        run = at * across // steps
+        first = (at - run * steps // across) * rows.shape[0] // WIDTH * FEW
+        for down in range(WIDTH // FEW):
+            lines = part[down * FEW : (down + 1) * FEW, :]
+            for k in range(0, rows.shape[0], 2 * WIDTH):
+                pair = jnp.concatenate([lines[:, k : k + WIDTH], lines[:, k + WIDTH : k + 2 * WIDTH]], axis=0)
+                start = first + k // WIDTH * FEW
+                staged[down * across + run, start : start + 2 * FEW, :] = pair.astype(BF16)
+        if (at + 1) * across % steps == 0:
+            for down in range(WIDTH // FEW):
+                c = down * across + run
+                stores.append(pltpu.make_async_copy(staged.at[c], out.at[c], sems.at[c]))
+                stores[-1].start()
     for store in stores:
         store.wait()
 
@@ -327,24 +323,6 @@
     grad_values[...] = value_sum[...].astype(BF16)
 
 
-def assemble_kernel(gathered, out, staged, sems):
-    tall = out.shape[0] // ROW_BLOCKS
-    wide = out.shape[1] // COL_BLOCKS
-    stores = []
-    for at in range(COL_BLOCKS):
-        for down in range(ROW_BLOCKS):
-            for k in range(wide // WIDTH):
-                column = at * wide + k * WIDTH
-                staged[down * tall : (down + 1) * tall, column : column + WIDTH] = gathered[
-                    at * ROW_BLOCKS + down, k * tall : (k + 1) * tall, :
-                ]
-        span = pl.ds(at * wide, wide)
-        stores.append(pltpu.make_async_copy(staged.at[:, span], out.at[:, span], sems.at[at]))
-        stores[-1].start()
-    for store in stores:
-        store.wait()
-
-
 def exchange(blocks):
     return lax.all_to_all(blocks, "seq", split_axis=0, concat_axis=0, tiled=True)
 
@@ -353,8 +331,9 @@
     return lax.ppermute(array, "core", [(0, 1), (1, 0)])
 
 
-def swap_chips(array, apart):
-    return lax.ppermute(array, "z", [(z, z ^ apart) for z in range(lax.axis_size("z"))])
+def to_chip(array, apart):
+    chips = lax.axis_size("z")
+    return lax.ppermute(array, "z", [(z, (z + apart) % chips) for z in range(chips)])
 
 
 def body(queries, keys, values, out_weight, grad_mixed, kv_tiles, kv_counts):
@@ -404,26 +383,34 @@
     other_t = swap_cores(grad_t)
     core = lax.axis_index("core")[None].astype(jnp.int32)
 
-    second, attention, grads, stats = pl.pallas_call(
+    grads = pl.pallas_call(
+        grad_kernel,
+        out_shape=block,
+        in_specs=[SMEM, VMEM, VMEM, HBM],
+        out_specs=VMEM,
+        scratch_shapes=[pltpu.VMEM(out_weight.shape, BF16), pltpu.SemaphoreType.DMA],
+        compiler_params=PARAMS,
+        cost_estimate=pl.CostEstimate(flops=3_000_000_000, bytes_accessed=3_000_000, transcendentals=0),
+        name="attention_grad",
+    )(core, grad_t, other_t, stay(out_weight))
+
+    second, attention, stats = pl.pallas_call(
         functools.partial(forward_kernel, scale, list_length),
         out_shape=(
             pltpu.HBM((seq_count, chunk + TILE + STAT_ROWS, row_width), BF16),
             block,
-            block,
             jax.ShapeDtypeStruct((WIDTH, WIDTH), F32),
         ),
-        in_specs=[SMEM, VMEM, VMEM, SMEM, HBM, HBM, HBM],
-        out_specs=(HBM, VMEM, VMEM, VMEM),
+        in_specs=[SMEM, VMEM, VMEM, SMEM, VMEM, VMEM, VMEM],
+        out_specs=(HBM, VMEM, VMEM),
         scratch_shapes=[
-            pltpu.VMEM((model, tok_rows), BF16),
-            pltpu.VMEM(out_weight.shape, BF16),
             pltpu.VMEM((tiles_dev, TILE + STAT_ROWS, row_width), BF16),
             pltpu.VMEM((seq_count, chunk + TILE + STAT_ROWS, row_width), BF16),
-            pltpu.SemaphoreType.DMA((COL_BLOCKS + GATHERED,)),
+            pltpu.SemaphoreType.DMA((seq_count,)),
         ],
         compiler_params=PARAMS,
         name="forward",
-    )(table, fetched, queries, core, stay(grad_t), stay(other_t), stay(out_weight))
+    )(table, fetched, queries, core, grad_t, other_t, grads)
     arrived = exchange(second)
 
     run = grad_mixed.shape[1]
@@ -438,13 +425,17 @@
         compiler_params=PARAMS,
         name="mixed_share",
     )(core, stay(out_weight), attention)
-    far = blocks // NEAR
     mine, *sent = pl.pallas_call(
         pair_kernel,
-        out_shape=(jax.ShapeDtypeStruct((far, run, tok_rows), F32),)
-        + (jax.ShapeDtypeStruct((far, run, tok_rows), BF16),) * (NEAR - 1),
+        out_shape=(
+            jax.ShapeDtypeStruct((2, run, tok_rows), F32),
+            jax.ShapeDtypeStruct((2, run, tok_rows), BF16),
+            jax.ShapeDtypeStruct((2, run, tok_rows), BF16),
+            jax.ShapeDtypeStruct((1, run, tok_rows), BF16),
+            jax.ShapeDtypeStruct((1, run, tok_rows), BF16),
+        ),
         in_specs=[SMEM, VMEM, VMEM],
-        out_specs=(VMEM,) * NEAR,
+        out_specs=(VMEM,) * 5,
         compiler_params=PARAMS,
         name="mixed_pair",
     )(lax.axis_index("z")[None].astype(jnp.int32), mine, swap_cores(sent))
@@ -454,11 +445,11 @@
             jax.ShapeDtypeStruct((run, tok_rows), F32),
             jax.ShapeDtypeStruct((run, tok_rows), BF16),
         ),
-        in_specs=[VMEM] * NEAR,
+        in_specs=[VMEM] * 5,
         out_specs=(VMEM, VMEM),
         compiler_params=PARAMS,
         name="mixed_near",
-    )(mine, *(swap_chips(part, near + 1) for near, part in enumerate(sent)))
+    )(mine, *(to_chip(part, apart) for part, apart in zip(sent, (1, -1, 2, -2), strict=True)))
 
     grad_queries = pl.pallas_call(
         functools.partial(query_kernel, scale, list_length),
@@ -473,12 +464,12 @@
     third = pl.pallas_call(
         functools.partial(sum_kernel, chunk),
         out_shape=pltpu.HBM((seq_count, chunk, row_width), BF16),
-        in_specs=[VMEM, ANY, ANY],
+        in_specs=[VMEM, ANY, HBM],
         out_specs=HBM,
         scratch_shapes=[pltpu.VMEM((4, chunk, row_width), BF16), pltpu.SemaphoreType.DMA((seq_count // 4,))],
         compiler_params=PARAMS,
         name="sum_share",
-    )(arrived, sent, grad_queries)
+    )(arrived, sent, stay(grad_queries))
     gathered = exchange(third)
 
     grad_keys, grad_values = pl.pallas_call(
@@ -494,23 +485,16 @@
     mixed = pl.pallas_call(
         last_kernel,
         out_shape=jax.ShapeDtypeStruct((run, tok_rows), BF16),
-        in_specs=[VMEM, VMEM, ANY],
+        in_specs=[VMEM, VMEM, HBM],
         out_specs=VMEM,
         compiler_params=PARAMS,
         name="mixed_last",
-    )(mine, swap_chips(sent, 4), grad_keys).T
-    weight_grad = pl.pallas_call(
-        assemble_kernel,
-        out_shape=pltpu.HBM(out_weight.shape, BF16),
-        in_specs=[VMEM],
-        out_specs=HBM,
-        scratch_shapes=[
-            pltpu.VMEM(out_weight.shape, BF16),
-            pltpu.SemaphoreType.DMA((COL_BLOCKS,)),
-        ],
-        compiler_params=PARAMS,
-        name="assemble",
-    )(gathered)
+    )(mine, to_chip(sent, 4), stay(grad_keys)).T
+    weight_grad = (
+        gathered.reshape(row_width // FEW, seq_count * FEW // row_width, chunk // FEW, FEW, WIDTH)
+        .transpose(0, 3, 1, 2, 4)
+        .reshape(out_weight.shape)
+    )
     return (mixed, grad_queries, grad_keys, grad_values, weight_grad)
 
 

time: 139 us -> 135 us (0.971)
  the two profiles are of different devices: /device:TPU:66 before, /device:TPU:2 now
where the time goes in v4:
time: 135 us; the launch traced here: 134 us
  starting transfers between devices  54.5 us (40%)
  blocking collectives  32.4 us (24%)
  Pallas kernels  23.1 us (17%)
  waiting for transfers between devices  19.3 us (14%)
  local copies, waits for them, and re-layouts  4.09 us (3%)
    all_gather x1, blocking collectives, body(): grad_t = lax.all_gather(grad_mixed.T, 'z', axis=0, tiled=True)  32.4 us
    all_to_all x3, starting transfers between devices, exchange(): lax.all_to_all(blocks, 'seq', split_axis=0, concat_axis=0, tiled=True)  27.7 us
    ppermute x5, starting transfers between devices, to_chip(): lax.ppermute(array, 'z', [(z, (z + apart) % chips) for z in range(chips)])  22.9 us
    all_to_all x3, waiting for transfers between devices, exchange(): lax.all_to_all(blocks, 'seq', split_axis=0, concat_axis=0, tiled=True)  12.9 us
    pallas_call x1, Pallas kernels, body(): pl.pallas_call(functools.partial(owner_kernel, scale, chunk, 4), out_shap...  5.73 us
    ppermute x2, waiting for transfers between devices, swap_cores(): return lax.ppermute(array, 'core', [(0, 1), (1, 0)])  4.84 us
    unnamed x13, local copies, waits for them, and re-layouts  4.09 us
    pallas_call x1, Pallas kernels, body(): pl.pallas_call(functools.partial(forward_kernel, scale, list_length), out...  4.01 us
  transfers between devices with their start and end apart: 10, of which 6 were waited for; matrix products, arithmetic and copies ran while one was open for 0% of the time, Pallas kernels for 11%

profile of v4, /device:TPU:2, one launch (start us, length us, event | category | flops | bytes accessed | tf_op | source)
XLA Modules:
  0.0 134.2 jit_solution(8615984015998393137)
XLA Ops:
  0.6 3.3 %pack.1 = (bf16[32,192,128]{2,1,0:T(8,128)(2,1)}, s32[5,32]{1,0:T(8,128)S(1)}) custom-call(s32[1]{0:T(128)} %bitcast.2.place, s32[8,128]{1,0:T(8,128)} %bitcast.14, s32[1,128]{1,0:T(1,128)} %bitcast.15, bf16[256,128]{1,0:T(8,128)(2,1)} %queries.5, bf16[256,128]{1,0:T(8,128)(2,1)} %keys.3, bf16[256,128]{1,0:T(8,128)(2,1)} %values.3), custom_call_target="tpu_custom_call" | custom-call | tf_op jit(solution)/shard_map/pack/pallas_call | solution.py:353
  4.0 0.0 copy-start.5
  4.0 10.4 %all-to-all-start = ((bf16[32,192,128]{2,1,0:T(8,128)(2,1)}), bf16[32,192,128]{2,1,0:T(8,128)(2,1)S(1)}, u32[]{:S(2)}, u32[]{:S(2)}) async-start(bf16[32,192,128]{2,1,0:T(8,128)(2,1)} %get-tuple-element.22), calls=%async_computation | async-start | bytes 3145728 | tf_op jit(solution)/shard_map/all_to_all | solution.py:327
  14.4 0.0 copy-done.5
  14.4 32.4 %all_gather.3.own = bf16[1536,256]{1,0:T(8,128)(2,1)S(1)} all-gather(bf16[192,256]{1,0:T(8,128)(2,1)S(1)} %bitcast.12), channel_id=1, replica_groups=mesh['seq'=32,'z'=8,'core'=2] {'z'}, dimensions={0}, use_global_device_ids=true | all-gather | bytes 884736 | tf_op jit(solution)/shard_map/all_gather | solution.py:350
  46.8 1.9 %collective-permute-start = (bf16[1536,256]{1,0:T(8,128)(2,1)S(1)}, bf16[1536,256]{1,0:T(8,128)(2,1)S(1)}, u32[]{:S(2)}, u32[]{:S(2)}) collective-permute-start(bf16[1536,256]{1,0:T(8,128)(2,1)S(1)} %all_gather.3.own), channel_id=1, source_target_pairs={{0,1},{1,0},{2,3},{3,2},{4,5},{5,4},{6,7},{7,6},{8,9},{9,8},{10,11... | collective-permute-start | bytes 2359304 | tf_op jit(solution)/shard_map/ppermute | solution.py:331
  48.7 2.2 %collective-permute-done.other = bf16[1536,256]{1,0:T(8,128)(2,1)S(1)} collective-permute-done((bf16[1536,256]{1,0:T(8,128)(2,1)S(1)}, bf16[1536,256]{1,0:T(8,128)(2,1)S(1)}, u32[]{:S(2)}, u32[]{:S(2)}) %collective-permute-start) | collective-permute-done | bytes 786464 | tf_op jit(solution)/shard_map/ppermute | solution.py:331
  51.0 0.0 copy-start.2
  51.0 1.7 %attention_grad.1.grads = bf16[256,128]{1,0:T(8,128)(2,1)S(1)} custom-call(s32[1]{0:T(128)} %bitcast.1.core, bf16[1536,256]{1,0:T(8,128)(2,1)S(1)} %all_gather.3.own, bf16[1536,256]{1,0:T(8,128)(2,1)S(1)} %collective-permute-done.other, bf16[128,3072]{1,0:T(8,128)(2,1)} %weight_h.3), custom_call_target="tpu_custom_call" | custom-call | flops 3000000000 | bytes 3000000 | tf_op jit(solution)/shard_map/attention_grad/pallas_call | solution.py:386
  52.7 0.0 all-to-all-done.fetched
  52.7 0.0 copy-done.2
  52.7 4.0 %forward.1 = (bf16[32,168,128]{2,1,0:T(8,128)(2,1)}, bf16[256,128]{1,0:T(8,128)(2,1)S(1)}, f32[128,128]{1,0:T(8,128)S(1)}) custom-call(s32[5,32]{1,0:T(8,128)S(1)} %get-tuple-element.21.table, bf16[32,192,128]{2,1,0:T(8,128)(2,1)S(1)} %all-to-all-done.fetched, bf16[256,128]{1,0:T(8,128)(2,1)S(1)} %copy-done.2, s32[1]{0:T(128)} %bitcast.1.core, ...), custom_call_target="tpu_custom_call" | custom-call | tf_op jit(solution)/shard_map/forward/pallas_call | solution.py:397
  56.8 9.8 %all-to-all-start.1 = ((bf16[32,168,128]{2,1,0:T(8,128)(2,1)}), bf16[32,168,128]{2,1,0:T(8,128)(2,1)S(1)}, u32[]{:S(2)}, u32[]{:S(2)}) async-start(bf16[32,168,128]{2,1,0:T(8,128)(2,1)} %get-tuple-element.33), calls=%async_computation.1 | async-start | bytes 2752512 | tf_op jit(solution)/shard_map/all_to_all | solution.py:327
  66.5 2.6 %mixed_share.1 = (bf16[8,192,256]{2,1,0:T(8,128)(2,1)S(1)}, bf16[8,192,256]{2,1,0:T(8,128)(2,1)}) custom-call(s32[1]{0:T(128)} %bitcast.1.core, bf16[128,3072]{1,0:T(8,128)(2,1)} %weight_h.3, bf16[256,128]{1,0:T(8,128)(2,1)S(1)} %get-tuple-element.23.attention), custom_call_target="tpu_custom_call" | custom-call | tf_op jit(solution)/shard_map/mixed_share/pallas_call | solution.py:419
  69.2 0.0 copy-start
  69.2 0.9 copy-done
  70.1 1.9 %collective-permute-start.1 = (bf16[8,192,256]{2,1,0:T(8,128)(2,1)}, bf16[8,192,256]{2,1,0:T(8,128)(2,1)}, u32[]{:S(2)}, u32[]{:S(2)}) collective-permute-start(bf16[8,192,256]{2,1,0:T(8,128)(2,1)} %get-tuple-element.25), channel_id=1, source_target_pairs={{0,1},{1,0},{2,3},{3,2},{4,5},{5,4},{6,7},{7,6},{8,9},{9,8},{10,11... | collective-permute-start | bytes 2359304 | tf_op jit(solution)/shard_map/ppermute | solution.py:331
  72.0 2.6 %collective-permute-done.1.arrived = bf16[8,192,256]{2,1,0:T(8,128)(2,1)} collective-permute-done((bf16[8,192,256]{2,1,0:T(8,128)(2,1)}, bf16[8,192,256]{2,1,0:T(8,128)(2,1)}, u32[]{:S(2)}, u32[]{:S(2)}) %collective-permute-start.1) | collective-permute-done | bytes 786464 | tf_op jit(solution)/shard_map/ppermute | solution.py:331
  74.6 0.0 copy-start.1
  74.6 1.1 copy-done.1
  75.7 1.6 %mixed_pair.1 = (f32[2,192,256]{2,1,0:T(8,128)S(1)}, bf16[2,192,256]{2,1,0:T(8,128)(2,1)S(1)}, bf16[2,192,256]{2,1,0:T(8,128)(2,1)S(1)}, bf16[1,192,256]{2,1,0:T(8,128)(2,1)S(1)}, bf16[1,192,256]{2,1,0:T(8,128)(2,1)S(1)}) custom-call(s32[1]{0:T(128)} %bitcast.place, bf16[8,192,256]{2,1,0:T(8,128)(2,1)S(1)} %copy-done.1, ...), custom_call_target="tpu_custom_call" | custom-call | tf_op jit(solution)/shard_map/mixed_pair/pallas_call | solution.py:428
  77.4 3.5 %collective-permute-start.2 = (bf16[2,192,256]{2,1,0:T(8,128)(2,1)S(1)}, bf16[2,192,256]{2,1,0:T(8,128)(2,1)S(1)}, u32[]{:S(2)}, u32[]{:S(2)}) collective-permute-start(bf16[2,192,256]{2,1,0:T(8,128)(2,1)S(1)} %get-tuple-element.27), channel_id=1, source_target_pairs={{0,2},{2,4},{4,6},{6,8},{8,10},{10,12},{12,14},{14,0},{1,3},{3,5},... | collective-permute-start | bytes 589832 | tf_op jit(solution)/shard_map/ppermute | solution.py:336
  80.8 6.1 %collective-permute-start.3 = (bf16[2,192,256]{2,1,0:T(8,128)(2,1)S(1)}, bf16[2,192,256]{2,1,0:T(8,128)(2,1)S(1)}, u32[]{:S(2)}, u32[]{:S(2)}) collective-permute-start(bf16[2,192,256]{2,1,0:T(8,128)(2,1)S(1)} %get-tuple-element.28), channel_id=1, source_target_pairs={{0,14},{2,0},{4,2},{6,4},{8,6},{10,8},{12,10},{14,12},{1,15},{3,1}... | collective-permute-start | bytes 589832 | tf_op jit(solution)/shard_map/ppermute | solution.py:336
  87.0 1.9 %collective-permute-start.4 = (bf16[1,192,256]{2,1,0:T(8,128)(2,1)S(1)}, bf16[1,192,256]{2,1,0:T(8,128)(2,1)S(1)}, u32[]{:S(2)}, u32[]{:S(2)}) collective-permute-start(bf16[1,192,256]{2,1,0:T(8,128)(2,1)S(1)} %get-tuple-element.29), channel_id=1, source_target_pairs={{0,4},{2,6},{4,8},{6,10},{8,12},{10,14},{12,0},{14,2},{1,5},{3,7},... | collective-permute-start | bytes 294920 | tf_op jit(solution)/shard_map/ppermute | solution.py:336
  88.9 6.0 %collective-permute-start.5 = (bf16[1,192,256]{2,1,0:T(8,128)(2,1)S(1)}, bf16[1,192,256]{2,1,0:T(8,128)(2,1)S(1)}, u32[]{:S(2)}, u32[]{:S(2)}) collective-permute-start(bf16[1,192,256]{2,1,0:T(8,128)(2,1)S(1)} %get-tuple-element.30), channel_id=1, source_target_pairs={{0,12},{2,14},{4,0},{6,2},{8,4},{10,6},{12,8},{14,10},{1,13},{3,15... | collective-permute-start | bytes 294920 | tf_op jit(solution)/shard_map/ppermute | solution.py:336
  94.9 2.3 %query_grad.1.grad_queries = bf16[256,128]{1,0:T(8,128)(2,1)} custom-call(s32[5,32]{1,0:T(8,128)S(1)} %get-tuple-element.21.table, bf16[32,192,128]{2,1,0:T(8,128)(2,1)S(1)} %all-to-all-done.fetched, bf16[256,128]{1,0:T(8,128)(2,1)S(1)} %copy-done.2, bf16[256,128]{1,0:T(8,128)(2,1)S(1)} %attention_grad.1.grads, f32[128,128]{1,0:T(8,128)S(1)} %get-tuple-element.35.stats), custom_call_target="tpu_custom_call" | custom-call | flops 400000000 | bytes 4000000 | tf_op jit(solution)/shard_map/query_grad/pallas_call | solution.py:454
  97.2 0.4 collective-permute-done.4.next_2
  97.6 1.0 collective-permute-done.5.back_2
  98.7 0.0 collective-permute-done.2.next_1
  98.7 0.0 collective-permute-done.3.back_1
  98.7 0.1 mixed_near.1
  98.8 2.3 %all-to-all-done.1.arrived = bf16[32,168,128]{2,1,0:T(8,128)(2,1)S(1)} async-done(((bf16[32,168,128]{2,1,0:T(8,128)(2,1)}), bf16[32,168,128]{2,1,0:T(8,128)(2,1)S(1)}, u32[]{:S(2)}, u32[]{:S(2)}) %all-to-all-start.1) | async-done | bytes 1376288 | tf_op jit(solution)/shard_map/all_to_all | solution.py:327
  101.1 0.0 copy-start.3
  101.1 0.0 copy-start.4
  101.1 1.1 sum_share.1
  102.2 7.5 %all-to-all-start.2 = ((bf16[32,96,128]{2,1,0:T(8,128)(2,1)}), bf16[32,96,128]{2,1,0:T(8,128)(2,1)}, u32[]{:S(2)}, u32[]{:S(2)}) async-start(bf16[32,96,128]{2,1,0:T(8,128)(2,1)} %sum_share.1), calls=%async_computation.2 | async-start | bytes 1572864 | tf_op jit(solution)/shard_map/all_to_all | solution.py:327
  109.7 5.4 %collective-permute-start.6 = (bf16[192,256]{1,0:T(8,128)(2,1)S(1)}, bf16[192,256]{1,0:T(8,128)(2,1)S(1)}, u32[]{:S(2)}, u32[]{:S(2)}) collective-permute-start(bf16[192,256]{1,0:T(8,128)(2,1)S(1)} %get-tuple-element.32.mixed_part), channel_id=1, source_target_pairs={{0,8},{2,10},{4,12},{6,14},{8,0},{10,2},{12,4},{14,6},{1,9},{3,11}... | collective-permute-start | bytes 294920 | tf_op jit(solution)/shard_map/ppermute | solution.py:336
  115.1 0.0 copy-done.3
  115.1 0.0 copy-done.4
  115.1 5.7 %owner_grad.1 = (bf16[256,128]{1,0:T(8,128)(2,1)}, bf16[256,128]{1,0:T(8,128)(2,1)}) custom-call(s32[5,32]{1,0:T(8,128)S(1)} %get-tuple-element.21.table, bf16[32,192,128]{2,1,0:T(8,128)(2,1)S(1)} %all-to-all-done.fetched, bf16[32,168,128]{2,1,0:T(8,128)(2,1)S(1)} %all-to-all-done.1.arrived, bf16[256,128]{1,0:T(8,128)(2,1)S(1)} %copy-done.3, ...), custom_call_target="tpu_custom_call" | custom-call | flops 1100000000 | bytes 4000000 | tf_op jit(solution)/shard_map/owner_grad/pallas_call | solution.py:475
  120.9 0.0 collective-permute-done.6.arrived
  120.9 0.7 mixed_last.1
  121.5 10.6 %all-to-all-done.2 = bf16[32,96,128]{2,1,0:T(8,128)(2,1)} async-done(((bf16[32,96,128]{2,1,0:T(8,128)(2,1)}), bf16[32,96,128]{2,1,0:T(8,128)(2,1)}, u32[]{:S(2)}, u32[]{:S(2)}) %all-to-all-start.2) | async-done | bytes 786464 | tf_op jit(solution)/shard_map/all_to_all | solution.py:327
  132.1 2.1 %copy.13 = bf16[128,3072]{1,0:T(8,128)(2,1)} copy(bf16[128,3072]{1,0:T(8,128)(2,1)} %bitcast.9) | data formatting | bytes 1572864
Async XLA Ops:
  4.0 10.4 %copy-start.5 = (bf16[256,192]{0,1:T(8,128)(2,1)S(1)}, bf16[256,192]{0,1:T(8,128)(2,1)}, u32[]{:S(2)}) copy-start(bf16[256,192]{0,1:T(8,128)(2,1)} %param.11) | copy-start | bytes 294916
  4.0 48.8 %all-to-all-start = ((bf16[32,192,128]{2,1,0:T(8,128)(2,1)}), bf16[32,192,128]{2,1,0:T(8,128)(2,1)S(1)}, u32[]{:S(2)}, u32[]{:S(2)}) async-start(bf16[32,192,128]{2,1,0:T(8,128)(2,1)} %get-tuple-element.22), calls=%async_computation | async-start | bytes 3145728 | tf_op jit(solution)/shard_map/all_to_all | solution.py:327
  46.8 4.2 %collective-permute-start = (bf16[1536,256]{1,0:T(8,128)(2,1)S(1)}, bf16[1536,256]{1,0:T(8,128)(2,1)S(1)}, u32[]{:S(2)}, u32[]{:S(2)}) collective-permute-start(bf16[1536,256]{1,0:T(8,128)(2,1)S(1)} %all_gather.3.own), channel_id=1, source_target_pairs={{0,1},{1,0},{2,3},{3,2},{4,5},{5,4},{6,7},{7,6},{8,9},{9,8},{10,11... | collective-permute-start | bytes 2359304 | tf_op jit(solution)/shard_map/ppermute | solution.py:331
  51.0 1.8 %copy-start.2 = (bf16[256,128]{1,0:T(8,128)(2,1)S(1)}, bf16[256,128]{1,0:T(8,128)(2,1)}, u32[]{:S(2)}) copy-start(bf16[256,128]{1,0:T(8,128)(2,1)} %queries.5) | copy-start | bytes 196612
  56.8 44.4 %all-to-all-start.1 = ((bf16[32,168,128]{2,1,0:T(8,128)(2,1)}), bf16[32,168,128]{2,1,0:T(8,128)(2,1)S(1)}, u32[]{:S(2)}, u32[]{:S(2)}) async-start(bf16[32,168,128]{2,1,0:T(8,128)(2,1)} %get-tuple-element.33), calls=%async_computation.1 | async-start | bytes 2752512 | tf_op jit(solution)/shard_map/all_to_all | solution.py:327
  69.2 0.9 copy-start
  70.1 4.5 %collective-permute-start.1 = (bf16[8,192,256]{2,1,0:T(8,128)(2,1)}, bf16[8,192,256]{2,1,0:T(8,128)(2,1)}, u32[]{:S(2)}, u32[]{:S(2)}) collective-permute-start(bf16[8,192,256]{2,1,0:T(8,128)(2,1)} %get-tuple-element.25), channel_id=1, source_target_pairs={{0,1},{1,0},{2,3},{3,2},{4,5},{5,4},{6,7},{7,6},{8,9},{9,8},{10,11... | collective-permute-start | bytes 2359304 | tf_op jit(solution)/shard_map/ppermute | solution.py:331
  74.6 1.1 copy-start.1
  77.4 21.3 %collective-permute-start.2 = (bf16[2,192,256]{2,1,0:T(8,128)(2,1)S(1)}, bf16[2,192,256]{2,1,0:T(8,128)(2,1)S(1)}, u32[]{:S(2)}, u32[]{:S(2)}) collective-permute-start(bf16[2,192,256]{2,1,0:T(8,128)(2,1)S(1)} %get-tuple-element.27), channel_id=1, source_target_pairs={{0,2},{2,4},{4,6},{6,8},{8,10},{10,12},{12,14},{14,0},{1,3},{3,5},... | collective-permute-start | bytes 589832 | tf_op jit(solution)/shard_map/ppermute | solution.py:336
  80.8 17.9 %collective-permute-start.3 = (bf16[2,192,256]{2,1,0:T(8,128)(2,1)S(1)}, bf16[2,192,256]{2,1,0:T(8,128)(2,1)S(1)}, u32[]{:S(2)}, u32[]{:S(2)}) collective-permute-start(bf16[2,192,256]{2,1,0:T(8,128)(2,1)S(1)} %get-tuple-element.28), channel_id=1, source_target_pairs={{0,14},{2,0},{4,2},{6,4},{8,6},{10,8},{12,10},{14,12},{1,15},{3,1}... | collective-permute-start | bytes 589832 | tf_op jit(solution)/shard_map/ppermute | solution.py:336
  87.0 10.7 %collective-permute-start.4 = (bf16[1,192,256]{2,1,0:T(8,128)(2,1)S(1)}, bf16[1,192,256]{2,1,0:T(8,128)(2,1)S(1)}, u32[]{:S(2)}, u32[]{:S(2)}) collective-permute-start(bf16[1,192,256]{2,1,0:T(8,128)(2,1)S(1)} %get-tuple-element.29), channel_id=1, source_target_pairs={{0,4},{2,6},{4,8},{6,10},{8,12},{10,14},{12,0},{14,2},{1,5},{3,7},... | collective-permute-start | bytes 294920 | tf_op jit(solution)/shard_map/ppermute | solution.py:336
  88.9 9.8 %collective-permute-start.5 = (bf16[1,192,256]{2,1,0:T(8,128)(2,1)S(1)}, bf16[1,192,256]{2,1,0:T(8,128)(2,1)S(1)}, u32[]{:S(2)}, u32[]{:S(2)}) collective-permute-start(bf16[1,192,256]{2,1,0:T(8,128)(2,1)S(1)} %get-tuple-element.30), channel_id=1, source_target_pairs={{0,12},{2,14},{4,0},{6,2},{8,4},{10,6},{12,8},{14,10},{1,13},{3,15... | collective-permute-start | bytes 294920 | tf_op jit(solution)/shard_map/ppermute | solution.py:336
  101.1 14.0 %copy-start.3 = (bf16[256,128]{1,0:T(8,128)(2,1)S(1)}, bf16[256,128]{1,0:T(8,128)(2,1)}, u32[]{:S(2)}) copy-start(bf16[256,128]{1,0:T(8,128)(2,1)} %keys.3) | copy-start | bytes 196612
  101.1 14.0 %copy-start.4 = (bf16[256,128]{1,0:T(8,128)(2,1)S(1)}, bf16[256,128]{1,0:T(8,128)(2,1)}, u32[]{:S(2)}) copy-start(bf16[256,128]{1,0:T(8,128)(2,1)} %values.3) | copy-start | bytes 196612
  102.2 29.9 %all-to-all-start.2 = ((bf16[32,96,128]{2,1,0:T(8,128)(2,1)}), bf16[32,96,128]{2,1,0:T(8,128)(2,1)}, u32[]{:S(2)}, u32[]{:S(2)}) async-start(bf16[32,96,128]{2,1,0:T(8,128)(2,1)} %sum_share.1), calls=%async_computation.2 | async-start | bytes 1572864 | tf_op jit(solution)/shard_map/all_to_all | solution.py:327
  109.7 11.1 %collective-permute-start.6 = (bf16[192,256]{1,0:T(8,128)(2,1)S(1)}, bf16[192,256]{1,0:T(8,128)(2,1)S(1)}, u32[]{:S(2)}, u32[]{:S(2)}) collective-permute-start(bf16[192,256]{1,0:T(8,128)(2,1)S(1)} %get-tuple-element.32.mixed_part), channel_id=1, source_target_pairs={{0,8},{2,10},{4,12},{6,14},{8,0},{10,2},{12,4},{14,6},{1,9},{3,11}... | collective-permute-start | bytes 294920 | tf_op jit(solution)/shard_map/ppermute | solution.py:336

commit v5 on v4

--- a/solution.py
+++ b/solution.py
@@ -52,7 +52,7 @@
 
 def pack_kernel(
     place, lists_h, counts_h, queries, keys, values, out, table,
-    lists, counts, lists_v, counts_v, staged, codes_v, codes, held, sems,
+    lists, counts, lists_v, counts_v, staged, asking, codes_v, codes, held, sems,
 ):
     list_length, tile_count = lists_v.shape
     seq_count = out.shape[0]
@@ -85,27 +85,30 @@
             owner = lax.div(lists[j, device * tiles + tile], tiles)
             table[2, tile * list_length + j] = owner
             table[3, owner] = tile
-    groups = staged.shape[0]
+    groups = sems.shape[0] - 9
+    each = seq_count // groups
     loads[6].wait()
     for i in range(seq_count):
         mine = pl.ds(pl.multiple_of(table[3, i] * TILE, TILE), TILE)
-        staged[i * groups // seq_count, i % (seq_count // groups), 2 * TILE : 3 * TILE, :] = held[2, mine, :]
+        asking[i] = held[2, mine, :]
+    stores = [pltpu.make_async_copy(asking, out.at[:, pl.ds(2 * TILE, TILE), :], sems.at[8])]
+    stores[0].start()
     scalars.wait()
     for load in loads[4:6]:
         load.wait()
-    stores = []
     for group in range(groups):
-        for k in range(seq_count // groups):
-            i = group * (seq_count // groups) + k
+        span = pl.ds(group * each, each)
+        for i in range(group * each, (group + 1) * each):
             code = codes[0, i * tiles]
             asked = lax.rem(code, tiles)
             table[0, i] = asked
             table[1, i] = lax.div(code, tiles)
             tile = pl.ds(pl.multiple_of(asked * TILE, TILE), TILE)
-            staged[group, k, 0:TILE, :] = held[0, tile, :]
-            staged[group, k, TILE : 2 * TILE, :] = held[1, tile, :]
-        span = pl.ds(group * (seq_count // groups), seq_count // groups)
-        stores.append(pltpu.make_async_copy(staged.at[group], out.at[span], sems.at[8 + group]))
+            staged[i, 0:TILE, :] = held[0, tile, :]
+            staged[i, TILE : 2 * TILE, :] = held[1, tile, :]
+        stores.append(
+            pltpu.make_async_copy(staged.at[span], out.at[span, pl.ds(0, 2 * TILE), :], sems.at[9 + group])
+        )
         stores[-1].start()
     for store in stores:
         store.wait()
@@ -188,11 +191,13 @@
 
 
 def forward_kernel(
-    scale, list_length, table, fetched, queries, core, own, other, grads, out, attention, stats,
+    scale, list_length, table, fetched, queries, core, own, other, grads, out, attention, stats, requests,
     spread, staged, sems,
 ):
     tiles = queries.shape[0] // TILE
     seq_count = out.shape[0]
+    asked = pltpu.make_async_copy(fetched.at[:, pl.ds(2 * TILE, TILE), :], requests, sems.at[seq_count])
+    asked.start()
     model = 2 * own.shape[0]
     chunk = model // seq_count
     lane = lax.broadcasted_iota(jnp.int32, (WIDTH, WIDTH), 1)
@@ -249,6 +254,7 @@
                 stores[-1].start()
     for store in stores:
         store.wait()
+    asked.wait()
 
 
 def query_kernel(scale, list_length, table, fetched, queries, grads, stats, out):
@@ -280,7 +286,7 @@
         store.wait()
 
 
-def owner_kernel(scale, chunk, group, table, fetched, arrived, keys, values, grad_keys, grad_values, key_sum, value_sum):
+def owner_kernel(scale, chunk, group, table, requests, arrived, keys, values, grad_keys, grad_values, key_sum, value_sum):
     tok_rows = keys.shape[0]
     senders = arrived.shape[0]
     key_tile = lax.broadcasted_iota(jnp.int32, (tok_rows, WIDTH), 0) // TILE
@@ -291,7 +297,7 @@
         query2, grad2, logs, deltas, keeps = [], [], [], [], []
         for k in range(group):
             i = at * group + k
-            query2.append(split_heads(fetched[i, 2 * TILE : 3 * TILE, :]))
+            query2.append(split_heads(requests[i]))
             grad2.append(split_heads(arrived[i, chunk : chunk + TILE, :]))
             parts = arrived[i, chunk + TILE : chunk + TILE + STAT_ROWS, :].astype(F32)
             logs.append(parts[0:1] + parts[1:2] + parts[2:3])
@@ -323,6 +329,12 @@
     grad_values[...] = value_sum[...].astype(BF16)
 
 
+def write_kernel(gathered, out, sem):
+    copy = pltpu.make_async_copy(gathered, out, sem)
+    copy.start()
+    copy.wait()
+
+
 def exchange(blocks):
     return lax.all_to_all(blocks, "seq", split_axis=0, concat_axis=0, tiled=True)
 
@@ -363,11 +375,12 @@
             pltpu.SMEM((1,) + kv_counts.shape, jnp.int32),
             pltpu.VMEM(lists.shape, jnp.int32),
             pltpu.VMEM((1,) + kv_counts.shape, jnp.int32),
-            pltpu.VMEM((groups, seq_count // groups, 3 * TILE, row_width), BF16),
+            pltpu.VMEM((seq_count, 2 * TILE, row_width), BF16),
+            pltpu.VMEM((seq_count, TILE, row_width), BF16),
             pltpu.VMEM(lists.shape, jnp.int32),
             pltpu.SMEM(lists.shape, jnp.int32),
             pltpu.VMEM((3, tok_rows, row_width), BF16),
-            pltpu.SemaphoreType.DMA((8 + groups,)),
+            pltpu.SemaphoreType.DMA((9 + groups,)),
         ],
         compiler_params=PARAMS,
         name="pack",
@@ -394,19 +407,20 @@
         name="attention_grad",
     )(core, grad_t, other_t, stay(out_weight))
 
-    second, attention, stats = pl.pallas_call(
+    second, attention, stats, requests = pl.pallas_call(
         functools.partial(forward_kernel, scale, list_length),
         out_shape=(
             pltpu.HBM((seq_count, chunk + TILE + STAT_ROWS, row_width), BF16),
             block,
             jax.ShapeDtypeStruct((WIDTH, WIDTH), F32),
+            pltpu.HBM((seq_count, TILE, row_width), BF16),
         ),
         in_specs=[SMEM, VMEM, VMEM, SMEM, VMEM, VMEM, VMEM],
-        out_specs=(HBM, VMEM, VMEM),
+        out_specs=(HBM, VMEM, VMEM, HBM),
         scratch_shapes=[
             pltpu.VMEM((tiles_dev, TILE + STAT_ROWS, row_width), BF16),
             pltpu.VMEM((seq_count, chunk + TILE + STAT_ROWS, row_width), BF16),
-            pltpu.SemaphoreType.DMA((seq_count,)),
+            pltpu.SemaphoreType.DMA((seq_count + 1,)),
         ],
         compiler_params=PARAMS,
         name="forward",
@@ -481,7 +495,7 @@
         compiler_params=PARAMS,
         cost_estimate=pl.CostEstimate(flops=1_100_000_000, bytes_accessed=4_000_000, transcendentals=1_000_000),
         name="owner_grad",
-    )(table, fetched, arrived, keys, values)
+    )(table, requests, arrived, keys, values)
     mixed = pl.pallas_call(
         last_kernel,
         out_shape=jax.ShapeDtypeStruct((run, tok_rows), BF16),
@@ -490,8 +504,17 @@
         compiler_params=PARAMS,
         name="mixed_last",
     )(mine, to_chip(sent, 4), stay(grad_keys)).T
+    written = pl.pallas_call(
+        write_kernel,
+        out_shape=pltpu.HBM(gathered.shape, BF16),
+        in_specs=[VMEM],
+        out_specs=HBM,
+        scratch_shapes=[pltpu.SemaphoreType.DMA],
+        compiler_params=PARAMS,
+        name="write",
+    )(pltpu.with_memory_space_constraint(gathered, pltpu.VMEM))
     weight_grad = (
-        gathered.reshape(row_width // FEW, seq_count * FEW // row_width, chunk // FEW, FEW, WIDTH)
+        written.reshape(row_width // FEW, seq_count * FEW // row_width, chunk // FEW, FEW, WIDTH)
         .transpose(0, 3, 1, 2, 4)
         .reshape(out_weight.shape)
     )

time: 135 us -> 134 us (level)
    unnamed x13 -> x14, local copies, waits for them, and re-layouts: 4.09 us -> 3.05 us
where the time goes in v5:
time: 134 us; the launch traced here: 133 us
  starting transfers between devices  54.4 us (41%)
  blocking collectives  32.4 us (24%)
  Pallas kernels  24 us (18%)
  waiting for transfers between devices  18.1 us (14%)
  local copies, waits for them, and re-layouts  3.05 us (2%)
    all_gather x1, blocking collectives, body(): grad_t = lax.all_gather(grad_mixed.T, 'z', axis=0, tiled=True)  32.4 us
    all_to_all x3, starting transfers between devices, exchange(): lax.all_to_all(blocks, 'seq', split_axis=0, concat_axis=0, tiled=True)  27.7 us
    ppermute x5, starting transfers between devices, to_chip(): lax.ppermute(array, 'z', [(z, (z + apart) % chips) for z in range(chips)])  22.9 us
    all_to_all x3, waiting for transfers between devices, exchange(): lax.all_to_all(blocks, 'seq', split_axis=0, concat_axis=0, tiled=True)  11.8 us
    pallas_call x1, Pallas kernels, body(): pl.pallas_call(functools.partial(owner_kernel, scale, chunk, 4), out_shap...  5.73 us
    ppermute x2, waiting for transfers between devices, swap_cores(): return lax.ppermute(array, 'core', [(0, 1), (1, 0)])  4.84 us
    pallas_call x1, Pallas kernels, body(): pl.pallas_call(functools.partial(forward_kernel, scale, list_length), out...  4.12 us
    ppermute x2, starting transfers between devices, swap_cores(): return lax.ppermute(array, 'core', [(0, 1), (1, 0)])  3.82 us
  transfers between devices with their start and end apart: 10, of which 6 were waited for; matrix products, arithmetic and copies ran while one was open for 0% of the time, Pallas kernels for 11%

profile of v5, /device:TPU:2, one launch (start us, length us, event | category | flops | bytes accessed | tf_op | source)
XLA Modules:
  0.0 132.9 jit_solution(15884596354996031766)
XLA Ops:
  0.6 3.2 %pack.1 = (bf16[32,192,128]{2,1,0:T(8,128)(2,1)}, s32[5,32]{1,0:T(8,128)S(1)}) custom-call(s32[1]{0:T(128)} %bitcast.2.place, s32[8,128]{1,0:T(8,128)} %bitcast.15, s32[1,128]{1,0:T(1,128)} %bitcast.16, bf16[256,128]{1,0:T(8,128)(2,1)} %queries.5, bf16[256,128]{1,0:T(8,128)(2,1)} %keys.3, bf16[256,128]{1,0:T(8,128)(2,1)} %values.3), custom_call_target="tpu_custom_call" | custom-call | tf_op jit(solution)/shard_map/pack/pallas_call | solution.py:365
  3.8 0.0 copy-start.6
  3.8 10.4 %all-to-all-start = ((bf16[32,192,128]{2,1,0:T(8,128)(2,1)}), bf16[32,192,128]{2,1,0:T(8,128)(2,1)S(1)}, u32[]{:S(2)}, u32[]{:S(2)}) async-start(bf16[32,192,128]{2,1,0:T(8,128)(2,1)} %get-tuple-element.23), calls=%async_computation | async-start | bytes 3145728 | tf_op jit(solution)/shard_map/all_to_all | solution.py:339
  14.2 0.0 copy-done.6
  14.3 32.4 %all_gather.3.own = bf16[1536,256]{1,0:T(8,128)(2,1)S(1)} all-gather(bf16[192,256]{1,0:T(8,128)(2,1)S(1)} %bitcast.13), channel_id=1, replica_groups=mesh['seq'=32,'z'=8,'core'=2] {'z'}, dimensions={0}, use_global_device_ids=true | all-gather | bytes 884736 | tf_op jit(solution)/shard_map/all_gather | solution.py:362
  46.7 1.9 %collective-permute-start = (bf16[1536,256]{1,0:T(8,128)(2,1)S(1)}, bf16[1536,256]{1,0:T(8,128)(2,1)S(1)}, u32[]{:S(2)}, u32[]{:S(2)}) collective-permute-start(bf16[1536,256]{1,0:T(8,128)(2,1)S(1)} %all_gather.3.own), channel_id=1, source_target_pairs={{0,1},{1,0},{2,3},{3,2},{4,5},{5,4},{6,7},{7,6},{8,9},{9,8},{10,11... | collective-permute-start | bytes 2359304 | tf_op jit(solution)/shard_map/ppermute | solution.py:343
  48.6 2.2 %collective-permute-done.other = bf16[1536,256]{1,0:T(8,128)(2,1)S(1)} collective-permute-done((bf16[1536,256]{1,0:T(8,128)(2,1)S(1)}, bf16[1536,256]{1,0:T(8,128)(2,1)S(1)}, u32[]{:S(2)}, u32[]{:S(2)}) %collective-permute-start) | collective-permute-done | bytes 786464 | tf_op jit(solution)/shard_map/ppermute | solution.py:343
  50.8 0.0 copy-start.2
  50.8 1.7 %attention_grad.1.grads = bf16[256,128]{1,0:T(8,128)(2,1)S(1)} custom-call(s32[1]{0:T(128)} %bitcast.1.core, bf16[1536,256]{1,0:T(8,128)(2,1)S(1)} %all_gather.3.own, bf16[1536,256]{1,0:T(8,128)(2,1)S(1)} %collective-permute-done.other, bf16[128,3072]{1,0:T(8,128)(2,1)} %weight_h.3), custom_call_target="tpu_custom_call" | custom-call | flops 3000000000 | bytes 3000000 | tf_op jit(solution)/shard_map/attention_grad/pallas_call | solution.py:399
  52.6 0.0 all-to-all-done.fetched
  52.6 0.0 copy-done.2
  52.6 4.1 %forward.1 = (bf16[32,168,128]{2,1,0:T(8,128)(2,1)}, bf16[256,128]{1,0:T(8,128)(2,1)S(1)}, f32[128,128]{1,0:T(8,128)S(1)}, bf16[32,64,128]{2,1,0:T(8,128)(2,1)}) custom-call(s32[5,32]{1,0:T(8,128)S(1)} %get-tuple-element.22.table, bf16[32,192,128]{2,1,0:T(8,128)(2,1)S(1)} %all-to-all-done.fetched, bf16[256,128]{1,0:T(8,128)(2,1)S(1)} %copy-done.2, ...), custom_call_target="tpu_custom_call" | custom-call | tf_op jit(solution)/shard_map/forward/pallas_call | solution.py:410
  56.7 9.8 %all-to-all-start.1 = ((bf16[32,168,128]{2,1,0:T(8,128)(2,1)}), bf16[32,168,128]{2,1,0:T(8,128)(2,1)S(1)}, u32[]{:S(2)}, u32[]{:S(2)}) async-start(bf16[32,168,128]{2,1,0:T(8,128)(2,1)} %get-tuple-element.35), calls=%async_computation.1 | async-start | bytes 2752512 | tf_op jit(solution)/shard_map/all_to_all | solution.py:339
  66.5 2.6 %mixed_share.1 = (bf16[8,192,256]{2,1,0:T(8,128)(2,1)S(1)}, bf16[8,192,256]{2,1,0:T(8,128)(2,1)}) custom-call(s32[1]{0:T(128)} %bitcast.1.core, bf16[128,3072]{1,0:T(8,128)(2,1)} %weight_h.3, bf16[256,128]{1,0:T(8,128)(2,1)S(1)} %get-tuple-element.24.attention), custom_call_target="tpu_custom_call" | custom-call | tf_op jit(solution)/shard_map/mixed_share/pallas_call | solution.py:433
  69.2 0.0 copy-start
  69.2 0.9 copy-done
  70.0 1.9 %collective-permute-start.1 = (bf16[8,192,256]{2,1,0:T(8,128)(2,1)}, bf16[8,192,256]{2,1,0:T(8,128)(2,1)}, u32[]{:S(2)}, u32[]{:S(2)}) collective-permute-start(bf16[8,192,256]{2,1,0:T(8,128)(2,1)} %get-tuple-element.26), channel_id=1, source_target_pairs={{0,1},{1,0},{2,3},{3,2},{4,5},{5,4},{6,7},{7,6},{8,9},{9,8},{10,11... | collective-permute-start | bytes 2359304 | tf_op jit(solution)/shard_map/ppermute | solution.py:343
  72.0 2.6 %collective-permute-done.1.arrived = bf16[8,192,256]{2,1,0:T(8,128)(2,1)} collective-permute-done((bf16[8,192,256]{2,1,0:T(8,128)(2,1)}, bf16[8,192,256]{2,1,0:T(8,128)(2,1)}, u32[]{:S(2)}, u32[]{:S(2)}) %collective-permute-start.1) | collective-permute-done | bytes 786464 | tf_op jit(solution)/shard_map/ppermute | solution.py:343
  74.5 0.0 copy-start.1
  74.6 1.1 copy-done.1
  75.7 1.6 %mixed_pair.1 = (f32[2,192,256]{2,1,0:T(8,128)S(1)}, bf16[2,192,256]{2,1,0:T(8,128)(2,1)S(1)}, bf16[2,192,256]{2,1,0:T(8,128)(2,1)S(1)}, bf16[1,192,256]{2,1,0:T(8,128)(2,1)S(1)}, bf16[1,192,256]{2,1,0:T(8,128)(2,1)S(1)}) custom-call(s32[1]{0:T(128)} %bitcast.place, bf16[8,192,256]{2,1,0:T(8,128)(2,1)S(1)} %copy-done.1, ...), custom_call_target="tpu_custom_call" | custom-call | tf_op jit(solution)/shard_map/mixed_pair/pallas_call | solution.py:442
  77.3 3.5 %collective-permute-start.2 = (bf16[2,192,256]{2,1,0:T(8,128)(2,1)S(1)}, bf16[2,192,256]{2,1,0:T(8,128)(2,1)S(1)}, u32[]{:S(2)}, u32[]{:S(2)}) collective-permute-start(bf16[2,192,256]{2,1,0:T(8,128)(2,1)S(1)} %get-tuple-element.28), channel_id=1, source_target_pairs={{0,2},{2,4},{4,6},{6,8},{8,10},{10,12},{12,14},{14,0},{1,3},{3,5},... | collective-permute-start | bytes 589832 | tf_op jit(solution)/shard_map/ppermute | solution.py:348
  80.8 6.2 %collective-permute-start.3 = (bf16[2,192,256]{2,1,0:T(8,128)(2,1)S(1)}, bf16[2,192,256]{2,1,0:T(8,128)(2,1)S(1)}, u32[]{:S(2)}, u32[]{:S(2)}) collective-permute-start(bf16[2,192,256]{2,1,0:T(8,128)(2,1)S(1)} %get-tuple-element.29), channel_id=1, source_target_pairs={{0,14},{2,0},{4,2},{6,4},{8,6},{10,8},{12,10},{14,12},{1,15},{3,1}... | collective-permute-start | bytes 589832 | tf_op jit(solution)/shard_map/ppermute | solution.py:348
  86.9 1.9 %collective-permute-start.4 = (bf16[1,192,256]{2,1,0:T(8,128)(2,1)S(1)}, bf16[1,192,256]{2,1,0:T(8,128)(2,1)S(1)}, u32[]{:S(2)}, u32[]{:S(2)}) collective-permute-start(bf16[1,192,256]{2,1,0:T(8,128)(2,1)S(1)} %get-tuple-element.30), channel_id=1, source_target_pairs={{0,4},{2,6},{4,8},{6,10},{8,12},{10,14},{12,0},{14,2},{1,5},{3,7},... | collective-permute-start | bytes 294920 | tf_op jit(solution)/shard_map/ppermute | solution.py:348
  88.9 6.0 %collective-permute-start.5 = (bf16[1,192,256]{2,1,0:T(8,128)(2,1)S(1)}, bf16[1,192,256]{2,1,0:T(8,128)(2,1)S(1)}, u32[]{:S(2)}, u32[]{:S(2)}) collective-permute-start(bf16[1,192,256]{2,1,0:T(8,128)(2,1)S(1)} %get-tuple-element.31), channel_id=1, source_target_pairs={{0,12},{2,14},{4,0},{6,2},{8,4},{10,6},{12,8},{14,10},{1,13},{3,15... | collective-permute-start | bytes 294920 | tf_op jit(solution)/shard_map/ppermute | solution.py:348
  94.9 2.3 %query_grad.1.grad_queries = bf16[256,128]{1,0:T(8,128)(2,1)} custom-call(s32[5,32]{1,0:T(8,128)S(1)} %get-tuple-element.22.table, bf16[32,192,128]{2,1,0:T(8,128)(2,1)S(1)} %all-to-all-done.fetched, bf16[256,128]{1,0:T(8,128)(2,1)S(1)} %copy-done.2, bf16[256,128]{1,0:T(8,128)(2,1)S(1)} %attention_grad.1.grads, f32[128,128]{1,0:T(8,128)S(1)} %get-tuple-element.37.stats), custom_call_target="tpu_custom_call" | custom-call | flops 400000000 | bytes 4000000 | tf_op jit(solution)/shard_map/query_grad/pallas_call | solution.py:468
  97.2 0.4 collective-permute-done.4.next_2
  97.6 1.0 collective-permute-done.5.back_2
  98.6 0.0 collective-permute-done.2.next_1
  98.6 0.0 collective-permute-done.3.back_1
  98.7 0.1 mixed_near.1
  98.8 2.3 %all-to-all-done.1.arrived = bf16[32,168,128]{2,1,0:T(8,128)(2,1)S(1)} async-done(((bf16[32,168,128]{2,1,0:T(8,128)(2,1)}), bf16[32,168,128]{2,1,0:T(8,128)(2,1)S(1)}, u32[]{:S(2)}, u32[]{:S(2)}) %all-to-all-start.1) | async-done | bytes 1376288 | tf_op jit(solution)/shard_map/all_to_all | solution.py:339
  101.1 0.0 copy-start.3
  101.1 0.0 copy-start.4
  101.1 1.1 sum_share.1
  102.1 7.5 %all-to-all-start.2 = ((bf16[32,96,128]{2,1,0:T(8,128)(2,1)}), bf16[32,96,128]{2,1,0:T(8,128)(2,1)S(1)}, u32[]{:S(2)}, u32[]{:S(2)}) async-start(bf16[32,96,128]{2,1,0:T(8,128)(2,1)} %sum_share.1), calls=%async_computation.2 | async-start | bytes 1572864 | tf_op jit(solution)/shard_map/all_to_all | solution.py:339
  109.6 5.4 %collective-permute-start.6 = (bf16[192,256]{1,0:T(8,128)(2,1)S(1)}, bf16[192,256]{1,0:T(8,128)(2,1)S(1)}, u32[]{:S(2)}, u32[]{:S(2)}) collective-permute-start(bf16[192,256]{1,0:T(8,128)(2,1)S(1)} %get-tuple-element.33.mixed_part), channel_id=1, source_target_pairs={{0,8},{2,10},{4,12},{6,14},{8,0},{10,2},{12,4},{14,6},{1,9},{3,11}... | collective-permute-start | bytes 294920 | tf_op jit(solution)/shard_map/ppermute | solution.py:348
  115.0 0.0 copy-done.3
  115.0 0.0 copy-done.4
  115.1 0.0 copy-start.5
  115.1 1.0 copy-done.5
  116.1 5.7 %owner_grad.1 = (bf16[256,128]{1,0:T(8,128)(2,1)}, bf16[256,128]{1,0:T(8,128)(2,1)}) custom-call(s32[5,32]{1,0:T(8,128)S(1)} %get-tuple-element.22.table, bf16[32,64,128]{2,1,0:T(8,128)(2,1)S(1)} %copy-done.5, bf16[32,168,128]{2,1,0:T(8,128)(2,1)S(1)} %all-to-all-done.1.arrived, bf16[256,128]{1,0:T(8,128)(2,1)S(1)} %copy-done.3, bf16[256,128]{1,0:T(8,128)(2,1)S(1)} %copy-done.4), custom_call_target="tpu_custom_call" | custom-call | flops 1100000000 | bytes 4000000 | tf_op jit(solution)/shard_map/owner_grad/pallas_call | solution.py:489
  121.8 0.0 collective-permute-done.6.arrived
  121.8 0.7 mixed_last.1
  122.5 9.5 %all-to-all-done.2.gathered = bf16[32,96,128]{2,1,0:T(8,128)(2,1)S(1)} async-done(((bf16[32,96,128]{2,1,0:T(8,128)(2,1)}), bf16[32,96,128]{2,1,0:T(8,128)(2,1)S(1)}, u32[]{:S(2)}, u32[]{:S(2)}) %all-to-all-start.2) | async-done | bytes 786464 | tf_op jit(solution)/shard_map/all_to_all | solution.py:339
  132.0 0.9 write.1
Async XLA Ops:
  3.8 10.4 %copy-start.6 = (bf16[256,192]{0,1:T(8,128)(2,1)S(1)}, bf16[256,192]{0,1:T(8,128)(2,1)}, u32[]{:S(2)}) copy-start(bf16[256,192]{0,1:T(8,128)(2,1)} %param.11) | copy-start | bytes 294916
  3.8 48.8 %all-to-all-start = ((bf16[32,192,128]{2,1,0:T(8,128)(2,1)}), bf16[32,192,128]{2,1,0:T(8,128)(2,1)S(1)}, u32[]{:S(2)}, u32[]{:S(2)}) async-start(bf16[32,192,128]{2,1,0:T(8,128)(2,1)} %get-tuple-element.23), calls=%async_computation | async-start | bytes 3145728 | tf_op jit(solution)/shard_map/all_to_all | solution.py:339
  46.7 4.2 %collective-permute-start = (bf16[1536,256]{1,0:T(8,128)(2,1)S(1)}, bf16[1536,256]{1,0:T(8,128)(2,1)S(1)}, u32[]{:S(2)}, u32[]{:S(2)}) collective-permute-start(bf16[1536,256]{1,0:T(8,128)(2,1)S(1)} %all_gather.3.own), channel_id=1, source_target_pairs={{0,1},{1,0},{2,3},{3,2},{4,5},{5,4},{6,7},{7,6},{8,9},{9,8},{10,11... | collective-permute-start | bytes 2359304 | tf_op jit(solution)/shard_map/ppermute | solution.py:343
  50.8 1.8 %copy-start.2 = (bf16[256,128]{1,0:T(8,128)(2,1)S(1)}, bf16[256,128]{1,0:T(8,128)(2,1)}, u32[]{:S(2)}) copy-start(bf16[256,128]{1,0:T(8,128)(2,1)} %queries.5) | copy-start | bytes 196612
  56.7 44.3 %all-to-all-start.1 = ((bf16[32,168,128]{2,1,0:T(8,128)(2,1)}), bf16[32,168,128]{2,1,0:T(8,128)(2,1)S(1)}, u32[]{:S(2)}, u32[]{:S(2)}) async-start(bf16[32,168,128]{2,1,0:T(8,128)(2,1)} %get-tuple-element.35), calls=%async_computation.1 | async-start | bytes 2752512 | tf_op jit(solution)/shard_map/all_to_all | solution.py:339
  69.2 0.9 copy-start
  70.0 4.5 %collective-permute-start.1 = (bf16[8,192,256]{2,1,0:T(8,128)(2,1)}, bf16[8,192,256]{2,1,0:T(8,128)(2,1)}, u32[]{:S(2)}, u32[]{:S(2)}) collective-permute-start(bf16[8,192,256]{2,1,0:T(8,128)(2,1)} %get-tuple-element.26), channel_id=1, source_target_pairs={{0,1},{1,0},{2,3},{3,2},{4,5},{5,4},{6,7},{7,6},{8,9},{9,8},{10,11... | collective-permute-start | bytes 2359304 | tf_op jit(solution)/shard_map/ppermute | solution.py:343
  74.5 1.1 copy-start.1
  77.3 21.3 %collective-permute-start.2 = (bf16[2,192,256]{2,1,0:T(8,128)(2,1)S(1)}, bf16[2,192,256]{2,1,0:T(8,128)(2,1)S(1)}, u32[]{:S(2)}, u32[]{:S(2)}) collective-permute-start(bf16[2,192,256]{2,1,0:T(8,128)(2,1)S(1)} %get-tuple-element.28), channel_id=1, source_target_pairs={{0,2},{2,4},{4,6},{6,8},{8,10},{10,12},{12,14},{14,0},{1,3},{3,5},... | collective-permute-start | bytes 589832 | tf_op jit(solution)/shard_map/ppermute | solution.py:348
  80.8 17.9 %collective-permute-start.3 = (bf16[2,192,256]{2,1,0:T(8,128)(2,1)S(1)}, bf16[2,192,256]{2,1,0:T(8,128)(2,1)S(1)}, u32[]{:S(2)}, u32[]{:S(2)}) collective-permute-start(bf16[2,192,256]{2,1,0:T(8,128)(2,1)S(1)} %get-tuple-element.29), channel_id=1, source_target_pairs={{0,14},{2,0},{4,2},{6,4},{8,6},{10,8},{12,10},{14,12},{1,15},{3,1}... | collective-permute-start | bytes 589832 | tf_op jit(solution)/shard_map/ppermute | solution.py:348
  86.9 10.7 %collective-permute-start.4 = (bf16[1,192,256]{2,1,0:T(8,128)(2,1)S(1)}, bf16[1,192,256]{2,1,0:T(8,128)(2,1)S(1)}, u32[]{:S(2)}, u32[]{:S(2)}) collective-permute-start(bf16[1,192,256]{2,1,0:T(8,128)(2,1)S(1)} %get-tuple-element.30), channel_id=1, source_target_pairs={{0,4},{2,6},{4,8},{6,10},{8,12},{10,14},{12,0},{14,2},{1,5},{3,7},... | collective-permute-start | bytes 294920 | tf_op jit(solution)/shard_map/ppermute | solution.py:348
  88.9 9.8 %collective-permute-start.5 = (bf16[1,192,256]{2,1,0:T(8,128)(2,1)S(1)}, bf16[1,192,256]{2,1,0:T(8,128)(2,1)S(1)}, u32[]{:S(2)}, u32[]{:S(2)}) collective-permute-start(bf16[1,192,256]{2,1,0:T(8,128)(2,1)S(1)} %get-tuple-element.31), channel_id=1, source_target_pairs={{0,12},{2,14},{4,0},{6,2},{8,4},{10,6},{12,8},{14,10},{1,13},{3,15... | collective-permute-start | bytes 294920 | tf_op jit(solution)/shard_map/ppermute | solution.py:348
  101.1 14.0 %copy-start.3 = (bf16[256,128]{1,0:T(8,128)(2,1)S(1)}, bf16[256,128]{1,0:T(8,128)(2,1)}, u32[]{:S(2)}) copy-start(bf16[256,128]{1,0:T(8,128)(2,1)} %keys.3) | copy-start | bytes 196612
  101.1 14.0 %copy-start.4 = (bf16[256,128]{1,0:T(8,128)(2,1)S(1)}, bf16[256,128]{1,0:T(8,128)(2,1)}, u32[]{:S(2)}) copy-start(bf16[256,128]{1,0:T(8,128)(2,1)} %values.3) | copy-start | bytes 196612
  102.1 29.8 %all-to-all-start.2 = ((bf16[32,96,128]{2,1,0:T(8,128)(2,1)}), bf16[32,96,128]{2,1,0:T(8,128)(2,1)S(1)}, u32[]{:S(2)}, u32[]{:S(2)}) async-start(bf16[32,96,128]{2,1,0:T(8,128)(2,1)} %sum_share.1), calls=%async_computation.2 | async-start | bytes 1572864 | tf_op jit(solution)/shard_map/all_to_all | solution.py:339
  109.6 12.2 %collective-permute-start.6 = (bf16[192,256]{1,0:T(8,128)(2,1)S(1)}, bf16[192,256]{1,0:T(8,128)(2,1)S(1)}, u32[]{:S(2)}, u32[]{:S(2)}) collective-permute-start(bf16[192,256]{1,0:T(8,128)(2,1)S(1)} %get-tuple-element.33.mixed_part), channel_id=1, source_target_pairs={{0,8},{2,10},{4,12},{6,14},{8,0},{10,2},{12,4},{14,6},{1,9},{3,11}... | collective-permute-start | bytes 294920 | tf_op jit(solution)/shard_map/ppermute | solution.py:348
  115.1 1.0 copy-start.5

commit v6 on v5

--- a/solution.py
+++ b/solution.py
@@ -121,15 +121,24 @@
     return jnp.concatenate([jnp.where(first, mine, theirs), jnp.where(first, theirs, mine)], axis=0)
 
 
-def grad_kernel(core, own, other, weight_h, grads, weight, sem):
+def partial_grad(core, weight, mine, theirs):
+    none = jnp.zeros_like(mine if theirs is None else theirs)
+    own, other = (none if half is None else half for half in (mine, theirs))
+    wide = 2 * weight.shape[1] // GATHERED
+    return sum(
+        dot(weight[:, z * wide : (z + 1) * wide], joined(core, own, other, z)) for z in range(GATHERED // 2)
+    )
+
+
+def own_grad_kernel(core, own, weight_h, partial, weight, sem):
     load = pltpu.make_async_copy(weight_h, weight, sem)
     load.start()
     load.wait()
-    wide = 2 * weight.shape[1] // GATHERED
-    total = jnp.zeros((WIDTH, grads.shape[0]), F32)
-    for z in range(GATHERED // 2):
-        total += dot(weight[:, z * wide : (z + 1) * wide], joined(core[0], own, other, z))
-    grads[...] = total.T.astype(BF16)
+    partial[...] = partial_grad(core[0], weight, own[...], None)
+
+
+def other_grad_kernel(core, other, weight, partial, grads):
+    grads[...] = (partial[...] + partial_grad(core[0], weight, None, other[...])).T.astype(BF16)
 
 
 def mixed_kernel(core, weight_h, attention, keep, send, weight, sem):
@@ -164,14 +173,15 @@
                 target[slot] = total.astype(target.dtype)
 
 
-def near_kernel(mine, next_1, back_1, next_2, back_2, keep, send):
+def near_kernel(mine, next_1, back_1, next_2, keep, send):
     here, opposite = (mine[i] + next_1[i].astype(F32) + back_1[i].astype(F32) for i in range(2))
-    keep[...] = here + next_2[0].astype(F32) + back_2[0].astype(F32)
+    keep[...] = here + next_2[0].astype(F32)
     send[...] = opposite.astype(BF16)
 
 
-def last_kernel(mine, arrived, grad_keys, out):
-    out[...] = (mine[...] + arrived[...].astype(F32)).astype(BF16)
+def last_kernel(mine, back_2, arrived, grad_keys, out):
+    total = mine[...] + back_2[0].astype(F32)
+    out[...] = (total + arrived[...].astype(F32)).astype(BF16)
 
 
 def listed(table, fetched, tile, list_length, part):
@@ -396,16 +406,27 @@
     other_t = swap_cores(grad_t)
     core = lax.axis_index("core")[None].astype(jnp.int32)
 
+    partial, weight_v = pl.pallas_call(
+        own_grad_kernel,
+        out_shape=(
+            jax.ShapeDtypeStruct((row_width, tok_rows), F32),
+            jax.ShapeDtypeStruct(out_weight.shape, BF16),
+        ),
+        in_specs=[SMEM, VMEM, HBM],
+        out_specs=(VMEM, VMEM),
+        scratch_shapes=[pltpu.SemaphoreType.DMA],
+        compiler_params=PARAMS,
+        cost_estimate=pl.CostEstimate(flops=3_000_000_000, bytes_accessed=3_000_000, transcendentals=0),
+        name="own_grad",
+    )(core, grad_t, stay(out_weight))
     grads = pl.pallas_call(
-        grad_kernel,
+        other_grad_kernel,
         out_shape=block,
-        in_specs=[SMEM, VMEM, VMEM, HBM],
+        in_specs=[SMEM, VMEM, VMEM, VMEM],
         out_specs=VMEM,
-        scratch_shapes=[pltpu.VMEM(out_weight.shape, BF16), pltpu.SemaphoreType.DMA],
-        compiler_params=PARAMS,
-        cost_estimate=pl.CostEstimate(flops=3_000_000_000, bytes_accessed=3_000_000, transcendentals=0),
-        name="attention_grad",
-    )(core, grad_t, other_t, stay(out_weight))
+        compiler_params=PARAMS,
+        name="other_grad",
+    )(core, other_t, weight_v, partial)
 
     second, attention, stats, requests = pl.pallas_call(
         functools.partial(forward_kernel, scale, list_length),
@@ -439,7 +460,7 @@
         compiler_params=PARAMS,
         name="mixed_share",
     )(core, stay(out_weight), attention)
-    mine, *sent = pl.pallas_call(
+    mine, next_1, back_1, next_2, back_2 = pl.pallas_call(
         pair_kernel,
         out_shape=(
             jax.ShapeDtypeStruct((2, run, tok_rows), F32),
@@ -459,11 +480,11 @@
             jax.ShapeDtypeStruct((run, tok_rows), F32),
             jax.ShapeDtypeStruct((run, tok_rows), BF16),
         ),
-        in_specs=[VMEM] * 5,
+        in_specs=[VMEM] * 4,
         out_specs=(VMEM, VMEM),
         compiler_params=PARAMS,
         name="mixed_near",
-    )(mine, *(to_chip(part, apart) for part, apart in zip(sent, (1, -1, 2, -2), strict=True)))
+    )(mine, to_chip(next_1, 1), to_chip(back_1, -1), to_chip(next_2, 2))
 
     grad_queries = pl.pallas_call(
         functools.partial(query_kernel, scale, list_length),
@@ -499,11 +520,11 @@
     mixed = pl.pallas_call(
         last_kernel,
         out_shape=jax.ShapeDtypeStruct((run, tok_rows), BF16),
-        in_specs=[VMEM, VMEM, HBM],
+        in_specs=[VMEM, VMEM, VMEM, HBM],
         out_specs=VMEM,
         compiler_params=PARAMS,
         name="mixed_last",
-    )(mine, to_chip(sent, 4), stay(grad_keys)).T
+    )(mine, to_chip(back_2, -2), to_chip(sent, 4), stay(grad_keys)).T
     written = pl.pallas_call(
         write_kernel,
         out_shape=pltpu.HBM(gathered.shape, BF16),

time: 134 us -> 130 us (0.970)
  starting transfers between devices: 54.4 us -> 51.2 us
    ppermute x5, waiting for transfers between devices: 1.48 us -> 9.23 us  [to_chip(): lax.ppermute(array, 'z', [(z, (z + apart) % chips) for z in range(chips)])]
    all_to_all x3, waiting for transfers between devices: 11.8 us -> 5.2 us  [exchange(): lax.all_to_all(blocks, 'seq', split_axis=0, concat_axis=0, tiled=True)]
    ppermute x5, starting transfers between devices: 22.9 us -> 20.8 us  [to_chip(): lax.ppermute(array, 'z', [(z, (z + apart) % chips) for z in range(chips)])]
    ppermute x2, waiting for transfers between devices: 4.84 us -> 3.24 us  [swap_cores(): return lax.ppermute(array, 'core', [(0, 1), (1, 0)])]
  transfers between devices with their start and end apart: 10 -> 10, of which waited for: 6 -> 7; matrix products, arithmetic and copies ran while one was open for 0% -> 0% of each run, Pallas kernels for 11% -> 12%
where the time goes in v6:
time: 130 us
  starting transfers between devices  51.2 us (39%)
  blocking collectives  32.4 us (25%)
  Pallas kernels  24.3 us (19%)
  waiting for transfers between devices  17.7 us (14%)
  local copies, waits for them, and re-layouts  3.06 us (2%)
    all_gather x1, blocking collectives, body(): grad_t = lax.all_gather(grad_mixed.T, 'z', axis=0, tiled=True)  32.4 us
    all_to_all x3, starting transfers between devices, exchange(): lax.all_to_all(blocks, 'seq', split_axis=0, concat_axis=0, tiled=True)  26.6 us
    ppermute x5, starting transfers between devices, to_chip(): lax.ppermute(array, 'z', [(z, (z + apart) % chips) for z in range(chips)])  20.8 us
    ppermute x5, waiting for transfers between devices, to_chip(): lax.ppermute(array, 'z', [(z, (z + apart) % chips) for z in range(chips)])  9.23 us
    pallas_call x1, Pallas kernels, body(): pl.pallas_call(functools.partial(owner_kernel, scale, chunk, 4), out_shap...  5.72 us
    all_to_all x3, waiting for transfers between devices, exchange(): lax.all_to_all(blocks, 'seq', split_axis=0, concat_axis=0, tiled=True)  5.2 us
    pallas_call x1, Pallas kernels, body(): pl.pallas_call(functools.partial(forward_kernel, scale, list_length), out...  4.15 us
    ppermute x2, starting transfers between devices, swap_cores(): return lax.ppermute(array, 'core', [(0, 1), (1, 0)])  3.82 us
  transfers between devices with their start and end apart: 10, of which 7 were waited for; matrix products, arithmetic and copies ran while one was open for 0% of the time, Pallas kernels for 12%

profile of v6, /device:TPU:2, one launch (start us, length us, event | category | flops | bytes accessed | tf_op | source)
XLA Modules:
  0.0 129.6 jit_solution(198889689590702862)
XLA Ops:
  0.6 3.2 %pack.1 = (bf16[32,192,128]{2,1,0:T(8,128)(2,1)}, s32[5,32]{1,0:T(8,128)S(1)}) custom-call(s32[1]{0:T(128)} %bitcast.2.place, s32[8,128]{1,0:T(8,128)} %bitcast.15, s32[1,128]{1,0:T(1,128)} %bitcast.16, bf16[256,128]{1,0:T(8,128)(2,1)} %queries.5, bf16[256,128]{1,0:T(8,128)(2,1)} %keys.3, bf16[256,128]{1,0:T(8,128)(2,1)} %values.3), custom_call_target="tpu_custom_call" | custom-call | tf_op jit(solution)/shard_map/pack/pallas_call | solution.py:375
  3.8 0.0 copy-start.6
  3.8 10.4 %all-to-all-start = ((bf16[32,192,128]{2,1,0:T(8,128)(2,1)}), bf16[32,192,128]{2,1,0:T(8,128)(2,1)S(1)}, u32[]{:S(2)}, u32[]{:S(2)}) async-start(bf16[32,192,128]{2,1,0:T(8,128)(2,1)} %get-tuple-element.25), calls=%async_computation | async-start | bytes 3145728 | tf_op jit(solution)/shard_map/all_to_all | solution.py:349
  14.2 0.0 copy-done.6
  14.2 32.4 %all_gather.3.own = bf16[1536,256]{1,0:T(8,128)(2,1)S(1)} all-gather(bf16[192,256]{1,0:T(8,128)(2,1)S(1)} %bitcast.13), channel_id=1, replica_groups=mesh['seq'=32,'z'=8,'core'=2] {'z'}, dimensions={0}, use_global_device_ids=true | all-gather | bytes 884736 | tf_op jit(solution)/shard_map/all_gather | solution.py:372
  46.6 1.9 %collective-permute-start = (bf16[1536,256]{1,0:T(8,128)(2,1)S(1)}, bf16[1536,256]{1,0:T(8,128)(2,1)S(1)}, u32[]{:S(2)}, u32[]{:S(2)}) collective-permute-start(bf16[1536,256]{1,0:T(8,128)(2,1)S(1)} %all_gather.3.own), channel_id=1, source_target_pairs={{0,1},{1,0},{2,3},{3,2},{4,5},{5,4},{6,7},{7,6},{8,9},{9,8},{10,11... | collective-permute-start | bytes 2359304 | tf_op jit(solution)/shard_map/ppermute | solution.py:353
  48.6 1.6 %own_grad.1 = (f32[128,256]{1,0:T(8,128)S(1)}, bf16[128,3072]{1,0:T(8,128)(2,1)S(1)}) custom-call(s32[1]{0:T(128)} %bitcast.1.core, bf16[1536,256]{1,0:T(8,128)(2,1)S(1)} %all_gather.3.own, bf16[128,3072]{1,0:T(8,128)(2,1)} %weight_h.3), custom_call_target="tpu_custom_call" | custom-call | flops 3000000000 | bytes 3000000 | tf_op jit(solution)/shard_map/own_grad/pallas_call | solution.py:409
  50.1 0.0 copy-start.2
  50.2 0.7 collective-permute-done.other
  50.8 0.5 other_grad.1.grads
  51.3 1.2 all-to-all-done.fetched
  52.6 0.0 copy-done.2
  52.6 4.2 %forward.1 = (bf16[32,168,128]{2,1,0:T(8,128)(2,1)}, bf16[256,128]{1,0:T(8,128)(2,1)S(1)}, f32[128,128]{1,0:T(8,128)S(1)}, bf16[32,64,128]{2,1,0:T(8,128)(2,1)}) custom-call(s32[5,32]{1,0:T(8,128)S(1)} %get-tuple-element.24.table, bf16[32,192,128]{2,1,0:T(8,128)(2,1)S(1)} %all-to-all-done.fetched, bf16[256,128]{1,0:T(8,128)(2,1)S(1)} %copy-done.2, ...), custom_call_target="tpu_custom_call" | custom-call | tf_op jit(solution)/shard_map/forward/pallas_call | solution.py:431
  56.7 8.6 %all-to-all-start.1 = ((bf16[32,168,128]{2,1,0:T(8,128)(2,1)}), bf16[32,168,128]{2,1,0:T(8,128)(2,1)S(1)}, u32[]{:S(2)}, u32[]{:S(2)}) async-start(bf16[32,168,128]{2,1,0:T(8,128)(2,1)} %get-tuple-element.39), calls=%async_computation.1 | async-start | bytes 2752512 | tf_op jit(solution)/shard_map/all_to_all | solution.py:349
  65.3 2.6 %mixed_share.1 = (bf16[8,192,256]{2,1,0:T(8,128)(2,1)S(1)}, bf16[8,192,256]{2,1,0:T(8,128)(2,1)}) custom-call(s32[1]{0:T(128)} %bitcast.1.core, bf16[128,3072]{1,0:T(8,128)(2,1)} %weight_h.3, bf16[256,128]{1,0:T(8,128)(2,1)S(1)} %get-tuple-element.28.attention), custom_call_target="tpu_custom_call" | custom-call | tf_op jit(solution)/shard_map/mixed_share/pallas_call | solution.py:454
  68.0 0.0 copy-start
  68.0 0.9 copy-done
  68.9 1.9 %collective-permute-start.1 = (bf16[8,192,256]{2,1,0:T(8,128)(2,1)}, bf16[8,192,256]{2,1,0:T(8,128)(2,1)}, u32[]{:S(2)}, u32[]{:S(2)}) collective-permute-start(bf16[8,192,256]{2,1,0:T(8,128)(2,1)} %get-tuple-element.30), channel_id=1, source_target_pairs={{0,1},{1,0},{2,3},{3,2},{4,5},{5,4},{6,7},{7,6},{8,9},{9,8},{10,11... | collective-permute-start | bytes 2359304 | tf_op jit(solution)/shard_map/ppermute | solution.py:353
  70.8 2.6 %collective-permute-done.1.arrived = bf16[8,192,256]{2,1,0:T(8,128)(2,1)} collective-permute-done((bf16[8,192,256]{2,1,0:T(8,128)(2,1)}, bf16[8,192,256]{2,1,0:T(8,128)(2,1)}, u32[]{:S(2)}, u32[]{:S(2)}) %collective-permute-start.1) | collective-permute-done | bytes 786464 | tf_op jit(solution)/shard_map/ppermute | solution.py:353
  73.4 0.0 copy-start.1
  73.4 1.1 copy-done.1
  74.5 1.6 %mixed_pair.1 = (f32[2,192,256]{2,1,0:T(8,128)S(1)}, bf16[2,192,256]{2,1,0:T(8,128)(2,1)S(1)}, bf16[2,192,256]{2,1,0:T(8,128)(2,1)S(1)}, bf16[1,192,256]{2,1,0:T(8,128)(2,1)S(1)}, bf16[1,192,256]{2,1,0:T(8,128)(2,1)S(1)}) custom-call(s32[1]{0:T(128)} %bitcast.place, bf16[8,192,256]{2,1,0:T(8,128)(2,1)S(1)} %copy-done.1, ...), custom_call_target="tpu_custom_call" | custom-call | tf_op jit(solution)/shard_map/mixed_pair/pallas_call | solution.py:463
  76.1 3.5 %collective-permute-start.2 = (bf16[2,192,256]{2,1,0:T(8,128)(2,1)S(1)}, bf16[2,192,256]{2,1,0:T(8,128)(2,1)S(1)}, u32[]{:S(2)}, u32[]{:S(2)}) collective-permute-start(bf16[2,192,256]{2,1,0:T(8,128)(2,1)S(1)} %get-tuple-element.32), channel_id=1, source_target_pairs={{0,2},{2,4},{4,6},{6,8},{8,10},{10,12},{12,14},{14,0},{1,3},{3,5},... | collective-permute-start | bytes 589832 | tf_op jit(solution)/shard_map/ppermute | solution.py:358
  79.6 7.4 %collective-permute-start.3 = (bf16[2,192,256]{2,1,0:T(8,128)(2,1)S(1)}, bf16[2,192,256]{2,1,0:T(8,128)(2,1)S(1)}, u32[]{:S(2)}, u32[]{:S(2)}) collective-permute-start(bf16[2,192,256]{2,1,0:T(8,128)(2,1)S(1)} %get-tuple-element.33), channel_id=1, source_target_pairs={{0,14},{2,0},{4,2},{6,4},{8,6},{10,8},{12,10},{14,12},{1,15},{3,1}... | collective-permute-start | bytes 589832 | tf_op jit(solution)/shard_map/ppermute | solution.py:358
  87.0 1.9 %collective-permute-start.4 = (bf16[1,192,256]{2,1,0:T(8,128)(2,1)S(1)}, bf16[1,192,256]{2,1,0:T(8,128)(2,1)S(1)}, u32[]{:S(2)}, u32[]{:S(2)}) collective-permute-start(bf16[1,192,256]{2,1,0:T(8,128)(2,1)S(1)} %get-tuple-element.34), channel_id=1, source_target_pairs={{0,4},{2,6},{4,8},{6,10},{8,12},{10,14},{12,0},{14,2},{1,5},{3,7},... | collective-permute-start | bytes 294920 | tf_op jit(solution)/shard_map/ppermute | solution.py:358
  88.9 2.3 %query_grad.1.grad_queries = bf16[256,128]{1,0:T(8,128)(2,1)} custom-call(s32[5,32]{1,0:T(8,128)S(1)} %get-tuple-element.24.table, bf16[32,192,128]{2,1,0:T(8,128)(2,1)S(1)} %all-to-all-done.fetched, bf16[256,128]{1,0:T(8,128)(2,1)S(1)} %copy-done.2, bf16[256,128]{1,0:T(8,128)(2,1)S(1)} %other_grad.1.grads, f32[128,128]{1,0:T(8,128)S(1)} %get-tuple-element.41.stats), custom_call_target="tpu_custom_call" | custom-call | flops 400000000 | bytes 4000000 | tf_op jit(solution)/shard_map/query_grad/pallas_call | solution.py:489
  91.2 6.5 %collective-permute-done.4.next_2 = bf16[1,192,256]{2,1,0:T(8,128)(2,1)S(1)} collective-permute-done((bf16[1,192,256]{2,1,0:T(8,128)(2,1)S(1)}, bf16[1,192,256]{2,1,0:T(8,128)(2,1)S(1)}, u32[]{:S(2)}, u32[]{:S(2)}) %collective-permute-start.4) | collective-permute-done | bytes 98336 | tf_op jit(solution)/shard_map/ppermute | solution.py:358
  97.6 0.0 collective-permute-done.2.next_1
  97.6 0.0 collective-permute-done.3.back_1
  97.6 0.1 mixed_near.1
  97.7 2.2 %all-to-all-done.1.arrived = bf16[32,168,128]{2,1,0:T(8,128)(2,1)S(1)} async-done(((bf16[32,168,128]{2,1,0:T(8,128)(2,1)}), bf16[32,168,128]{2,1,0:T(8,128)(2,1)S(1)}, u32[]{:S(2)}, u32[]{:S(2)}) %all-to-all-start.1) | async-done | bytes 1376288 | tf_op jit(solution)/shard_map/all_to_all | solution.py:349
  99.9 0.0 copy-start.3
  99.9 0.0 copy-start.4
  99.9 1.1 sum_share.1
  100.9 7.7 %all-to-all-start.2 = ((bf16[32,96,128]{2,1,0:T(8,128)(2,1)}), bf16[32,96,128]{2,1,0:T(8,128)(2,1)S(1)}, u32[]{:S(2)}, u32[]{:S(2)}) async-start(bf16[32,96,128]{2,1,0:T(8,128)(2,1)} %sum_share.1), calls=%async_computation.2 | async-start | bytes 1572864 | tf_op jit(solution)/shard_map/all_to_all | solution.py:349
  108.6 6.1 %collective-permute-start.5 = (bf16[1,192,256]{2,1,0:T(8,128)(2,1)S(1)}, bf16[1,192,256]{2,1,0:T(8,128)(2,1)S(1)}, u32[]{:S(2)}, u32[]{:S(2)}) collective-permute-start(bf16[1,192,256]{2,1,0:T(8,128)(2,1)S(1)} %get-tuple-element.36), channel_id=1, source_target_pairs={{0,12},{2,14},{4,0},{6,2},{8,4},{10,6},{12,8},{14,10},{1,13},{3,15... | collective-permute-start | bytes 294920 | tf_op jit(solution)/shard_map/ppermute | solution.py:358
  114.7 1.9 %collective-permute-start.6 = (bf16[192,256]{1,0:T(8,128)(2,1)S(1)}, bf16[192,256]{1,0:T(8,128)(2,1)S(1)}, u32[]{:S(2)}, u32[]{:S(2)}) collective-permute-start(bf16[192,256]{1,0:T(8,128)(2,1)S(1)} %get-tuple-element.37.mixed_part), channel_id=1, source_target_pairs={{0,8},{2,10},{4,12},{6,14},{8,0},{10,2},{12,4},{14,6},{1,9},{3,11}... | collective-permute-start | bytes 294920 | tf_op jit(solution)/shard_map/ppermute | solution.py:358
  116.7 0.0 copy-done.3
  116.7 0.0 copy-done.4
  116.7 0.0 copy-start.5
  116.7 1.0 copy-done.5
  117.7 5.7 %owner_grad.1 = (bf16[256,128]{1,0:T(8,128)(2,1)}, bf16[256,128]{1,0:T(8,128)(2,1)}) custom-call(s32[5,32]{1,0:T(8,128)S(1)} %get-tuple-element.24.table, bf16[32,64,128]{2,1,0:T(8,128)(2,1)S(1)} %copy-done.5, bf16[32,168,128]{2,1,0:T(8,128)(2,1)S(1)} %all-to-all-done.1.arrived, bf16[256,128]{1,0:T(8,128)(2,1)S(1)} %copy-done.3, bf16[256,128]{1,0:T(8,128)(2,1)S(1)} %copy-done.4), custom_call_target="tpu_custom_call" | custom-call | flops 1100000000 | bytes 4000000 | tf_op jit(solution)/shard_map/owner_grad/pallas_call | solution.py:510
  123.5 0.0 collective-permute-done.5.back_2
  123.5 2.8 %collective-permute-done.6.arrived = bf16[192,256]{1,0:T(8,128)(2,1)S(1)} collective-permute-done((bf16[192,256]{1,0:T(8,128)(2,1)S(1)}, bf16[192,256]{1,0:T(8,128)(2,1)S(1)}, u32[]{:S(2)}, u32[]{:S(2)}) %collective-permute-start.6) | collective-permute-done | bytes 98336 | tf_op jit(solution)/shard_map/ppermute | solution.py:358
  126.2 0.7 mixed_last.1
  126.9 1.8 %all-to-all-done.2.gathered = bf16[32,96,128]{2,1,0:T(8,128)(2,1)S(1)} async-done(((bf16[32,96,128]{2,1,0:T(8,128)(2,1)}), bf16[32,96,128]{2,1,0:T(8,128)(2,1)S(1)}, u32[]{:S(2)}, u32[]{:S(2)}) %all-to-all-start.2) | async-done | bytes 786464 | tf_op jit(solution)/shard_map/all_to_all | solution.py:349
  128.7 0.9 write.1
Async XLA Ops:
  3.8 10.4 %copy-start.6 = (bf16[256,192]{0,1:T(8,128)(2,1)S(1)}, bf16[256,192]{0,1:T(8,128)(2,1)}, u32[]{:S(2)}) copy-start(bf16[256,192]{0,1:T(8,128)(2,1)} %param.11) | copy-start | bytes 294916
  3.8 48.8 %all-to-all-start = ((bf16[32,192,128]{2,1,0:T(8,128)(2,1)}), bf16[32,192,128]{2,1,0:T(8,128)(2,1)S(1)}, u32[]{:S(2)}, u32[]{:S(2)}) async-start(bf16[32,192,128]{2,1,0:T(8,128)(2,1)} %get-tuple-element.25), calls=%async_computation | async-start | bytes 3145728 | tf_op jit(solution)/shard_map/all_to_all | solution.py:349
  46.6 4.2 %collective-permute-start = (bf16[1536,256]{1,0:T(8,128)(2,1)S(1)}, bf16[1536,256]{1,0:T(8,128)(2,1)S(1)}, u32[]{:S(2)}, u32[]{:S(2)}) collective-permute-start(bf16[1536,256]{1,0:T(8,128)(2,1)S(1)} %all_gather.3.own), channel_id=1, source_target_pairs={{0,1},{1,0},{2,3},{3,2},{4,5},{5,4},{6,7},{7,6},{8,9},{9,8},{10,11... | collective-permute-start | bytes 2359304 | tf_op jit(solution)/shard_map/ppermute | solution.py:353
  50.1 2.4 %copy-start.2 = (bf16[256,128]{1,0:T(8,128)(2,1)S(1)}, bf16[256,128]{1,0:T(8,128)(2,1)}, u32[]{:S(2)}) copy-start(bf16[256,128]{1,0:T(8,128)(2,1)} %queries.5) | copy-start | bytes 196612
  56.7 43.2 %all-to-all-start.1 = ((bf16[32,168,128]{2,1,0:T(8,128)(2,1)}), bf16[32,168,128]{2,1,0:T(8,128)(2,1)S(1)}, u32[]{:S(2)}, u32[]{:S(2)}) async-start(bf16[32,168,128]{2,1,0:T(8,128)(2,1)} %get-tuple-element.39), calls=%async_computation.1 | async-start | bytes 2752512 | tf_op jit(solution)/shard_map/all_to_all | solution.py:349
  68.0 0.9 copy-start
  68.9 4.5 %collective-permute-start.1 = (bf16[8,192,256]{2,1,0:T(8,128)(2,1)}, bf16[8,192,256]{2,1,0:T(8,128)(2,1)}, u32[]{:S(2)}, u32[]{:S(2)}) collective-permute-start(bf16[8,192,256]{2,1,0:T(8,128)(2,1)} %get-tuple-element.30), channel_id=1, source_target_pairs={{0,1},{1,0},{2,3},{3,2},{4,5},{5,4},{6,7},{7,6},{8,9},{9,8},{10,11... | collective-permute-start | bytes 2359304 | tf_op jit(solution)/shard_map/ppermute | solution.py:353
  73.4 1.1 copy-start.1
  76.1 21.5 %collective-permute-start.2 = (bf16[2,192,256]{2,1,0:T(8,128)(2,1)S(1)}, bf16[2,192,256]{2,1,0:T(8,128)(2,1)S(1)}, u32[]{:S(2)}, u32[]{:S(2)}) collective-permute-start(bf16[2,192,256]{2,1,0:T(8,128)(2,1)S(1)} %get-tuple-element.32), channel_id=1, source_target_pairs={{0,2},{2,4},{4,6},{6,8},{8,10},{10,12},{12,14},{14,0},{1,3},{3,5},... | collective-permute-start | bytes 589832 | tf_op jit(solution)/shard_map/ppermute | solution.py:358
  79.6 18.0 %collective-permute-start.3 = (bf16[2,192,256]{2,1,0:T(8,128)(2,1)S(1)}, bf16[2,192,256]{2,1,0:T(8,128)(2,1)S(1)}, u32[]{:S(2)}, u32[]{:S(2)}) collective-permute-start(bf16[2,192,256]{2,1,0:T(8,128)(2,1)S(1)} %get-tuple-element.33), channel_id=1, source_target_pairs={{0,14},{2,0},{4,2},{6,4},{8,6},{10,8},{12,10},{14,12},{1,15},{3,1}... | collective-permute-start | bytes 589832 | tf_op jit(solution)/shard_map/ppermute | solution.py:358
  87.0 10.7 %collective-permute-start.4 = (bf16[1,192,256]{2,1,0:T(8,128)(2,1)S(1)}, bf16[1,192,256]{2,1,0:T(8,128)(2,1)S(1)}, u32[]{:S(2)}, u32[]{:S(2)}) collective-permute-start(bf16[1,192,256]{2,1,0:T(8,128)(2,1)S(1)} %get-tuple-element.34), channel_id=1, source_target_pairs={{0,4},{2,6},{4,8},{6,10},{8,12},{10,14},{12,0},{14,2},{1,5},{3,7},... | collective-permute-start | bytes 294920 | tf_op jit(solution)/shard_map/ppermute | solution.py:358
  99.9 16.8 %copy-start.3 = (bf16[256,128]{1,0:T(8,128)(2,1)S(1)}, bf16[256,128]{1,0:T(8,128)(2,1)}, u32[]{:S(2)}) copy-start(bf16[256,128]{1,0:T(8,128)(2,1)} %keys.3) | copy-start | bytes 196612
  99.9 16.8 %copy-start.4 = (bf16[256,128]{1,0:T(8,128)(2,1)S(1)}, bf16[256,128]{1,0:T(8,128)(2,1)}, u32[]{:S(2)}) copy-start(bf16[256,128]{1,0:T(8,128)(2,1)} %values.3) | copy-start | bytes 196612
  100.9 27.8 %all-to-all-start.2 = ((bf16[32,96,128]{2,1,0:T(8,128)(2,1)}), bf16[32,96,128]{2,1,0:T(8,128)(2,1)S(1)}, u32[]{:S(2)}, u32[]{:S(2)}) async-start(bf16[32,96,128]{2,1,0:T(8,128)(2,1)} %sum_share.1), calls=%async_computation.2 | async-start | bytes 1572864 | tf_op jit(solution)/shard_map/all_to_all | solution.py:349
  108.6 14.8 %collective-permute-start.5 = (bf16[1,192,256]{2,1,0:T(8,128)(2,1)S(1)}, bf16[1,192,256]{2,1,0:T(8,128)(2,1)S(1)}, u32[]{:S(2)}, u32[]{:S(2)}) collective-permute-start(bf16[1,192,256]{2,1,0:T(8,128)(2,1)S(1)} %get-tuple-element.36), channel_id=1, source_target_pairs={{0,12},{2,14},{4,0},{6,2},{8,4},{10,6},{12,8},{14,10},{1,13},{3,15... | collective-permute-start | bytes 294920 | tf_op jit(solution)/shard_map/ppermute | solution.py:358
  114.7 11.5 %collective-permute-start.6 = (bf16[192,256]{1,0:T(8,128)(2,1)S(1)}, bf16[192,256]{1,0:T(8,128)(2,1)S(1)}, u32[]{:S(2)}, u32[]{:S(2)}) collective-permute-start(bf16[192,256]{1,0:T(8,128)(2,1)S(1)} %get-tuple-element.37.mixed_part), channel_id=1, source_target_pairs={{0,8},{2,10},{4,12},{6,14},{8,0},{10,2},{12,4},{14,6},{1,9},{3,11}... | collective-permute-start | bytes 294920 | tf_op jit(solution)/shard_map/ppermute | solution.py:358
  116.7 1.0 copy-start.5

commit v7 on v6

--- a/solution.py
+++ b/solution.py
@@ -201,13 +201,11 @@
 
 
 def forward_kernel(
-    scale, list_length, table, fetched, queries, core, own, other, grads, out, attention, stats, requests,
+    scale, list_length, table, fetched, queries, core, own, other, grads, out, attention, stats,
     spread, staged, sems,
 ):
     tiles = queries.shape[0] // TILE
     seq_count = out.shape[0]
-    asked = pltpu.make_async_copy(fetched.at[:, pl.ds(2 * TILE, TILE), :], requests, sems.at[seq_count])
-    asked.start()
     model = 2 * own.shape[0]
     chunk = model // seq_count
     lane = lax.broadcasted_iota(jnp.int32, (WIDTH, WIDTH), 1)
@@ -264,10 +262,11 @@
                 stores[-1].start()
     for store in stores:
         store.wait()
-    asked.wait()
-
-
-def query_kernel(scale, list_length, table, fetched, queries, grads, stats, out):
+
+
+def query_kernel(scale, list_length, table, fetched, queries, grads, stats, out, requests, sem):
+    asked = pltpu.make_async_copy(fetched.at[:, pl.ds(2 * TILE, TILE), :], requests, sem)
+    asked.start()
     tiles = queries.shape[0] // TILE
     for tile in range(tiles):
         rows = slice(tile * TILE, (tile + 1) * TILE)
@@ -278,6 +277,7 @@
         grad_probs = dot_nt(split_heads(grads[rows, :]), value_rows)
         grad_scores = (probs * (grad_probs - stats[:, tiles + tile : tiles + tile + 1])).astype(BF16)
         out[rows, :] = (join_heads(dot(grad_scores, key_rows)) * scale).astype(BF16)
+    asked.wait()
 
 
 def sum_kernel(chunk, arrived, mixed_part, grad_queries, out, total_of, sems):
@@ -296,14 +296,26 @@
         store.wait()
 
 
-def owner_kernel(scale, chunk, group, table, requests, arrived, keys, values, grad_keys, grad_values, key_sum, value_sum):
+def owner_kernel(
+    scale, chunk, group, table, requests_h, arrived, keys, values, grad_keys, grad_values,
+    key_sum, value_sum, requests, sems,
+):
     tok_rows = keys.shape[0]
     senders = arrived.shape[0]
     key_tile = lax.broadcasted_iota(jnp.int32, (tok_rows, WIDTH), 0) // TILE
+    loads = [
+        pltpu.make_async_copy(
+            requests_h.at[pl.ds(at * group, group)], requests.at[pl.ds(at * group, group)], sems.at[at]
+        )
+        for at in range(senders // group)
+    ]
+    for load in loads:
+        load.start()
     key_sum[...] = jnp.zeros_like(key_sum)
     value_sum[...] = jnp.zeros_like(value_sum)
 
-    def step(at, carry):
+    def step(at):
+        loads[at].wait()
         query2, grad2, logs, deltas, keeps = [], [], [], [], []
         for k in range(group):
             i = at * group + k
@@ -332,9 +344,9 @@
         grad_scores = (probs * (grad_probs - delta)).astype(BF16)
         key_sum[...] += dot(grad_scores, query2)
         value_sum[...] += dot(probs.astype(BF16), grad2)
-        return carry
-
-    lax.fori_loop(0, senders // group, step, 0)
+
+    for at in range(senders // group):
+        step(at)
     grad_keys[...] = (key_sum[...] * scale).astype(BF16)
     grad_values[...] = value_sum[...].astype(BF16)
 
@@ -428,20 +440,19 @@
         name="other_grad",
     )(core, other_t, weight_v, partial)
 
-    second, attention, stats, requests = pl.pallas_call(
+    second, attention, stats = pl.pallas_call(
         functools.partial(forward_kernel, scale, list_length),
         out_shape=(
             pltpu.HBM((seq_count, chunk + TILE + STAT_ROWS, row_width), BF16),
             block,
             jax.ShapeDtypeStruct((WIDTH, WIDTH), F32),
-            pltpu.HBM((seq_count, TILE, row_width), BF16),
         ),
         in_specs=[SMEM, VMEM, VMEM, SMEM, VMEM, VMEM, VMEM],
-        out_specs=(HBM, VMEM, VMEM, HBM),
+        out_specs=(HBM, VMEM, VMEM),
         scratch_shapes=[
             pltpu.VMEM((tiles_dev, TILE + STAT_ROWS, row_width), BF16),
             pltpu.VMEM((seq_count, chunk + TILE + STAT_ROWS, row_width), BF16),
-            pltpu.SemaphoreType.DMA((seq_count + 1,)),
+            pltpu.SemaphoreType.DMA((seq_count,)),
         ],
         compiler_params=PARAMS,
         name="forward",
@@ -486,11 +497,12 @@
         name="mixed_near",
     )(mine, to_chip(next_1, 1), to_chip(back_1, -1), to_chip(next_2, 2))
 
-    grad_queries = pl.pallas_call(
+    grad_queries, requests = pl.pallas_call(
         functools.partial(query_kernel, scale, list_length),
-        out_shape=block,
+        out_shape=(block, pltpu.HBM((seq_count, TILE, row_width), BF16)),
         in_specs=[SMEM, VMEM, VMEM, VMEM, VMEM],
-        out_specs=VMEM,
+        out_specs=(VMEM, HBM),
+        scratch_shapes=[pltpu.SemaphoreType.DMA],
         compiler_params=PARAMS,
         cost_estimate=pl.CostEstimate(flops=400_000_000, bytes_accessed=4_000_000, transcendentals=300_000),
         name="query_grad",
@@ -510,13 +522,18 @@
     grad_keys, grad_values = pl.pallas_call(
         functools.partial(owner_kernel, scale, chunk, 4),
         out_shape=(block, block),
-        in_specs=[SMEM, VMEM, VMEM, VMEM, VMEM],
+        in_specs=[SMEM, HBM, VMEM, VMEM, VMEM],
         out_specs=(VMEM, VMEM),
-        scratch_shapes=[pltpu.VMEM((tok_rows, row_width), F32), pltpu.VMEM((tok_rows, row_width), F32)],
+        scratch_shapes=[
+            pltpu.VMEM((tok_rows, row_width), F32),
+            pltpu.VMEM((tok_rows, row_width), F32),
+            pltpu.VMEM((seq_count, TILE, row_width), BF16),
+            pltpu.SemaphoreType.DMA((seq_count // 4,)),
+        ],
         compiler_params=PARAMS,
         cost_estimate=pl.CostEstimate(flops=1_100_000_000, bytes_accessed=4_000_000, transcendentals=1_000_000),
         name="owner_grad",
-    )(table, requests, arrived, keys, values)
+    )(table, stay(requests), arrived, keys, values)
     mixed = pl.pallas_call(
         last_kernel,
         out_shape=jax.ShapeDtypeStruct((run, tok_rows), BF16),

time: 130 us -> 130 us (level)
    unnamed x14 -> x12, local copies, waits for them, and re-layouts: 3.06 us -> 2.03 us
  transfers between devices with their start and end apart: 10 -> 10, of which waited for: 7 -> 7; matrix products, arithmetic and copies ran while one was open for 0% -> 0% of each run, Pallas kernels for 12% -> 13%
where the time goes in v7:
time: 130 us; the launch traced here: 129 us
  starting transfers between devices  51.2 us (39%)
  blocking collectives  32.4 us (25%)
  Pallas kernels  25.4 us (20%)
  waiting for transfers between devices  17.5 us (13%)
  local copies, waits for them, and re-layouts  2.03 us (2%)
    all_gather x1, blocking collectives, body(): grad_t = lax.all_gather(grad_mixed.T, 'z', axis=0, tiled=True)  32.4 us
    all_to_all x3, starting transfers between devices, exchange(): lax.all_to_all(blocks, 'seq', split_axis=0, concat_axis=0, tiled=True)  26.6 us
    ppermute x5, starting transfers between devices, to_chip(): lax.ppermute(array, 'z', [(z, (z + apart) % chips) for z in range(chips)])  20.8 us
    ppermute x5, waiting for transfers between devices, to_chip(): lax.ppermute(array, 'z', [(z, (z + apart) % chips) for z in range(chips)])  9.1 us
    pallas_call x1, Pallas kernels, body(): pl.pallas_call(functools.partial(owner_kernel, scale, chunk, 4), out_shap...  6.52 us
    all_to_all x3, waiting for transfers between devices, exchange(): lax.all_to_all(blocks, 'seq', split_axis=0, concat_axis=0, tiled=True)  5.19 us
    pallas_call x1, Pallas kernels, body(): pl.pallas_call(functools.partial(forward_kernel, scale, list_length), out...  4.06 us
    ppermute x2, starting transfers between devices, swap_cores(): return lax.ppermute(array, 'core', [(0, 1), (1, 0)])  3.82 us
  transfers between devices with their start and end apart: 10, of which 7 were waited for; matrix products, arithmetic and copies ran while one was open for 0% of the time, Pallas kernels for 13%

profile of v7, /device:TPU:2, one launch (start us, length us, event | category | flops | bytes accessed | tf_op | source)
XLA Modules:
  0.0 129.5 jit_solution(12637640347439570548)
XLA Ops:
  0.6 3.2 %pack.1 = (bf16[32,192,128]{2,1,0:T(8,128)(2,1)}, s32[5,32]{1,0:T(8,128)S(1)}) custom-call(s32[1]{0:T(128)} %bitcast.2.place, s32[8,128]{1,0:T(8,128)} %bitcast.15, s32[1,128]{1,0:T(1,128)} %bitcast.16, bf16[256,128]{1,0:T(8,128)(2,1)} %queries.5, bf16[256,128]{1,0:T(8,128)(2,1)} %keys.3, bf16[256,128]{1,0:T(8,128)(2,1)} %values.3), custom_call_target="tpu_custom_call" | custom-call | tf_op jit(solution)/shard_map/pack/pallas_call | solution.py:387
  3.8 0.0 copy-start.5
  3.8 10.4 %all-to-all-start = ((bf16[32,192,128]{2,1,0:T(8,128)(2,1)}), bf16[32,192,128]{2,1,0:T(8,128)(2,1)S(1)}, u32[]{:S(2)}, u32[]{:S(2)}) async-start(bf16[32,192,128]{2,1,0:T(8,128)(2,1)} %get-tuple-element.26), calls=%async_computation | async-start | bytes 3145728 | tf_op jit(solution)/shard_map/all_to_all | solution.py:361
  14.2 0.0 copy-done.5
  14.2 32.4 %all_gather.3.own = bf16[1536,256]{1,0:T(8,128)(2,1)S(1)} all-gather(bf16[192,256]{1,0:T(8,128)(2,1)S(1)} %bitcast.13), channel_id=1, replica_groups=mesh['seq'=32,'z'=8,'core'=2] {'z'}, dimensions={0}, use_global_device_ids=true | all-gather | bytes 884736 | tf_op jit(solution)/shard_map/all_gather | solution.py:384
  46.6 1.9 %collective-permute-start = (bf16[1536,256]{1,0:T(8,128)(2,1)S(1)}, bf16[1536,256]{1,0:T(8,128)(2,1)S(1)}, u32[]{:S(2)}, u32[]{:S(2)}) collective-permute-start(bf16[1536,256]{1,0:T(8,128)(2,1)S(1)} %all_gather.3.own), channel_id=1, source_target_pairs={{0,1},{1,0},{2,3},{3,2},{4,5},{5,4},{6,7},{7,6},{8,9},{9,8},{10,11... | collective-permute-start | bytes 2359304 | tf_op jit(solution)/shard_map/ppermute | solution.py:365
  48.6 1.6 %own_grad.1 = (f32[128,256]{1,0:T(8,128)S(1)}, bf16[128,3072]{1,0:T(8,128)(2,1)S(1)}) custom-call(s32[1]{0:T(128)} %bitcast.1.core, bf16[1536,256]{1,0:T(8,128)(2,1)S(1)} %all_gather.3.own, bf16[128,3072]{1,0:T(8,128)(2,1)} %weight_h.3), custom_call_target="tpu_custom_call" | custom-call | flops 3000000000 | bytes 3000000 | tf_op jit(solution)/shard_map/own_grad/pallas_call | solution.py:421
  50.1 0.0 copy-start.2
  50.2 0.7 collective-permute-done.other
  50.8 0.5 other_grad.1.grads
  51.3 1.2 all-to-all-done.fetched
  52.6 0.0 copy-done.2
  52.6 4.1 %forward.1 = (bf16[32,168,128]{2,1,0:T(8,128)(2,1)}, bf16[256,128]{1,0:T(8,128)(2,1)S(1)}, f32[128,128]{1,0:T(8,128)S(1)}) custom-call(s32[5,32]{1,0:T(8,128)S(1)} %get-tuple-element.25.table, bf16[32,192,128]{2,1,0:T(8,128)(2,1)S(1)} %all-to-all-done.fetched, bf16[256,128]{1,0:T(8,128)(2,1)S(1)} %copy-done.2, s32[1]{0:T(128)} %bitcast.1.core, ...), custom_call_target="tpu_custom_call" | custom-call | tf_op jit(solution)/shard_map/forward/pallas_call | solution.py:443
  56.6 8.6 %all-to-all-start.1 = ((bf16[32,168,128]{2,1,0:T(8,128)(2,1)}), bf16[32,168,128]{2,1,0:T(8,128)(2,1)S(1)}, u32[]{:S(2)}, u32[]{:S(2)}) async-start(bf16[32,168,128]{2,1,0:T(8,128)(2,1)} %get-tuple-element.41), calls=%async_computation.1 | async-start | bytes 2752512 | tf_op jit(solution)/shard_map/all_to_all | solution.py:361
  65.2 2.6 %mixed_share.1 = (bf16[8,192,256]{2,1,0:T(8,128)(2,1)S(1)}, bf16[8,192,256]{2,1,0:T(8,128)(2,1)}) custom-call(s32[1]{0:T(128)} %bitcast.1.core, bf16[128,3072]{1,0:T(8,128)(2,1)} %weight_h.3, bf16[256,128]{1,0:T(8,128)(2,1)S(1)} %get-tuple-element.29.attention), custom_call_target="tpu_custom_call" | custom-call | tf_op jit(solution)/shard_map/mixed_share/pallas_call | solution.py:465
  67.9 0.0 copy-start
  67.9 0.9 copy-done
  68.8 1.9 %collective-permute-start.1 = (bf16[8,192,256]{2,1,0:T(8,128)(2,1)}, bf16[8,192,256]{2,1,0:T(8,128)(2,1)}, u32[]{:S(2)}, u32[]{:S(2)}) collective-permute-start(bf16[8,192,256]{2,1,0:T(8,128)(2,1)} %get-tuple-element.31), channel_id=1, source_target_pairs={{0,1},{1,0},{2,3},{3,2},{4,5},{5,4},{6,7},{7,6},{8,9},{9,8},{10,11... | collective-permute-start | bytes 2359304 | tf_op jit(solution)/shard_map/ppermute | solution.py:365
  70.7 2.6 %collective-permute-done.1.arrived = bf16[8,192,256]{2,1,0:T(8,128)(2,1)} collective-permute-done((bf16[8,192,256]{2,1,0:T(8,128)(2,1)}, bf16[8,192,256]{2,1,0:T(8,128)(2,1)}, u32[]{:S(2)}, u32[]{:S(2)}) %collective-permute-start.1) | collective-permute-done | bytes 786464 | tf_op jit(solution)/shard_map/ppermute | solution.py:365
  73.3 0.0 copy-start.1
  73.3 1.1 copy-done.1
  74.4 1.6 %mixed_pair.1 = (f32[2,192,256]{2,1,0:T(8,128)S(1)}, bf16[2,192,256]{2,1,0:T(8,128)(2,1)S(1)}, bf16[2,192,256]{2,1,0:T(8,128)(2,1)S(1)}, bf16[1,192,256]{2,1,0:T(8,128)(2,1)S(1)}, bf16[1,192,256]{2,1,0:T(8,128)(2,1)S(1)}) custom-call(s32[1]{0:T(128)} %bitcast.place, bf16[8,192,256]{2,1,0:T(8,128)(2,1)S(1)} %copy-done.1, ...), custom_call_target="tpu_custom_call" | custom-call | tf_op jit(solution)/shard_map/mixed_pair/pallas_call | solution.py:474
  76.0 3.5 %collective-permute-start.2 = (bf16[2,192,256]{2,1,0:T(8,128)(2,1)S(1)}, bf16[2,192,256]{2,1,0:T(8,128)(2,1)S(1)}, u32[]{:S(2)}, u32[]{:S(2)}) collective-permute-start(bf16[2,192,256]{2,1,0:T(8,128)(2,1)S(1)} %get-tuple-element.33), channel_id=1, source_target_pairs={{0,2},{2,4},{4,6},{6,8},{8,10},{10,12},{12,14},{14,0},{1,3},{3,5},... | collective-permute-start | bytes 589832 | tf_op jit(solution)/shard_map/ppermute | solution.py:370
  79.5 7.4 %collective-permute-start.3 = (bf16[2,192,256]{2,1,0:T(8,128)(2,1)S(1)}, bf16[2,192,256]{2,1,0:T(8,128)(2,1)S(1)}, u32[]{:S(2)}, u32[]{:S(2)}) collective-permute-start(bf16[2,192,256]{2,1,0:T(8,128)(2,1)S(1)} %get-tuple-element.34), channel_id=1, source_target_pairs={{0,14},{2,0},{4,2},{6,4},{8,6},{10,8},{12,10},{14,12},{1,15},{3,1}... | collective-permute-start | bytes 589832 | tf_op jit(solution)/shard_map/ppermute | solution.py:370
  86.9 1.9 %collective-permute-start.4 = (bf16[1,192,256]{2,1,0:T(8,128)(2,1)S(1)}, bf16[1,192,256]{2,1,0:T(8,128)(2,1)S(1)}, u32[]{:S(2)}, u32[]{:S(2)}) collective-permute-start(bf16[1,192,256]{2,1,0:T(8,128)(2,1)S(1)} %get-tuple-element.35), channel_id=1, source_target_pairs={{0,4},{2,6},{4,8},{6,10},{8,12},{10,14},{12,0},{14,2},{1,5},{3,7},... | collective-permute-start | bytes 294920 | tf_op jit(solution)/shard_map/ppermute | solution.py:370
  88.8 2.6 %query_grad.1 = (bf16[256,128]{1,0:T(8,128)(2,1)}, bf16[32,64,128]{2,1,0:T(8,128)(2,1)}) custom-call(s32[5,32]{1,0:T(8,128)S(1)} %get-tuple-element.25.table, bf16[32,192,128]{2,1,0:T(8,128)(2,1)S(1)} %all-to-all-done.fetched, bf16[256,128]{1,0:T(8,128)(2,1)S(1)} %copy-done.2, bf16[256,128]{1,0:T(8,128)(2,1)S(1)} %other_grad.1.grads, ...), custom_call_target="tpu_custom_call" | custom-call | flops 400000000 | bytes 4000000 | tf_op jit(solution)/shard_map/query_grad/pallas_call | solution.py:500
  91.4 6.1 %collective-permute-done.4.next_2 = bf16[1,192,256]{2,1,0:T(8,128)(2,1)S(1)} collective-permute-done((bf16[1,192,256]{2,1,0:T(8,128)(2,1)S(1)}, bf16[1,192,256]{2,1,0:T(8,128)(2,1)S(1)}, u32[]{:S(2)}, u32[]{:S(2)}) %collective-permute-start.4) | collective-permute-done | bytes 98336 | tf_op jit(solution)/shard_map/ppermute | solution.py:370
  97.5 0.0 collective-permute-done.2.next_1
  97.5 0.0 collective-permute-done.3.back_1
  97.5 0.1 mixed_near.1
  97.6 2.2 %all-to-all-done.1.arrived = bf16[32,168,128]{2,1,0:T(8,128)(2,1)S(1)} async-done(((bf16[32,168,128]{2,1,0:T(8,128)(2,1)}), bf16[32,168,128]{2,1,0:T(8,128)(2,1)S(1)}, u32[]{:S(2)}, u32[]{:S(2)}) %all-to-all-start.1) | async-done | bytes 1376288 | tf_op jit(solution)/shard_map/all_to_all | solution.py:361
  99.8 0.0 copy-start.3
  99.8 0.0 copy-start.4
  99.8 1.1 sum_share.1
  100.9 7.7 %all-to-all-start.2 = ((bf16[32,96,128]{2,1,0:T(8,128)(2,1)}), bf16[32,96,128]{2,1,0:T(8,128)(2,1)S(1)}, u32[]{:S(2)}, u32[]{:S(2)}) async-start(bf16[32,96,128]{2,1,0:T(8,128)(2,1)} %sum_share.1), calls=%async_computation.2 | async-start | bytes 1572864 | tf_op jit(solution)/shard_map/all_to_all | solution.py:361
  108.5 6.1 %collective-permute-start.5 = (bf16[1,192,256]{2,1,0:T(8,128)(2,1)S(1)}, bf16[1,192,256]{2,1,0:T(8,128)(2,1)S(1)}, u32[]{:S(2)}, u32[]{:S(2)}) collective-permute-start(bf16[1,192,256]{2,1,0:T(8,128)(2,1)S(1)} %get-tuple-element.37), channel_id=1, source_target_pairs={{0,12},{2,14},{4,0},{6,2},{8,4},{10,6},{12,8},{14,10},{1,13},{3,15... | collective-permute-start | bytes 294920 | tf_op jit(solution)/shard_map/ppermute | solution.py:370
  114.6 1.9 %collective-permute-start.6 = (bf16[192,256]{1,0:T(8,128)(2,1)S(1)}, bf16[192,256]{1,0:T(8,128)(2,1)S(1)}, u32[]{:S(2)}, u32[]{:S(2)}) collective-permute-start(bf16[192,256]{1,0:T(8,128)(2,1)S(1)} %get-tuple-element.38.mixed_part), channel_id=1, source_target_pairs={{0,8},{2,10},{4,12},{6,14},{8,0},{10,2},{12,4},{14,6},{1,9},{3,11}... | collective-permute-start | bytes 294920 | tf_op jit(solution)/shard_map/ppermute | solution.py:370
  116.6 0.0 copy-done.3
  116.6 0.0 copy-done.4
  116.6 6.5 %owner_grad.1 = (bf16[256,128]{1,0:T(8,128)(2,1)}, bf16[256,128]{1,0:T(8,128)(2,1)}) custom-call(s32[5,32]{1,0:T(8,128)S(1)} %get-tuple-element.25.table, bf16[32,64,128]{2,1,0:T(8,128)(2,1)} %get-tuple-element.40.requests_h, bf16[32,168,128]{2,1,0:T(8,128)(2,1)S(1)} %all-to-all-done.1.arrived, bf16[256,128]{1,0:T(8,128)(2,1)S(1)} %copy-done.3, ...), custom_call_target="tpu_custom_call" | custom-call | flops 1100000000 | bytes 4000000 | tf_op jit(solution)/shard_map/owner_grad/pallas_call | solution.py:522
  123.1 0.0 collective-permute-done.5.back_2
  123.1 3.0 %collective-permute-done.6.arrived = bf16[192,256]{1,0:T(8,128)(2,1)S(1)} collective-permute-done((bf16[192,256]{1,0:T(8,128)(2,1)S(1)}, bf16[192,256]{1,0:T(8,128)(2,1)S(1)}, u32[]{:S(2)}, u32[]{:S(2)}) %collective-permute-start.6) | collective-permute-done | bytes 98336 | tf_op jit(solution)/shard_map/ppermute | solution.py:370
  126.1 0.7 mixed_last.1
  126.8 1.8 %all-to-all-done.2.gathered = bf16[32,96,128]{2,1,0:T(8,128)(2,1)S(1)} async-done(((bf16[32,96,128]{2,1,0:T(8,128)(2,1)}), bf16[32,96,128]{2,1,0:T(8,128)(2,1)S(1)}, u32[]{:S(2)}, u32[]{:S(2)}) %all-to-all-start.2) | async-done | bytes 786464 | tf_op jit(solution)/shard_map/all_to_all | solution.py:361
  128.6 0.9 write.1
Async XLA Ops:
  3.8 10.4 %copy-start.5 = (bf16[256,192]{0,1:T(8,128)(2,1)S(1)}, bf16[256,192]{0,1:T(8,128)(2,1)}, u32[]{:S(2)}) copy-start(bf16[256,192]{0,1:T(8,128)(2,1)} %param.11) | copy-start | bytes 294916
  3.8 48.8 %all-to-all-start = ((bf16[32,192,128]{2,1,0:T(8,128)(2,1)}), bf16[32,192,128]{2,1,0:T(8,128)(2,1)S(1)}, u32[]{:S(2)}, u32[]{:S(2)}) async-start(bf16[32,192,128]{2,1,0:T(8,128)(2,1)} %get-tuple-element.26), calls=%async_computation | async-start | bytes 3145728 | tf_op jit(solution)/shard_map/all_to_all | solution.py:361
  46.6 4.2 %collective-permute-start = (bf16[1536,256]{1,0:T(8,128)(2,1)S(1)}, bf16[1536,256]{1,0:T(8,128)(2,1)S(1)}, u32[]{:S(2)}, u32[]{:S(2)}) collective-permute-start(bf16[1536,256]{1,0:T(8,128)(2,1)S(1)} %all_gather.3.own), channel_id=1, source_target_pairs={{0,1},{1,0},{2,3},{3,2},{4,5},{5,4},{6,7},{7,6},{8,9},{9,8},{10,11... | collective-permute-start | bytes 2359304 | tf_op jit(solution)/shard_map/ppermute | solution.py:365
  50.1 2.4 %copy-start.2 = (bf16[256,128]{1,0:T(8,128)(2,1)S(1)}, bf16[256,128]{1,0:T(8,128)(2,1)}, u32[]{:S(2)}) copy-start(bf16[256,128]{1,0:T(8,128)(2,1)} %queries.5) | copy-start | bytes 196612
  56.6 43.1 %all-to-all-start.1 = ((bf16[32,168,128]{2,1,0:T(8,128)(2,1)}), bf16[32,168,128]{2,1,0:T(8,128)(2,1)S(1)}, u32[]{:S(2)}, u32[]{:S(2)}) async-start(bf16[32,168,128]{2,1,0:T(8,128)(2,1)} %get-tuple-element.41), calls=%async_computation.1 | async-start | bytes 2752512 | tf_op jit(solution)/shard_map/all_to_all | solution.py:361
  67.9 0.9 copy-start
  68.8 4.5 %collective-permute-start.1 = (bf16[8,192,256]{2,1,0:T(8,128)(2,1)}, bf16[8,192,256]{2,1,0:T(8,128)(2,1)}, u32[]{:S(2)}, u32[]{:S(2)}) collective-permute-start(bf16[8,192,256]{2,1,0:T(8,128)(2,1)} %get-tuple-element.31), channel_id=1, source_target_pairs={{0,1},{1,0},{2,3},{3,2},{4,5},{5,4},{6,7},{7,6},{8,9},{9,8},{10,11... | collective-permute-start | bytes 2359304 | tf_op jit(solution)/shard_map/ppermute | solution.py:365
  73.3 1.1 copy-start.1
  76.0 21.5 %collective-permute-start.2 = (bf16[2,192,256]{2,1,0:T(8,128)(2,1)S(1)}, bf16[2,192,256]{2,1,0:T(8,128)(2,1)S(1)}, u32[]{:S(2)}, u32[]{:S(2)}) collective-permute-start(bf16[2,192,256]{2,1,0:T(8,128)(2,1)S(1)} %get-tuple-element.33), channel_id=1, source_target_pairs={{0,2},{2,4},{4,6},{6,8},{8,10},{10,12},{12,14},{14,0},{1,3},{3,5},... | collective-permute-start | bytes 589832 | tf_op jit(solution)/shard_map/ppermute | solution.py:370
  79.5 18.0 %collective-permute-start.3 = (bf16[2,192,256]{2,1,0:T(8,128)(2,1)S(1)}, bf16[2,192,256]{2,1,0:T(8,128)(2,1)S(1)}, u32[]{:S(2)}, u32[]{:S(2)}) collective-permute-start(bf16[2,192,256]{2,1,0:T(8,128)(2,1)S(1)} %get-tuple-element.34), channel_id=1, source_target_pairs={{0,14},{2,0},{4,2},{6,4},{8,6},{10,8},{12,10},{14,12},{1,15},{3,1}... | collective-permute-start | bytes 589832 | tf_op jit(solution)/shard_map/ppermute | solution.py:370
  86.9 10.7 %collective-permute-start.4 = (bf16[1,192,256]{2,1,0:T(8,128)(2,1)S(1)}, bf16[1,192,256]{2,1,0:T(8,128)(2,1)S(1)}, u32[]{:S(2)}, u32[]{:S(2)}) collective-permute-start(bf16[1,192,256]{2,1,0:T(8,128)(2,1)S(1)} %get-tuple-element.35), channel_id=1, source_target_pairs={{0,4},{2,6},{4,8},{6,10},{8,12},{10,14},{12,0},{14,2},{1,5},{3,7},... | collective-permute-start | bytes 294920 | tf_op jit(solution)/shard_map/ppermute | solution.py:370
  99.8 16.8 %copy-start.3 = (bf16[256,128]{1,0:T(8,128)(2,1)S(1)}, bf16[256,128]{1,0:T(8,128)(2,1)}, u32[]{:S(2)}) copy-start(bf16[256,128]{1,0:T(8,128)(2,1)} %keys.3) | copy-start | bytes 196612
  99.8 16.8 %copy-start.4 = (bf16[256,128]{1,0:T(8,128)(2,1)S(1)}, bf16[256,128]{1,0:T(8,128)(2,1)}, u32[]{:S(2)}) copy-start(bf16[256,128]{1,0:T(8,128)(2,1)} %values.3) | copy-start | bytes 196612
  100.9 27.8 %all-to-all-start.2 = ((bf16[32,96,128]{2,1,0:T(8,128)(2,1)}), bf16[32,96,128]{2,1,0:T(8,128)(2,1)S(1)}, u32[]{:S(2)}, u32[]{:S(2)}) async-start(bf16[32,96,128]{2,1,0:T(8,128)(2,1)} %sum_share.1), calls=%async_computation.2 | async-start | bytes 1572864 | tf_op jit(solution)/shard_map/all_to_all | solution.py:361
  108.5 14.6 %collective-permute-start.5 = (bf16[1,192,256]{2,1,0:T(8,128)(2,1)S(1)}, bf16[1,192,256]{2,1,0:T(8,128)(2,1)S(1)}, u32[]{:S(2)}, u32[]{:S(2)}) collective-permute-start(bf16[1,192,256]{2,1,0:T(8,128)(2,1)S(1)} %get-tuple-element.37), channel_id=1, source_target_pairs={{0,12},{2,14},{4,0},{6,2},{8,4},{10,6},{12,8},{14,10},{1,13},{3,15... | collective-permute-start | bytes 294920 | tf_op jit(solution)/shard_map/ppermute | solution.py:370
  114.6 11.5 %collective-permute-start.6 = (bf16[192,256]{1,0:T(8,128)(2,1)S(1)}, bf16[192,256]{1,0:T(8,128)(2,1)S(1)}, u32[]{:S(2)}, u32[]{:S(2)}) collective-permute-start(bf16[192,256]{1,0:T(8,128)(2,1)S(1)} %get-tuple-element.38.mixed_part), channel_id=1, source_target_pairs={{0,8},{2,10},{4,12},{6,14},{8,0},{10,2},{12,4},{14,6},{1,9},{3,11}... | collective-permute-start | bytes 294920 | tf_op jit(solution)/shard_map/ppermute | solution.py:370
